TPU v7x, 32 devices: a whole 2x2x4 slice. The times are simulated.
32 devices in a mesh: seq: 8 (over y, x, core), dp: 4 (over z).
Axes of the slice: x: 2, y: 2, z: 4, core: 2. Of those that a mesh axis runs over, the one named last changes fastest.
Arguments:
- query_heads: bfloat16 [4, 2048, 1024], P('dp', 'seq'), may hold values from -6 to 6
- key_heads: bfloat16 [4, 2048, 1024], P('dp', 'seq'), may hold values from -6 to 6
- value_heads: bfloat16 [4, 2048, 1024], P('dp', 'seq'), may hold values from -6 to 6
- beta_logits: float32 [4, 2048, 8], P('dp', 'seq'), may hold values from -8 to 3.5
- segment_ids: int32 [4, 2048], P('dp', 'seq'), may hold values from 0 to 5, as said below
- output_cotangent: bfloat16 [4, 2048, 1024], P('dp', 'seq'), may hold values from -6 to 6
- norm_gain: float32 [128], replicated, may hold values from 0.25 to 1.75
Outputs:
- mixed_heads: bfloat16 [4, 2048, 1024], P('dp', 'seq')
- grad_query: bfloat16 [4, 2048, 1024], P('dp', 'seq')
- grad_key: bfloat16 [4, 2048, 1024], P('dp', 'seq')
- grad_value: bfloat16 [4, 2048, 1024], P('dp', 'seq')
- grad_beta: float32 [4, 2048, 8], P('dp', 'seq')
- grad_gain: float32 [128], replicated
Inputs may be any that keep to these rules, and one draw needn't show every extreme that they name: `segment_ids`: in every row the ids start at 0, never fall, and rise by at most one from a token to the next; the row's first span of 256 tokens and each span in the row's second half hold exactly one document start after the span's first token, the other spans none.
All inputs are finite; a program needn't handle non-finite values.
Results may differ from a plain program's by a relative error of at most 0.001.
Values sent between devices are 32-bit elements; how exact they have to be, the bound alone decides.
No kernel may reach another device: no remote copies, remote signals or barrier semaphores. Data moves between devices by JAX's collectives and lax.ppermute only.
A program may use at most 192 MiB of HBM per device.

v0:
```python
from functools import partial

import jax
import jax.numpy as jnp
from jax import lax
from jax.sharding import PartitionSpec as P

HEADS = 8
HEAD_DIM = 128
BLOCK = 64


HIGHEST = lax.Precision.HIGHEST


def shifted(value, axis, steps):
    count = lax.axis_size(axis)
    first, last = (max(0, -steps), min(count, count - steps))
    return lax.ppermute(value, axis, [(source, source + steps) for source in range(first, last)])


def entering_2(value, axis, combine, identity):
    size, here = (lax.axis_size(axis), lax.axis_index(axis))
    everything = jax.tree.map(lambda part: lax.all_gather(part, axis), value)
    start = jax.tree.map(
        lambda part, zero: jnp.broadcast_to(jnp.asarray(zero, part.dtype), part.shape),
        value,
        identity,
    )

    def lap(k, before):
        at = size - 1 - k
        reached = at > here
        new = combine(before, jax.tree.map(lambda part: part[at], everything))
        return jax.tree.map(lambda a, b: jnp.where(reached, a, b), new, before)

    return lax.fori_loop(0, size, lap, start)


def normalize(vectors):
    return vectors * lax.rsqrt(jnp.sum(vectors * vectors, axis=-1, keepdims=True) + 1e-06)


def block_step(carried, inputs, want_out):
    memory, prior_id = carried
    query_block, keys_block, value_block, rates_block, ident_block = inputs
    block_size = keys_block.shape[0]
    position = jnp.arange(block_size)
    same_doc = ident_block[:, None] == ident_block[None, :]
    strict = (position[:, None] > position[None, :]) & same_doc
    causal = (position[:, None] >= position[None, :]) & same_doc
    keep_in = (ident_block == prior_id).astype(jnp.float32)
    in_last = (ident_block == ident_block[block_size - 1]).astype(jnp.float32)
    carry_on = (ident_block[block_size - 1] == prior_id).astype(jnp.float32)
    rate_rows = jnp.transpose(rates_block)[:, :, None]
    key_inner = jnp.einsum("thd,shd->hts", keys_block, keys_block, precision=HIGHEST)
    system = (
        jnp.eye(block_size, dtype=jnp.float32)[None]
        + jnp.where(strict[None], key_inner, 0.0) * rate_rows
    )
    recalled = jnp.einsum("thd,hvd->htv", keys_block, memory, precision=HIGHEST)
    target = rate_rows * (jnp.transpose(value_block, (1, 0, 2)) - keep_in[None, :, None] * recalled)
    update = lax.linalg.triangular_solve(
        system, target, left_side=True, lower=True, unit_diagonal=True
    )
    new_memory = carry_on * memory + jnp.einsum(
        "hsv,shd->hvd", update * in_last[None, :, None], keys_block, precision=HIGHEST
    )
    output = None
    if want_out:
        scores = jnp.where(
            causal[None],
            jnp.einsum("thd,shd->hts", query_block, keys_block, precision=HIGHEST),
            0.0,
        )
        output = keep_in[:, None, None] * jnp.einsum(
            "thd,hvd->thv", query_block, memory, precision=HIGHEST
        )
        output = output + jnp.einsum("hts,hsv->thv", scores, update, precision=HIGHEST)
    return ((new_memory, ident_block[block_size - 1]), output)


def span_pass(query_norm, key_norm, values_in, rates, doc_ids, prior_id, memory, want_out):
    tokens_here = doc_ids.shape[0]
    count_blocks = tokens_here // BLOCK
    blocks = (
        query_norm.reshape(count_blocks, BLOCK, query_norm.shape[1], query_norm.shape[2]),
        key_norm.reshape(count_blocks, BLOCK, key_norm.shape[1], key_norm.shape[2]),
        values_in.reshape(count_blocks, BLOCK, values_in.shape[1], values_in.shape[2]),
        rates.reshape(count_blocks, BLOCK, rates.shape[1]),
        doc_ids.reshape(count_blocks, BLOCK),
    )
    final, outputs = lax.scan(partial(block_step, want_out=want_out), (memory, prior_id), blocks)
    if want_out:
        outputs = outputs.reshape(tokens_here, outputs.shape[2], outputs.shape[3])
    return (final[0], outputs)


def local_layer(query_wide, key_wide, value_wide, logits, gain_vec, memory, doc_ids, prior_id):
    tokens_here = doc_ids.shape[0]
    query_norm = normalize(query_wide.reshape(tokens_here, HEADS, HEAD_DIM))
    key_norm = normalize(key_wide.reshape(tokens_here, HEADS, HEAD_DIM))
    values_in = value_wide.reshape(tokens_here, HEADS, HEAD_DIM)
    rates = jax.nn.sigmoid(logits)
    final_memory, output = span_pass(
        query_norm, key_norm, values_in, rates, doc_ids, prior_id, memory, True
    )
    inverse_rms = lax.rsqrt(jnp.mean(output * output, axis=-1, keepdims=True) + 1e-05)
    mixed = (output * inverse_rms * gain_vec).reshape(tokens_here, HEADS * HEAD_DIM)
    return (mixed, final_memory)


def compose(earlier, later):
    linear_part = jnp.einsum("hde,hef->hdf", earlier[0], later[0], precision=HIGHEST)
    offset_part = jnp.einsum("hvd,hde->hve", earlier[1], later[0], precision=HIGHEST) + later[1]
    return (linear_part, offset_part)


def local(
    query_heads, key_heads, value_heads, beta_logits, segment_ids, output_cotangent, norm_gain
):
    query_wide = query_heads[0].astype(jnp.float32)
    key_wide = key_heads[0].astype(jnp.float32)
    value_wide = value_heads[0].astype(jnp.float32)
    logits = beta_logits[0]
    doc_ids = segment_ids[0]
    cotangent = output_cotangent[0].astype(jnp.float32)
    tokens_here = doc_ids.shape[0]
    prior_id = shifted(doc_ids[tokens_here - 1 :], "seq", 1)[0]
    query_norm = normalize(query_wide.reshape(tokens_here, HEADS, HEAD_DIM))
    key_norm = normalize(key_wide.reshape(tokens_here, HEADS, HEAD_DIM))
    rates = jax.nn.sigmoid(logits)
    stacked = jnp.concatenate(
        [
            value_wide.reshape(tokens_here, HEADS, HEAD_DIM),
            jnp.zeros((tokens_here, HEADS, HEAD_DIM), jnp.float32),
        ],
        axis=2,
    )
    identity = jnp.broadcast_to(jnp.eye(HEAD_DIM, dtype=jnp.float32), (HEADS, HEAD_DIM, HEAD_DIM))
    initial = jnp.concatenate(
        [jnp.zeros((HEADS, HEAD_DIM, HEAD_DIM), jnp.float32), identity], axis=1
    )
    summary, unused = span_pass(
        query_norm, key_norm, stacked, rates, doc_ids, prior_id, initial, False
    )
    offset = summary[:, :HEAD_DIM]
    linear = summary[:, HEAD_DIM:]
    empty = jnp.zeros_like(offset)
    devices_seq = lax.axis_size("seq")

    def relay_step(turn_index, incoming):
        outgoing = jnp.einsum("hvd,hde->hve", incoming, linear, precision=HIGHEST) + offset
        return shifted(outgoing, "seq", 1)

    entering = lax.fori_loop(0, devices_seq - 1, relay_step, empty)

    def layer_fn(query_arg, key_arg, value_arg, logit_arg, gain_arg, memory_arg):
        return local_layer(
            query_arg, key_arg, value_arg, logit_arg, gain_arg, memory_arg, doc_ids, prior_id
        )

    (mixed_out, leaving), pullback = jax.vjp(
        layer_fn, query_wide, key_wide, value_wide, logits, norm_gain, entering
    )
    local_grads = pullback((cotangent, jnp.zeros_like(leaving)))
    back_linear = jnp.transpose(linear, (0, 2, 1))
    adjoint_out = entering_2((back_linear, local_grads[5]), "seq", compose, (identity, empty))[1]
    second = pullback((jnp.zeros_like(cotangent), adjoint_out))
    gradients = [local_grads[index] + second[index] for index in range(5)]
    gain_total = lax.psum(gradients[4], ("seq", "dp"))
    return (
        mixed_out.astype(jnp.bfloat16)[None],
        gradients[0].astype(jnp.bfloat16)[None],
        gradients[1].astype(jnp.bfloat16)[None],
        gradients[2].astype(jnp.bfloat16)[None],
        gradients[3][None],
        gain_total,
    )


def solution(mesh):
    in_specs = (
        P("dp", "seq", None),
        P("dp", "seq", None),
        P("dp", "seq", None),
        P("dp", "seq", None),
        P("dp", "seq"),
        P("dp", "seq", None),
        P(),
    )
    out_specs = (
        P("dp", "seq", None),
        P("dp", "seq", None),
        P("dp", "seq", None),
        P("dp", "seq", None),
        P("dp", "seq", None),
        P(),
    )
    return jax.shard_map(local, mesh=mesh, in_specs=in_specs, out_specs=out_specs, check_vma=False)
```

profile of v0, /device:TPU:0, one launch (start us, length us, event | category | flops | bytes accessed | tf_op | source)
XLA Modules:
  0.0 1258.5 jit_solution(3897669240535066890)
XLA Ops:
  35.2 191.9 %while.129 = (s32[]{:T(128)}, f32[8,256,128]{2,1,0:T(8,128)S(1)}, s32[]{:T(128)}, s32[4,64]{1,0:T(4,128)S(1)}, f32[4,64,8,128]{3,1,2,0:T(8,128)S(1)}, /*index=5*...) while((s32[]{:T(128)}, f32[8,256,128]{2,1,0:T(8,128)S(1)}, s32[]{:T(128)}, s32[4,64]{1,0:T(4,128)S(1)}, ...), condition=%wide.region_2.3_spmd, body=%wide.region_1.2_spmd.sunk | while | flops 554893632 | bytes 8002455 | solution.py:93
  36.2 39.3 %custom-call.42 = f32[8,1,64,64]{2,3,1,0:T(8,128)S(1)} custom-call(f32[8,1,64,64]{3,2,1,0:T(8,128)S(1)} %fusion.373), custom_call_target="InvertDiagBlocksLowerTriangular" | custom-call | tf_op jit(solution)/shard_map/while/body/eval_jaxpr/triangular_solve | solution.py:63
  84.1 39.3 %custom-call.42 = f32[8,1,64,64]{2,3,1,0:T(8,128)S(1)} custom-call(f32[8,1,64,64]{3,2,1,0:T(8,128)S(1)} %fusion.373), custom_call_target="InvertDiagBlocksLowerTriangular" | custom-call | tf_op jit(solution)/shard_map/while/body/eval_jaxpr/triangular_solve | solution.py:63
  132.1 39.3 %custom-call.42 = f32[8,1,64,64]{2,3,1,0:T(8,128)S(1)} custom-call(f32[8,1,64,64]{3,2,1,0:T(8,128)S(1)} %fusion.373), custom_call_target="InvertDiagBlocksLowerTriangular" | custom-call | tf_op jit(solution)/shard_map/while/body/eval_jaxpr/triangular_solve | solution.py:63
  180.0 39.3 %custom-call.42 = f32[8,1,64,64]{2,3,1,0:T(8,128)S(1)} custom-call(f32[8,1,64,64]{3,2,1,0:T(8,128)S(1)} %fusion.373), custom_call_target="InvertDiagBlocksLowerTriangular" | custom-call | tf_op jit(solution)/shard_map/while/body/eval_jaxpr/triangular_solve | solution.py:63
  232.3 86.0 %while.130 = (s32[]{:T(128)}, f32[8,128,128]{2,1,0:T(8,128)S(1)}, f32[8,128,128]{2,1,0:T(8,128)}, f32[8,128,128]{2,1,0:T(8,128)}, s32[]{:T(128)}) while((s32[]{:T(128)}, f32[8,128,128]{2,1,0:T(8,128)S(1)}, f32[8,128,128]{2,1,0:T(8,128)}, f32[8,128,128]{2,1,0:T(8,128)}, s32[]{:T(128)}) %tuple.261), condition=%wide.region_4.5_spmd, body=%wide.region_3.4_spmd.sunk | while | flops 201457664 | bytes 4194405 | solution.py:156
  319.4 237.1 %while.131 = (s32[]{:T(128)}, f32[8,128,128]{2,1,0:T(8,128)S(1)}, s32[]{:T(128)}, f32[4,64,8,128]{3,1,2,0:T(8,128)}, pred[4,8,64,64]{3,2,1,0:T(32,128)(4,1)}, /*...) while((s32[]{:T(128)}, f32[8,128,128]{2,1,0:T(8,128)S(1)}, ...), condition=%wide.region_7.8_spmd.clone, body=%wide.region_6.7_spmd.clone.sunk | while | flops 504341184 | bytes 11705691 | solution.py:93
  322.4 40.0 %custom-call.43 = f32[8,1,64,64]{2,3,1,0:T(8,128)} custom-call(f32[8,1,64,64]{3,2,1,0:T(8,128)S(1)} %add_bitcast_fusion.2), custom_call_target="InvertDiagBlocksLowerTriangular" | custom-call | tf_op jit(solution)/shard_map/jvp()/while/body/eval_jaxpr/triangular_solve | solution.py:63
  381.6 40.0 %custom-call.43 = f32[8,1,64,64]{2,3,1,0:T(8,128)} custom-call(f32[8,1,64,64]{3,2,1,0:T(8,128)S(1)} %add_bitcast_fusion.2), custom_call_target="InvertDiagBlocksLowerTriangular" | custom-call | tf_op jit(solution)/shard_map/jvp()/while/body/eval_jaxpr/triangular_solve | solution.py:63
  440.8 40.0 %custom-call.43 = f32[8,1,64,64]{2,3,1,0:T(8,128)} custom-call(f32[8,1,64,64]{3,2,1,0:T(8,128)S(1)} %add_bitcast_fusion.2), custom_call_target="InvertDiagBlocksLowerTriangular" | custom-call | tf_op jit(solution)/shard_map/jvp()/while/body/eval_jaxpr/triangular_solve | solution.py:63
  500.0 40.0 %custom-call.43 = f32[8,1,64,64]{2,3,1,0:T(8,128)} custom-call(f32[8,1,64,64]{3,2,1,0:T(8,128)S(1)} %add_bitcast_fusion.2), custom_call_target="InvertDiagBlocksLowerTriangular" | custom-call | tf_op jit(solution)/shard_map/jvp()/while/body/eval_jaxpr/triangular_solve | solution.py:63
  569.7 258.7 %while.133 = (s32[]{:T(128)}, f32[8,128,128]{2,1,0:T(8,128)S(1)}, f32[4,64,8,128]{3,1,2,0:T(8,128)}, f32[4,64,8,128]{3,1,2,0:T(8,128)}, f32[4,64,8,128]{3,1,2,0:...) while((s32[]{:T(128)}, f32[8,128,128]{2,1,0:T(8,128)S(1)}, ...), condition=%wide.region_13.16_spmd.clone, body=%wide.region_10.15_spmd.clone.sunk | while | flops 1034137152 | bytes 26107376 | solution.py:93
  576.2 40.0 %custom-call.45 = f32[8,1,64,64]{2,3,1,0:T(8,128)S(1)} custom-call(f32[8,1,64,64]{3,2,1,0:T(8,128)} %fusion.450), custom_call_target="InvertDiagBlocksLowerTriangular" | custom-call | tf_op jit(solution)/shard_map/transpose(jvp())/while/body/eval_jaxpr/triangular_solve/custom-call.2 | solution.py:63
  641.0 40.0 %custom-call.45 = f32[8,1,64,64]{2,3,1,0:T(8,128)S(1)} custom-call(f32[8,1,64,64]{3,2,1,0:T(8,128)} %fusion.450), custom_call_target="InvertDiagBlocksLowerTriangular" | custom-call | tf_op jit(solution)/shard_map/transpose(jvp())/while/body/eval_jaxpr/triangular_solve/custom-call.2 | solution.py:63
  705.7 40.0 %custom-call.45 = f32[8,1,64,64]{2,3,1,0:T(8,128)S(1)} custom-call(f32[8,1,64,64]{3,2,1,0:T(8,128)} %fusion.450), custom_call_target="InvertDiagBlocksLowerTriangular" | custom-call | tf_op jit(solution)/shard_map/transpose(jvp())/while/body/eval_jaxpr/triangular_solve/custom-call.2 | solution.py:63
  770.3 40.0 %custom-call.45 = f32[8,1,64,64]{2,3,1,0:T(8,128)S(1)} custom-call(f32[8,1,64,64]{3,2,1,0:T(8,128)} %fusion.450), custom_call_target="InvertDiagBlocksLowerTriangular" | custom-call | tf_op jit(solution)/shard_map/transpose(jvp())/while/body/eval_jaxpr/triangular_solve/custom-call.2 | solution.py:63
  854.7 53.4 %psum.7 = f32[128]{0:T(128)} all-reduce(f32[128]{0:T(128)S(1)} %add.264), channel_id=1, replica_groups=mesh['seq'=8,'dp'=4] {'seq','dp'}, use_global_device_ids=true, to_apply=%region_27.30 | all-reduce | flops 128 | bytes 1024 | tf_op jit(solution)/shard_map/psum | solution.py:171
  908.0 12.3 all-gather.5.cloned.1.call-done
  920.4 41.5 %while.134 = (s32[]{:T(128)}, f32[8,128,128]{1,2,0:T(8,128)}, s32[]{:T(128)}, f32[8,8,128,128]{3,2,1,0:T(8,128)}, f32[8,8,128,128]{3,2,1,0:T(8,128)}, /*index=5*/s32[]{:T(128)}, s32[]{:T(128)}, s32[]{:T(128)}, s32[]{:T(128)}) while((s32[]{:T(128)}, f32[8,128,128]{1,2,0:T(8,128)}, s32[]{:T(128)}, f32[8,8,128,128]{3,2,1,0:T(8,128)}, ...), condition=%wide.region_16.19_spmd.clone, body=%wide.region_15.18_spmd.clone.sunk | while | flops 201850880 | bytes 5769377 | solution.py:37
  966.4 256.5 %while.132 = (s32[]{:T(128)}, f32[8,128,128]{2,1,0:T(8,128)S(1)}, f32[4,64,8,128]{3,1,2,0:T(8,128)}, f32[4,64,8,128]{3,1,2,0:T(8,128)}, f32[4,64,8,128]{3,1,2,0:...) while((s32[]{:T(128)}, f32[8,128,128]{2,1,0:T(8,128)S(1)}, ...), condition=%wide.region_21.24_spmd.clone, body=%wide.region_18.23_spmd.clone.sunk | while | flops 1033743936 | bytes 26111360 | solution.py:93
  973.0 40.0 %custom-call.44 = f32[8,1,64,64]{2,3,1,0:T(8,128)S(1)} custom-call(f32[8,1,64,64]{3,2,1,0:T(8,128)} %fusion.415), custom_call_target="InvertDiagBlocksLowerTriangular" | custom-call | tf_op jit(solution)/shard_map/transpose(jvp())/while/body/eval_jaxpr/triangular_solve/custom-call.2 | solution.py:63
  1037.1 40.0 %custom-call.44 = f32[8,1,64,64]{2,3,1,0:T(8,128)S(1)} custom-call(f32[8,1,64,64]{3,2,1,0:T(8,128)} %fusion.415), custom_call_target="InvertDiagBlocksLowerTriangular" | custom-call | tf_op jit(solution)/shard_map/transpose(jvp())/while/body/eval_jaxpr/triangular_solve/custom-call.2 | solution.py:63
  1101.2 40.0 %custom-call.44 = f32[8,1,64,64]{2,3,1,0:T(8,128)S(1)} custom-call(f32[8,1,64,64]{3,2,1,0:T(8,128)} %fusion.415), custom_call_target="InvertDiagBlocksLowerTriangular" | custom-call | tf_op jit(solution)/shard_map/transpose(jvp())/while/body/eval_jaxpr/triangular_solve/custom-call.2 | solution.py:63
  1165.3 40.0 %custom-call.44 = f32[8,1,64,64]{2,3,1,0:T(8,128)S(1)} custom-call(f32[8,1,64,64]{3,2,1,0:T(8,128)} %fusion.415), custom_call_target="InvertDiagBlocksLowerTriangular" | custom-call | tf_op jit(solution)/shard_map/transpose(jvp())/while/body/eval_jaxpr/triangular_solve/custom-call.2 | solution.py:63
  (662 shorter events, 526.0 us)
Async XLA Ops:
  7.2 7.6 copy-start.13
  7.2 900.9 %all-gather.7.cloned.1.call-start = ((), (), s32[]{:S(2)}) async-start(), calls=%async_computation.1 | async-start | bytes 4718592 | tf_op jit(solution)/shard_map/all_gather | solution.py:24
  8.5 26.0 %collective-permute-start.1 = (s32[1]{0:T(128)}, s32[1]{0:T(128)}, u32[]{:S(2)}, u32[]{:S(2)}) collective-permute-start(s32[1]{0:T(128)} %bitcast.10), channel_id=1, source_target_pairs={{0,4},{4,8},{8,12},{12,16},{16,20},{20,24},{24,28},{1,5},{5,9},{9,... | collective-permute-start | bytes 20 | tf_op jit(solution)/shard_map/ppermute | solution.py:19
  22.2 10.5 copy-start.6
  232.3 87.1 %copy-start.1 = (f32[4,64,8,128]{3,1,2,0:T(8,128)S(1)}, f32[4,64,8,128]{3,1,2,0:T(8,128)}, u32[]{:S(2)}) copy-start(f32[4,64,8,128]{3,1,2,0:T(8,128)} %copy_multiply_fusion) | copy-start | bytes 3145732
  232.3 87.1 %copy-start.45 = (f32[4]{0:T(128)S(1)}, f32[4]{0:T(128)}, u32[]{:S(2)}) copy-start(f32[4]{0:T(128)} %custom-call.32) | copy-start | bytes 52
  235.0 5.7 collective-permute-start
  243.3 8.3 collective-permute-start
  254.3 10.7 collective-permute-start
  267.6 10.7 collective-permute-start
  281.0 10.7 collective-permute-start
  294.3 10.7 collective-permute-start
  307.6 10.7 collective-permute-start
  556.5 5.8 copy-start.41
  619.5 5.4 copy-start.9
  623.3 5.8 copy-start.47
  688.0 5.9 copy-start.47
  752.7 5.8 copy-start.47
  817.4 5.8 copy-start.47
  828.4 6.2 copy-start.34
  829.2 91.2 %all-gather.5.cloned.1.call-start = ((), (), s32[]{:S(2)}) async-start(), calls=%async_computation | async-start | bytes 4718592 | tf_op jit(solution)/shard_map/all_gather | solution.py:24
  1223.0 5.6 copy-start.36
  1223.0 5.7 copy-start.38
  1223.0 6.3 copy-start.8
  (56 other events, 190.1 us)
Sparse Core Ops, SparseCore 0:
  829.3 51.6 all-gather.6
  883.5 36.7 all-gather.4
where the time goes:
time: 1270 us; the launch traced here: 1260 us
  other arithmetic  714 us (56%)
  matrix products  234 us (18%)
  local copies, waits for them, and re-layouts  144 us (11%)
  starting transfers between devices  58.7 us (5%)
  blocking collectives  53.4 us (4%)
  waiting for transfers between devices  24.7 us (2%)
  between operations  15.6 us (1%)
  loops' own time  13.7 us (1%)
    another operation x60, other arithmetic, block_step(): lax.linalg.triangular_solve(system, target, left_side=True, lower=True, u...  653 us
    ppermute x8, starting transfers between devices, shifted(): lax.ppermute(value, axis, [(source, source + steps) for source in range(f...  58.5 us
    psum x1, blocking collectives, local(): gain_total = lax.psum(gradients[4], ('seq', 'dp'))  53.4 us
    dot_general x24, matrix products, block_step(): jnp.einsum('hsv,shd->hvd', update * in_last[None, :, None], keys_block, p...  34.9 us
    another operation x24, matrix products, block_step(): lax.linalg.triangular_solve(system, target, left_side=True, lower=True, u...  30.1 us
    dot_general x20, matrix products, block_step(): jnp.einsum('hts,hsv->thv', scores, update, precision=HIGHEST)  27.1 us
    dot_general x24, matrix products, block_step(): recalled = jnp.einsum('thd,hvd->htv', keys_block, memory, precision=HIGHEST)  26.8 us
  transfers between devices with their start and end apart: 10, of which 8 were waited for; matrix products, arithmetic and copies ran while one was open for 4% of the time, Pallas kernels for 0%

commit v1 on v0

v1 whole, which is shorter than its diff:
```python
import functools

import jax
import jax.numpy as jnp
from jax import lax
from jax.experimental import pallas as pl
from jax.experimental.pallas import tpu as pltpu
from jax.sharding import PartitionSpec as P

HEADS = 8
DIM = 128
GROUP = 2
HIGHEST = lax.Precision.HIGHEST
F32 = jnp.float32
BF16 = jnp.bfloat16

NN = (((1,), (0,)), ((), ()))
NT = (((1,), (1,)), ((), ()))
TN = (((0,), (0,)), ((), ()))


def split(x):
    hi = x.astype(BF16)
    return hi, (x - hi.astype(F32)).astype(BF16)


def mm(a, b, dims=NN):
    return lax.dot_general(a, b, dims, preferred_element_type=F32)


def dot3(a, b, dims=NN):
    return mm(a[0], b[0], dims) + (mm(a[0], b[1], dims) + mm(a[1], b[0], dims))


def dot2(a, b, dims=NN):
    return mm(a[0], b, dims) + mm(a[1], b, dims)


def dot2r(a, b, dims=NN):
    return mm(a, b[0], dims) + mm(a, b[1], dims)


def id_masks(ids_ref):
    row = ids_ref[...].astype(F32)
    n = row.shape[1]
    ii = lax.broadcasted_iota(jnp.int32, (n, n), 0)
    jj = lax.broadcasted_iota(jnp.int32, (n, n), 1)
    col = jnp.sum(jnp.where(ii == jj, row, 0.0), axis=1, keepdims=True)
    same = col == row
    first, last = row[:, :1], row[:, n - 1 :]
    keep = (col == first).astype(F32)
    tail = (col == last).astype(F32)
    through = (first == last).astype(F32)
    return same, ii, jj, keep, tail, through


def head(ref, j):
    return ref[:, DIM * j : DIM * (j + 1)]


def put(ref, j, value):
    ref[:, DIM * j : DIM * (j + 1)] = value.astype(ref.dtype)


def inv_norm(x):
    return lax.rsqrt(jnp.sum(x * x, axis=-1, keepdims=True) + 1e-06)


def logit_of(beta_ref, j):
    at = pl.program_id(0) * GROUP + j
    lane = lax.broadcasted_iota(jnp.int32, beta_ref.shape, 1)
    return jnp.sum(jnp.where(lane == at, beta_ref[...], 0.0), axis=1, keepdims=True)


def inverse(blocks):
    n = DIM
    ii = lax.broadcasted_iota(jnp.int32, (n, n), 0)
    jj = lax.broadcasted_iota(jnp.int32, (n, n), 1)
    eye = (ii == jj).astype(F32)

    def off(block, s):
        inside = (ii // (2 * s) == jj // (2 * s)) & (ii // s != jj // s)
        return jnp.where(inside, block, 0.0)

    ts = [eye - off(b, 1) for b in blocks]
    s = 2
    while s < n:
        offs = [split(off(b, s)) for b in blocks]
        tss = [split(t) for t in ts]
        mids = [dot3(o, t) for o, t in zip(offs, tss)]
        mids = [split(m) for m in mids]
        ts = [t - dot3(p, m) for t, p, m in zip(ts, tss, mids)]
        s *= 2
    return ts


def kernel_a(ids_ref, k_ref, v_ref, beta_ref, at_ref, bt_ref, th_ref, tl_ref, uw_ref):
    same, ii, jj, keep, tail, through = id_masks(ids_ref)
    strict = same & (ii > jj)
    heads = range(GROUP)
    ks = [head(k_ref, j) for j in heads]
    k32 = [k.astype(F32) for k in ks]
    iks = [inv_norm(k) for k in k32]
    rates = [jax.nn.sigmoid(logit_of(beta_ref, j)) for j in heads]
    cs = [r * i * i for r, i in zip(rates, iks)]
    ns = [jnp.where(strict, mm(k, k, NT), 0.0) * c for k, c in zip(ks, cs)]
    blocks = []
    for n in ns:
        blocks += [n[:DIM, :DIM], n[DIM:, DIM:]]
    ts = inverse(blocks)
    t1s = [split(t) for t in ts[0::2]]
    t2s = [split(t) for t in ts[1::2]]
    mids = [split(dot3(split(n[DIM:, :DIM]), t)) for n, t in zip(ns, t1s)]
    lows = [split(-dot3(t, m)) for t, m in zip(t2s, mids)]
    zero = jnp.zeros((DIM, DIM), BF16)
    fulls = [
        tuple(
            jnp.concatenate(
                [
                    jnp.concatenate([t1[p], zero], axis=1),
                    jnp.concatenate([lo[p], t2[p]], axis=1),
                ],
                axis=0,
            )
            for p in range(2)
        )
        for t1, t2, lo in zip(t1s, t2s, lows)
    ]
    eye = (
        lax.broadcasted_iota(jnp.int32, (DIM, DIM), 0)
        == lax.broadcasted_iota(jnp.int32, (DIM, DIM), 1)
    ).astype(F32)
    for j in heads:
        value = head(v_ref, j).astype(F32)
        right = jnp.concatenate(
            [value * (rates[j] * iks[j]), k32[j] * (cs[j] * keep)], axis=1
        )
        uw = dot3(fulls[j], split(right))
        ending = (k32[j] * tail).astype(BF16)
        both = dot2r(ending, split(uw), TN)
        bt_ref[j] = both[:, :DIM]
        at_ref[j] = eye * through - both[:, DIM:]
        th_ref[j] = fulls[j][0]
        tl_ref[j] = fulls[j][1]
        uw_ref[j] = uw


def kernel_b(ids_ref, q_ref, k_ref, uw_ref, o_ref, e_ref):
    same, ii, jj, keep, tail, through = id_masks(ids_ref)
    causal = same & (ii >= jj)
    for j in range(GROUP):
        q, k = head(q_ref, j), head(k_ref, j)
        scores = jnp.where(causal, mm(q, k, NT), 0.0)
        both = dot3(split(scores), split(uw_ref[j]))
        put(o_ref, j, both[:, :DIM])
        put(e_ref, j, q.astype(F32) * keep - both[:, DIM:])


def kernel_c(q_ref, o_ref, e_ref, s_ref, cot_ref, gain_ref, y_ref, do_ref, c_ref, dg_ref):
    gain = gain_ref[...]
    dgain = jnp.zeros((1, DIM), F32)
    for j in range(GROUP):
        iq = inv_norm(head(q_ref, j).astype(F32))
        effective = split(head(e_ref, j))
        raw = head(o_ref, j) + dot3(effective, split(s_ref[j]))
        out = raw * iq
        inv = lax.rsqrt(jnp.mean(out * out, axis=-1, keepdims=True) + 1e-05)
        unit = out * inv
        put(y_ref, j, unit * gain)
        cot = head(cot_ref, j).astype(F32)
        dgain = dgain + jnp.sum(cot * unit, axis=0, keepdims=True)
        pulled = cot * gain
        dout = inv * (pulled - unit * jnp.mean(pulled * unit, axis=-1, keepdims=True))
        draw = dout * iq
        put(do_ref, j, draw)
        c_ref[j] = dot3(effective, split(draw), TN)

    @pl.when(pl.program_id(0) == 0)
    def _():
        dg_ref[...] = jnp.zeros_like(dg_ref)

    dg_ref[...] += dgain


def kernel_d(ids_ref, q_ref, k_ref, do_ref, uw_ref, s_ref, dq_ref, u_ref, du_ref, dk_ref):
    same, ii, jj, keep, tail, through = id_masks(ids_ref)
    causal = same & (ii >= jj)
    for j in range(GROUP):
        q, k = head(q_ref, j), head(k_ref, j)
        q32 = q.astype(F32)
        state = split(s_ref[j])
        uw = uw_ref[j]
        update = uw[:, :DIM] - dot3(split(uw[:, DIM:]), state)
        draw = head(do_ref, j)
        draws = split(draw)
        scores = split(jnp.where(causal, mm(q, k, NT), 0.0))
        weights = split(jnp.where(causal, dot3(draws, split(update), NT), 0.0))
        dq = dot3(split(draw * keep), state, NT) + dot2(weights, k)
        iq = inv_norm(q32)
        dq = dq - q32 * (iq * iq * jnp.sum(q32 * dq, axis=-1, keepdims=True))
        put(dq_ref, j, dq)
        put(u_ref, j, update)
        put(du_ref, j, dot3(scores, draws, TN))
        put(dk_ref, j, dot2(weights, q, TN))


def kernel_e(
    ids_ref, k_ref, v_ref, beta_ref, th_ref, tl_ref, u_ref, du_ref, dkl_ref, s_ref, g_ref,
    dk_ref, dv_ref, db_ref,
):
    same, ii, jj, keep, tail, through = id_masks(ids_ref)
    strict = same & (ii > jj)
    lane = lax.broadcasted_iota(jnp.int32, db_ref.shape, 1)
    dbeta = jnp.zeros(db_ref.shape, F32)
    for j in range(GROUP):
        k = head(k_ref, j)
        k32 = k.astype(F32)
        ik = inv_norm(k32)
        logit = logit_of(beta_ref, j)
        rate = jax.nn.sigmoid(logit)
        update = head(u_ref, j)
        updates = split(update)
        back = split(g_ref[j])
        dupdate = head(du_ref, j) + tail * dot2r(k, back)
        dright = dot3((th_ref[j], tl_ref[j]), split(dupdate), TN)
        put(dv_ref, j, dright * (rate * ik))
        at = pl.program_id(0) * GROUP + j
        dlogit = jax.nn.sigmoid(-logit) * jnp.sum(dright * update, axis=-1, keepdims=True)
        dbeta = jnp.where(lane == at, dlogit, dbeta)
        scaled = dright * (rate * ik * ik)
        inner = split(jnp.where(strict, -dot3(split(scaled), updates, NT), 0.0))
        dk = head(dkl_ref, j) + (dot2(inner, k) + dot2(inner, k, TN))
        dk = dk + tail * dot3(updates, back, NT)
        dk = dk - dot3(split(scaled * keep), split(s_ref[j]), NT)
        dk = dk - k32 * (ik * ik * jnp.sum(k32 * dk, axis=-1, keepdims=True))
        put(dk_ref, j, dk)

    @pl.when(pl.program_id(0) == 0)
    def _():
        db_ref[...] = jnp.zeros_like(db_ref)

    db_ref[...] += dbeta


def call(kernel, ins, outs, kinds, flops, name):
    tokens = None
    for kind, arg in zip(kinds[0], ins):
        if kind == "wide":
            tokens = arg.shape[0]
    specs = {
        "wide": pl.BlockSpec((tokens, GROUP * DIM), lambda h: (0, h)),
        "state": pl.BlockSpec((GROUP, DIM, DIM), lambda h: (h, 0, 0)),
        "square": pl.BlockSpec((GROUP, tokens, tokens), lambda h: (h, 0, 0)),
        "uw": pl.BlockSpec((GROUP, tokens, 2 * DIM), lambda h: (h, 0, 0)),
        "ids": pl.BlockSpec((1, tokens), lambda h: (0, 0)),
        "beta": pl.BlockSpec((tokens, HEADS), lambda h: (0, 0)),
        "row": pl.BlockSpec((1, DIM), lambda h: (0, 0)),
    }
    return pl.pallas_call(
        kernel,
        grid=(HEADS // GROUP,),
        in_specs=[specs[kind] for kind in kinds[0]],
        out_specs=[specs[kind] for kind in kinds[1]],
        out_shape=outs,
        compiler_params=pltpu.CompilerParams(vmem_limit_bytes=48 * 1024 * 1024),
        cost_estimate=pl.CostEstimate(flops=flops, bytes_accessed=4_000_000, transcendentals=0),
        name=name,
    )(*ins)


def local(
    query_heads, key_heads, value_heads, beta_logits, segment_ids, output_cotangent, norm_gain
):
    q, k, v = query_heads[0], key_heads[0], value_heads[0]
    beta, ids, cot = beta_logits[0], segment_ids, output_cotangent[0]
    gain = norm_gain[None]
    tokens = q.shape[0]
    spans = lax.axis_size("seq")
    here = lax.axis_index("seq")
    half = spans // 2

    wide = jax.ShapeDtypeStruct((tokens, HEADS * DIM), F32)
    wide16 = jax.ShapeDtypeStruct((tokens, HEADS * DIM), BF16)
    states = jax.ShapeDtypeStruct((HEADS, DIM, DIM), F32)
    square = jax.ShapeDtypeStruct((HEADS, tokens, tokens), BF16)
    uw_shape = jax.ShapeDtypeStruct((HEADS, tokens, 2 * DIM), F32)
    unit = 2 * HEADS * tokens**3

    prior = lax.ppermute(ids[:, tokens - 1 :], "seq", [(s, s + 1) for s in range(spans - 1)])
    joined = ((prior == ids[:, :1]) & (here > 0)).astype(F32)[:, :, None]

    at, bt, th, tl, uw = call(
        kernel_a, (ids, k, v, beta), (states, states, square, square, uw_shape),
        (("ids", "wide", "wide", "beta"), ("state", "state", "square", "square", "uw")),
        20 * unit, "span_state",
    )
    o0, eff = call(
        kernel_b, (ids, q, k, uw), (wide, wide),
        (("ids", "wide", "wide", "uw"), ("wide", "wide")), 4 * unit, "span_out",
    )

    def advance(matrix, state, dims):
        return lax.dot_general(matrix, state, dims, precision=HIGHEST, preferred_element_type=F32)

    FWD = (((2,), (1,)), ((0,), (0,)))
    BWD = (((1,), (1,)), ((0,), (0,)))

    entering = jnp.zeros((HEADS, DIM, DIM), F32)
    outgoing = bt
    for turn in range(half):
        pairs = [(turn, turn + 1)]
        if turn == 0:
            pairs += [(s, s + 1) for s in range(half, spans - 1)]
        entering = entering + joined * lax.ppermute(outgoing, "seq", pairs)
        if turn < half - 1:
            outgoing = advance(at, entering, FWD) + bt

    mixed, draw, cs, dgain = call(
        kernel_c, (q, o0, eff, entering, cot, gain),
        (wide16, wide, states, jax.ShapeDtypeStruct((1, DIM), F32)),
        (("wide", "wide", "wide", "state", "wide", "row"), ("wide", "wide", "state", "row")),
        3 * unit, "span_norm",
    )
    gain_total = lax.psum(dgain[0], ("seq", "dp"))

    back = jnp.zeros((HEADS, DIM, DIM), F32)
    outgoing = joined * cs
    for turn in range(half):
        pairs = [(half - turn, half - turn - 1)]
        if turn == 0:
            pairs += [(s, s - 1) for s in range(half + 1, spans)]
        back = back + lax.ppermute(outgoing, "seq", pairs)
        if turn < half - 1:
            outgoing = joined * (advance(at, back, BWD) + cs)

    dq, update, dupdate, dkl = call(
        kernel_d, (ids, q, k, draw, uw, entering), (wide16, wide, wide, wide),
        (("ids", "wide", "wide", "wide", "uw", "state"), ("wide", "wide", "wide", "wide")),
        10 * unit, "span_query_grad",
    )
    dk, dv, dbeta = call(
        kernel_e, (ids, k, v, beta, th, tl, update, dupdate, dkl, entering, back),
        (wide16, wide16, jax.ShapeDtypeStruct((tokens, HEADS), F32)),
        (
            ("ids", "wide", "wide", "beta", "square", "square", "wide", "wide", "wide", "state",
             "state"),
            ("wide", "wide", "beta"),
        ),
        12 * unit, "span_key_grad",
    )
    return (mixed[None], dq[None], dk[None], dv[None], dbeta[None], gain_total)


def solution(mesh):
    rows = P("dp", "seq", None)
    return jax.shard_map(
        local,
        mesh=mesh,
        in_specs=(rows, rows, rows, rows, P("dp", "seq"), rows, P()),
        out_specs=(rows, rows, rows, rows, rows, P()),
        check_vma=False,
    )
```

time: 1270 us -> 149 us (0.12)
  other arithmetic: 714 us -> 0.38 us
  matrix products: 234 us -> 5.99 us
  local copies, waits for them, and re-layouts: 144 us -> 9.62 us
  starting transfers between devices: 58.7 us -> 9.74 us
  Pallas kernels: 0 us -> 41.8 us
  blocking collectives: 53.4 us -> 78.4 us
  waiting for transfers between devices: 24.7 us -> 0.59 us
  loops' own time: 13.7 us -> 0 us
  between operations: 15.6 us -> 2.18 us
    another operation x71 -> x0, other arithmetic: 653 us -> none  [the longest x60 653 us: block_step(): lax.linalg.triangular_solve(system, target, left_side=True, lower=True, u...]
    dot_general x155 -> x6, matrix products: 204 us -> 5.99 us  [advance(): lax.dot_general(matrix, state, dims, precision=HIGHEST, preferred_element...]
    ppermute x8 -> x9, starting transfers between devices: 58.5 us -> 9.74 us  [the longest x4 4.6 us: local(): entering = entering + joined * lax.ppermute(outgoing, 'seq', pairs)]
    pallas_call x0 -> x5, Pallas kernels: none -> 41.8 us  [call(): pl.pallas_call(kernel, grid=(HEADS // GROUP,), in_specs=[specs[kind] for...]
    dynamic_slice x40 -> x0, local copies, waits for them, and re-layouts: 30.9 us -> none  [the longest x24 20.7 us: span_pass(): lax.scan(partial(block_step, want_out=want_out), (memory, prior_id), blocks)]
    another operation x24 -> x0, matrix products: 30.1 us -> none  [block_step(): lax.linalg.triangular_solve(system, target, left_side=True, lower=True, u...]
    mul x33 -> x0, local copies, waits for them, and re-layouts: 28.1 us -> none  [the longest x4 8.29 us: normalize(): vectors * lax.rsqrt(jnp.sum(vectors * vectors, axis=-1, keepdims=True) +...]
    psum x1, blocking collectives: 53.4 us -> 78.4 us  [local(): gain_total = lax.psum(dgain[0], ('seq', 'dp'))]
  transfers between devices with their start and end apart: 10 -> 9, of which waited for: 8 -> 1; matrix products, arithmetic and copies ran while one was open for 4% -> 0% of each run, Pallas kernels for 0% -> 8%
where the time goes in v1:
time: 149 us
  blocking collectives  78.4 us (53%)
  Pallas kernels  41.8 us (28%)
  starting transfers between devices  9.74 us (7%)
  local copies, waits for them, and re-layouts  9.62 us (6%)
  matrix products  5.99 us (4%)
  between operations  2.18 us (1%)
    psum x1, blocking collectives, local(): gain_total = lax.psum(dgain[0], ('seq', 'dp'))  78.4 us
    pallas_call x5, Pallas kernels, call(): pl.pallas_call(kernel, grid=(HEADS // GROUP,), in_specs=[specs[kind] for...  41.8 us
    unnamed x38, local copies, waits for them, and re-layouts  9.03 us
    dot_general x6, matrix products, advance(): lax.dot_general(matrix, state, dims, precision=HIGHEST, preferred_element...  5.99 us
    ppermute x4, starting transfers between devices, local(): entering = entering + joined * lax.ppermute(outgoing, 'seq', pairs)  4.6 us
    ppermute x4, starting transfers between devices, local(): back = back + lax.ppermute(outgoing, 'seq', pairs)  3.36 us
  transfers between devices with their start and end apart: 9, of which 1 were waited for; matrix products, arithmetic and copies ran while one was open for 0% of the time, Pallas kernels for 8%

profile of v1, /device:TPU:0, one launch (start us, length us, event | category | flops | bytes accessed | tf_op | source)
XLA Modules:
  0.0 148.7 jit_solution(17151387470489016241)
XLA Ops:
  0.6 0.8 copy.13
  2.1 1.0 copy-done.5
  3.2 1.0 copy-done.7
  4.2 15.2 %span_state.1 = (f32[8,128,128]{2,1,0:T(8,128)S(1)}, f32[8,128,128]{2,1,0:T(8,128)S(1)}, bf16[8,256,256]{2,1,0:T(8,128)(2,1)S(1)}, bf16[8,256,256]{2,1,0:T(8,128)(2,1)S(1)}, f32[8,256,256]{2,1,0:T(8,128)}) custom-call(s32[1,256]{1,0:T(1,128)S(1)} %copy-done.2, bf16[256,1024]{1,0:T(8,128)(2,1)S(1)} %bitcast.31, bf16[256,1024]{1,0:T(8,128)(2,1)S(1)} %bitcast.35, ...), custom_call_target="tpu_custom_call" | custom-call | flops 5368709120 | bytes 4000000 | tf_op jit(solution)/shard_map/span_state/pallas_call | solution.py:259
  19.4 1.0 copy-done.10
  20.4 1.0 copy-done.12
  21.3 2.4 %collective-permute-start.1 = (f32[8,128,128]{2,1,0:T(8,128)S(1)}, f32[8,128,128]{2,1,0:T(8,128)S(1)}, u32[]{:S(2)}, u32[]{:S(2)}) collective-permute-start(f32[8,128,128]{2,1,0:T(8,128)S(1)} %get-tuple-element.27), channel_id=1, source_target_pairs={{0,4},{16,20},{20,24},{24,28},{1,5},{17,21},{21,25},{25,29},{2,6},... | collective-permute-start | bytes 1572872 | tf_op jit(solution)/shard_map/ppermute | solution.py:314
  24.3 1.8 %collective-permute-start = (s32[1,1]{1,0:T(1,128)}, s32[1,1]{1,0:T(1,128)}, u32[]{:S(2)}, u32[]{:S(2)}) collective-permute-start(s32[1,1]{1,0:T(1,128)} %get-tuple-element.49), channel_id=1, source_target_pairs={{0,4},{4,8},{8,12},{12,16},{16,20},{20,24},{24,28},{1,5},{5,9},{9,... | collective-permute-start | bytes 20 | tf_op jit(solution)/shard_map/ppermute | solution.py:289
  28.6 0.7 collective-permute-start.2
  29.3 0.7 convolution_add_fusion.4
  30.0 0.8 collective-permute-start.3
  30.9 0.7 convolution_add_fusion.3
  32.3 2.5 %span_out.1 = (f32[256,1024]{1,0:T(8,128)S(1)}, f32[256,1024]{1,0:T(8,128)S(1)}) custom-call(s32[1,256]{1,0:T(1,128)S(1)} %copy-done.3, bf16[256,1024]{1,0:T(8,128)(2,1)S(1)} %bitcast.24, bf16[256,1024]{1,0:T(8,128)(2,1)S(1)} %bitcast.32, f32[8,256,256]{2,1,0:T(8,128)S(1)} %copy-done.9), custom_call_target="tpu_custom_call" | custom-call | flops 1073741824 | bytes 4000000 | tf_op jit(solution)/shard_map/span_out/pallas_call | solution.py:259
  35.0 0.8 copy-done
  35.9 4.1 %span_norm.1 = (bf16[256,1024]{1,0:T(8,128)(2,1)}, f32[256,1024]{1,0:T(8,128)S(1)}, f32[8,128,128]{2,1,0:T(8,128)S(1)}, f32[1,128]{1,0:T(1,128)S(1)}) custom-call(bf16[256,1024]{1,0:T(8,128)(2,1)S(1)} %bitcast.25, f32[256,1024]{1,0:T(8,128)S(1)} %get-tuple-element.25.o_ref, f32[256,1024]{1,0:T(8,128)S(1)} %get-tuple-element.26.e_ref, ...), custom_call_target="tpu_custom_call" | custom-call | flops 805306368 | bytes 4000000 | tf_op jit(solution)/shard_map/span_norm/pallas_call | solution.py:259
  40.8 1.0 fusion.2
  42.6 1.0 fusion.1
  44.4 1.8 %fusion = f32[8,128,128]{2,1,0:T(8,128)} fusion(f32[8,128,128]{2,1,0:T(8,128)S(1)} %get-tuple-element.37, f32[8,128,128]{2,1,0:T(8,128)S(1)} %get-tuple-element.28, f32[8,128,128]{2,1,0:T(8,128)S(1)} %add.47, f32[]{:T(128)} %bitcast.5), kind=kOutput, calls=%fused_computation.1 | convolution fusion | flops 201588736 | bytes 2097156 | tf_op jit(solution)/shard_map/dot_general | solution.py:303
  46.3 1.3 collective-permute-start.8
  47.6 78.4 %psum.7 = f32[128]{0:T(128)} all-reduce(f32[128]{0:T(128)S(1)} %bitcast.37), channel_id=1, replica_groups=mesh['seq'=8,'dp'=4] {'seq','dp'}, use_global_device_ids=true, to_apply=%region_0.0 | all-reduce | flops 128 | bytes 1024 | tf_op jit(solution)/shard_map/psum | solution.py:324
  126.0 9.1 %span_query_grad.1 = (bf16[256,1024]{1,0:T(8,128)(2,1)}, f32[256,1024]{1,0:T(8,128)S(1)}, f32[256,1024]{1,0:T(8,128)S(1)}, f32[256,1024]{1,0:T(8,128)S(1)}) custom-call(s32[1,256]{1,0:T(1,128)S(1)} %copy-done.3, bf16[256,1024]{1,0:T(8,128)(2,1)S(1)} %bitcast.26, bf16[256,1024]{1,0:T(8,128)(2,1)S(1)} %bitcast.33, f32[256,1024]{1,0:T(8,128)S(1)} %get-tuple-element.30.do_ref, ...), custom_call_target="tpu_custom_call" | custom-call | flops 2684354560 | bytes 4000000 | tf_op jit(solution)/shard_map/span_query_grad/pallas_call | solution.py:259
  135.1 1.0 copy-done.14
  136.1 1.0 copy-done.15
  137.2 10.9 %span_key_grad.1 = (bf16[256,1024]{1,0:T(8,128)(2,1)}, bf16[256,1024]{1,0:T(8,128)(2,1)}, f32[256,8]{1,0:T(8,128)S(1)}) custom-call(s32[1,256]{1,0:T(1,128)S(1)} %copy-done.3, bf16[256,1024]{1,0:T(8,128)(2,1)S(1)} %bitcast.34, bf16[256,1024]{1,0:T(8,128)(2,1)S(1)} %bitcast.36, f32[256,8]{1,0:T(8,128)S(1)} %bitcast.28, bf16[8,256,256]{2,1,0:T(8,128)(2,1)S(1)} %copy-done.11, ...), custom_call_target="tpu_custom_call" | custom-call | flops 3221225472 | bytes 4000000 | tf_op jit(solution)/shard_map/span_key_grad/pallas_call | solution.py:259
  (50 shorter events, 6.4 us)
Async XLA Ops:
  2.1 1.0 copy-start.5
  3.2 1.0 copy-start.7
  19.4 1.0 copy-start.10
  21.3 6.5 %collective-permute-start.1 = (f32[8,128,128]{2,1,0:T(8,128)S(1)}, f32[8,128,128]{2,1,0:T(8,128)S(1)}, u32[]{:S(2)}, u32[]{:S(2)}) collective-permute-start(f32[8,128,128]{2,1,0:T(8,128)S(1)} %get-tuple-element.27), channel_id=1, source_target_pairs={{0,4},{16,20},{20,24},{24,28},{1,5},{17,21},{21,25},{25,29},{2,6},... | collective-permute-start | bytes 1572872 | tf_op jit(solution)/shard_map/ppermute | solution.py:314
  24.3 2.4 %collective-permute-start = (s32[1,1]{1,0:T(1,128)}, s32[1,1]{1,0:T(1,128)}, u32[]{:S(2)}, u32[]{:S(2)}) collective-permute-start(s32[1,1]{1,0:T(1,128)} %get-tuple-element.49), channel_id=1, source_target_pairs={{0,4},{4,8},{8,12},{12,16},{16,20},{20,24},{24,28},{1,5},{5,9},{9,... | collective-permute-start | bytes 20 | tf_op jit(solution)/shard_map/ppermute | solution.py:289
  28.6 0.7 collective-permute-start.2
  30.0 2.3 %copy-start.1 = (bf16[1,256,1024]{2,1,0:T(8,128)(2,1)S(1)}, bf16[1,256,1024]{2,1,0:T(8,128)(2,1)}, u32[]{:S(2)}) copy-start(bf16[1,256,1024]{2,1,0:T(8,128)(2,1)} %param.7) | copy-start | bytes 1572868
  30.0 2.3 %copy-start.3 = (s32[1,256]{1,0:T(1,128)S(1)}, s32[1,256]{1,0:T(1,128)}, u32[]{:S(2)}) copy-start(s32[1,256]{1,0:T(1,128)} %ids_ref.7) | copy-start | bytes 3076
  30.0 2.3 %copy-start.6 = (bf16[1,256,1024]{2,1,0:T(8,128)(2,1)S(1)}, bf16[1,256,1024]{2,1,0:T(8,128)(2,1)}, u32[]{:S(2)}) copy-start(bf16[1,256,1024]{2,1,0:T(8,128)(2,1)} %param.8) | copy-start | bytes 1572868
  30.0 2.3 %copy-start.9 = (f32[8,256,256]{2,1,0:T(8,128)S(1)}, f32[8,256,256]{2,1,0:T(8,128)}, u32[]{:S(2)}) copy-start(f32[8,256,256]{2,1,0:T(8,128)} %get-tuple-element.24.uw_ref) | copy-start | bytes 6291460
  30.0 0.8 collective-permute-start.3
  31.6 3.3 %collective-permute-start.4 = (f32[8,128,128]{2,1,0:T(8,128)S(1)}, f32[8,128,128]{2,1,0:T(8,128)S(1)}, u32[]{:S(2)}, u32[]{:S(2)}) collective-permute-start(f32[8,128,128]{2,1,0:T(8,128)S(1)} %convolution_add_fusion.3), channel_id=1, source_target_pairs={{12,16},{13,17},{14,18},{15,19}} | collective-permute-start | bytes 1572872 | tf_op jit(solution)/shard_map/ppermute | solution.py:314
  34.8 1.0 copy-start
  34.9 1.0 copy-start.4
  40.1 0.7 collective-permute-start.5
  41.8 0.7 collective-permute-start.6
  43.7 0.7 collective-permute-start.7
  44.4 1.8 %copy-start.16 = (f32[8,128,128]{2,1,0:T(8,128)}, f32[8,128,128]{2,1,0:T(8,128)S(1)}, u32[]{:S(2)}) copy-start(f32[8,128,128]{2,1,0:T(8,128)S(1)} %add.47) | copy-start | bytes 1572868
  46.3 90.8 %collective-permute-start.8 = (f32[8,128,128]{2,1,0:T(8,128)}, f32[8,128,128]{2,1,0:T(8,128)S(1)}, u32[]{:S(2)}, u32[]{:S(2)}) collective-permute-start(f32[8,128,128]{2,1,0:T(8,128)} %fusion), channel_id=1, source_target_pairs={{4,0},{5,1},{6,2},{7,3}} | collective-permute-start | bytes 1572872 | tf_op jit(solution)/shard_map/ppermute | solution.py:332
  126.0 11.1 %copy-start.17 = (f32[8,128,128]{2,1,0:T(8,128)S(1)}, f32[8,128,128]{2,1,0:T(8,128)}, u32[]{:S(2)}) copy-start(f32[8,128,128]{2,1,0:T(8,128)} %copy-done.16) | copy-start | bytes 1572868
  126.0 11.2 %copy-start.8 = (bf16[1,256,1024]{2,1,0:T(8,128)(2,1)S(1)}, bf16[1,256,1024]{2,1,0:T(8,128)(2,1)}, u32[]{:S(2)}) copy-start(bf16[1,256,1024]{2,1,0:T(8,128)(2,1)} %param.9) | copy-start | bytes 1572868
  126.0 11.2 %copy-start.11 = (bf16[8,256,256]{2,1,0:T(8,128)(2,1)S(1)}, bf16[8,256,256]{2,1,0:T(8,128)(2,1)}, u32[]{:S(2)}) copy-start(bf16[8,256,256]{2,1,0:T(8,128)(2,1)} %copy-done.10) | copy-start | bytes 3145732
  126.0 11.2 %copy-start.13 = (bf16[8,256,256]{2,1,0:T(8,128)(2,1)S(1)}, bf16[8,256,256]{2,1,0:T(8,128)(2,1)}, u32[]{:S(2)}) copy-start(bf16[8,256,256]{2,1,0:T(8,128)(2,1)} %copy-done.12) | copy-start | bytes 3145732
  135.1 1.0 copy-start.14
  (3 other events, 2.6 us)

commit v2 on v1

--- a/solution.py
+++ b/solution.py
@@ -9,7 +9,8 @@
 
 HEADS = 8
 DIM = 128
-GROUP = 2
+GROUP = 8
+BASE = 16
 HIGHEST = lax.Precision.HIGHEST
 F32 = jnp.float32
 BF16 = jnp.bfloat16
@@ -68,22 +69,57 @@
 
 def logit_of(beta_ref, j):
     at = pl.program_id(0) * GROUP + j
-    lane = lax.broadcasted_iota(jnp.int32, beta_ref.shape, 1)
-    return jnp.sum(jnp.where(lane == at, beta_ref[...], 0.0), axis=1, keepdims=True)
+    beta = jnp.transpose(beta_ref[...])
+    lane = lax.broadcasted_iota(jnp.int32, beta.shape, 1)
+    return jnp.sum(jnp.where(lane == at, beta, 0.0), axis=1, keepdims=True)
+
+
+def base_inverses(blocks):
+    n, base = DIM, BASE
+    groups = n // base
+    lane = lax.broadcasted_iota(jnp.int32, (base, n), 1)
+    row = lax.broadcasted_iota(jnp.int32, (base, n), 0)
+    compact = []
+    for block in blocks:
+        kept = [
+            jnp.where(lane // base == g, block[g * base : (g + 1) * base], 0.0)
+            for g in range(groups)
+        ]
+        while len(kept) > 1:
+            kept = [x + y for x, y in zip(kept[0::2], kept[1::2])]
+        compact.append(kept[0])
+    ii = lax.broadcasted_iota(jnp.int32, (n, n), 0)
+    jj = lax.broadcasted_iota(jnp.int32, (n, n), 1)
+    together = ii // base == jj // base
+    pick = jnp.concatenate(
+        [(together & (ii % base == j)).astype(F32).astype(BF16) for j in range(base - 1)], axis=1
+    )
+    high, low = split(jnp.concatenate(compact, axis=0))
+    columns = mm(high, pick) + mm(low, pick)
+    start = (lane % base == row).astype(F32)
+    ts = [start for _ in blocks]
+    for j in range(base - 1):
+        part = columns[:, j * n : (j + 1) * n]
+        ts = [
+            t - part[i * base : (i + 1) * base] * t[j : j + 1] for i, t in enumerate(ts)
+        ]
+    return [
+        jnp.concatenate([jnp.where(lane // base == g, t, 0.0) for g in range(groups)], axis=0)
+        for t in ts
+    ]
 
 
 def inverse(blocks):
     n = DIM
     ii = lax.broadcasted_iota(jnp.int32, (n, n), 0)
     jj = lax.broadcasted_iota(jnp.int32, (n, n), 1)
-    eye = (ii == jj).astype(F32)
 
     def off(block, s):
         inside = (ii // (2 * s) == jj // (2 * s)) & (ii // s != jj // s)
         return jnp.where(inside, block, 0.0)
 
-    ts = [eye - off(b, 1) for b in blocks]
-    s = 2
+    ts = base_inverses(blocks)
+    s = BASE
     while s < n:
         offs = [split(off(b, s)) for b in blocks]
         tss = [split(t) for t in ts]
@@ -94,7 +130,7 @@
     return ts
 
 
-def kernel_a(ids_ref, k_ref, v_ref, beta_ref, at_ref, bt_ref, th_ref, tl_ref, uw_ref):
+def kernel_a(ids_ref, k_ref, v_ref, beta_ref, at_ref, bt_ref, th_ref, tl_ref, z_ref):
     same, ii, jj, keep, tail, through = id_masks(ids_ref)
     strict = same & (ii > jj)
     heads = range(GROUP)
@@ -130,30 +166,37 @@
         lax.broadcasted_iota(jnp.int32, (DIM, DIM), 0)
         == lax.broadcasted_iota(jnp.int32, (DIM, DIM), 1)
     ).astype(F32)
+    zs = [dot2r((k * tail).astype(BF16), full, TN) for k, full in zip(k32, fulls)]
     for j in heads:
-        value = head(v_ref, j).astype(F32)
-        right = jnp.concatenate(
-            [value * (rates[j] * iks[j]), k32[j] * (cs[j] * keep)], axis=1
-        )
-        uw = dot3(fulls[j], split(right))
-        ending = (k32[j] * tail).astype(BF16)
-        both = dot2r(ending, split(uw), TN)
+        right = writes(head(v_ref, j).astype(F32), k32[j], rates[j], iks[j], keep)
+        both = dot3(split(zs[j]), split(right))
         bt_ref[j] = both[:, :DIM]
         at_ref[j] = eye * through - both[:, DIM:]
         th_ref[j] = fulls[j][0]
         tl_ref[j] = fulls[j][1]
-        uw_ref[j] = uw
-
-
-def kernel_b(ids_ref, q_ref, k_ref, uw_ref, o_ref, e_ref):
+        z_ref[j] = zs[j]
+
+
+def writes(value, key, rate, ik, keep):
+    return jnp.concatenate([value * (rate * ik), key * (rate * ik * ik * keep)], axis=1)
+
+
+def kernel_b(
+    ids_ref, q_ref, k_ref, v_ref, beta_ref, th_ref, tl_ref, o_ref, e_ref, uw_ref
+):
     same, ii, jj, keep, tail, through = id_masks(ids_ref)
     causal = same & (ii >= jj)
     for j in range(GROUP):
         q, k = head(q_ref, j), head(k_ref, j)
+        k32 = k.astype(F32)
+        rate = jax.nn.sigmoid(logit_of(beta_ref, j))
+        right = writes(head(v_ref, j).astype(F32), k32, rate, inv_norm(k32), keep)
+        uw = dot3((th_ref[j], tl_ref[j]), split(right))
         scores = jnp.where(causal, mm(q, k, NT), 0.0)
-        both = dot3(split(scores), split(uw_ref[j]))
+        both = dot3(split(scores), split(uw))
         put(o_ref, j, both[:, :DIM])
         put(e_ref, j, q.astype(F32) * keep - both[:, DIM:])
+        uw_ref[j] = uw
 
 
 def kernel_c(q_ref, o_ref, e_ref, s_ref, cot_ref, gain_ref, y_ref, do_ref, c_ref, dg_ref):
@@ -182,7 +225,10 @@
     dg_ref[...] += dgain
 
 
-def kernel_d(ids_ref, q_ref, k_ref, do_ref, uw_ref, s_ref, dq_ref, u_ref, du_ref, dk_ref):
+def kernel_d(
+    ids_ref, q_ref, k_ref, th_ref, tl_ref, do_ref, uw_ref, s_ref,
+    dq_ref, u_ref, dr_ref, dk_ref,
+):
     same, ii, jj, keep, tail, through = id_masks(ids_ref)
     causal = same & (ii >= jj)
     for j in range(GROUP):
@@ -200,19 +246,22 @@
         dq = dq - q32 * (iq * iq * jnp.sum(q32 * dq, axis=-1, keepdims=True))
         put(dq_ref, j, dq)
         put(u_ref, j, update)
-        put(du_ref, j, dot3(scores, draws, TN))
+        dupdate = dot3(scores, draws, TN)
+        put(dr_ref, j, dot3((th_ref[j], tl_ref[j]), split(dupdate), TN))
         put(dk_ref, j, dot2(weights, q, TN))
 
 
 def kernel_e(
-    ids_ref, k_ref, v_ref, beta_ref, th_ref, tl_ref, u_ref, du_ref, dkl_ref, s_ref, g_ref,
+    ids_ref, k_ref, v_ref, beta_ref, z_ref, u_ref, dr_ref, dkl_ref, s_ref, g_ref,
     dk_ref, dv_ref, db_ref,
 ):
     same, ii, jj, keep, tail, through = id_masks(ids_ref)
     strict = same & (ii > jj)
-    lane = lax.broadcasted_iota(jnp.int32, db_ref.shape, 1)
-    dbeta = jnp.zeros(db_ref.shape, F32)
-    for j in range(GROUP):
+    shape = (db_ref.shape[1], db_ref.shape[0])
+    lane = lax.broadcasted_iota(jnp.int32, shape, 1)
+    dbeta = jnp.zeros(shape, F32)
+    heads = range(GROUP)
+    for j in heads:
         k = head(k_ref, j)
         k32 = k.astype(F32)
         ik = inv_norm(k32)
@@ -221,8 +270,7 @@
         update = head(u_ref, j)
         updates = split(update)
         back = split(g_ref[j])
-        dupdate = head(du_ref, j) + tail * dot2r(k, back)
-        dright = dot3((th_ref[j], tl_ref[j]), split(dupdate), TN)
+        dright = head(dr_ref, j) + dot3(split(z_ref[j]), back, TN)
         put(dv_ref, j, dright * (rate * ik))
         at = pl.program_id(0) * GROUP + j
         dlogit = jax.nn.sigmoid(-logit) * jnp.sum(dright * update, axis=-1, keepdims=True)
@@ -239,7 +287,16 @@
     def _():
         db_ref[...] = jnp.zeros_like(db_ref)
 
-    db_ref[...] += dbeta
+    db_ref[...] += jnp.transpose(dbeta)
+
+
+def exchange_sum(value, axis):
+    size = lax.axis_size(axis)
+    step = 1
+    while step < size:
+        value = value + lax.ppermute(value, axis, [(i, i ^ step) for i in range(size)])
+        step *= 2
+    return value
 
 
 def call(kernel, ins, outs, kinds, flops, name):
@@ -251,9 +308,10 @@
         "wide": pl.BlockSpec((tokens, GROUP * DIM), lambda h: (0, h)),
         "state": pl.BlockSpec((GROUP, DIM, DIM), lambda h: (h, 0, 0)),
         "square": pl.BlockSpec((GROUP, tokens, tokens), lambda h: (h, 0, 0)),
+        "z": pl.BlockSpec((GROUP, DIM, tokens), lambda h: (h, 0, 0)),
         "uw": pl.BlockSpec((GROUP, tokens, 2 * DIM), lambda h: (h, 0, 0)),
         "ids": pl.BlockSpec((1, tokens), lambda h: (0, 0)),
-        "beta": pl.BlockSpec((tokens, HEADS), lambda h: (0, 0)),
+        "beta": pl.BlockSpec((HEADS, tokens), lambda h: (0, 0)),
         "row": pl.BlockSpec((1, DIM), lambda h: (0, 0)),
     }
     return pl.pallas_call(
@@ -262,7 +320,7 @@
         in_specs=[specs[kind] for kind in kinds[0]],
         out_specs=[specs[kind] for kind in kinds[1]],
         out_shape=outs,
-        compiler_params=pltpu.CompilerParams(vmem_limit_bytes=48 * 1024 * 1024),
+        compiler_params=pltpu.CompilerParams(vmem_limit_bytes=16 * 1024 * 1024),
         cost_estimate=pl.CostEstimate(flops=flops, bytes_accessed=4_000_000, transcendentals=0),
         name=name,
     )(*ins)
@@ -272,7 +330,7 @@
     query_heads, key_heads, value_heads, beta_logits, segment_ids, output_cotangent, norm_gain
 ):
     q, k, v = query_heads[0], key_heads[0], value_heads[0]
-    beta, ids, cot = beta_logits[0], segment_ids, output_cotangent[0]
+    beta, ids, cot = jnp.transpose(beta_logits[0]), segment_ids, output_cotangent[0]
     gain = norm_gain[None]
     tokens = q.shape[0]
     spans = lax.axis_size("seq")
@@ -289,14 +347,16 @@
     prior = lax.ppermute(ids[:, tokens - 1 :], "seq", [(s, s + 1) for s in range(spans - 1)])
     joined = ((prior == ids[:, :1]) & (here > 0)).astype(F32)[:, :, None]
 
-    at, bt, th, tl, uw = call(
-        kernel_a, (ids, k, v, beta), (states, states, square, square, uw_shape),
-        (("ids", "wide", "wide", "beta"), ("state", "state", "square", "square", "uw")),
+    z_shape = jax.ShapeDtypeStruct((HEADS, DIM, tokens), F32)
+    at, bt, th, tl, z = call(
+        kernel_a, (ids, k, v, beta), (states, states, square, square, z_shape),
+        (("ids", "wide", "wide", "beta"), ("state", "state", "square", "square", "z")),
         20 * unit, "span_state",
     )
-    o0, eff = call(
-        kernel_b, (ids, q, k, uw), (wide, wide),
-        (("ids", "wide", "wide", "uw"), ("wide", "wide")), 4 * unit, "span_out",
+    o0, eff, uw = call(
+        kernel_b, (ids, q, k, v, beta, th, tl), (wide, wide, uw_shape),
+        (("ids", "wide", "wide", "wide", "beta", "square", "square"), ("wide", "wide", "uw")),
+        8 * unit, "span_out",
     )
 
     def advance(matrix, state, dims):
@@ -321,7 +381,7 @@
         (("wide", "wide", "wide", "state", "wide", "row"), ("wide", "wide", "state", "row")),
         3 * unit, "span_norm",
     )
-    gain_total = lax.psum(dgain[0], ("seq", "dp"))
+    gain_total = exchange_sum(exchange_sum(dgain, "seq"), "dp")[0]
 
     back = jnp.zeros((HEADS, DIM, DIM), F32)
     outgoing = joined * cs
@@ -333,22 +393,24 @@
         if turn < half - 1:
             outgoing = joined * (advance(at, back, BWD) + cs)
 
-    dq, update, dupdate, dkl = call(
-        kernel_d, (ids, q, k, draw, uw, entering), (wide16, wide, wide, wide),
-        (("ids", "wide", "wide", "wide", "uw", "state"), ("wide", "wide", "wide", "wide")),
-        10 * unit, "span_query_grad",
+    dq, update, dright, dkl = call(
+        kernel_d, (ids, q, k, th, tl, draw, uw, entering), (wide16, wide, wide, wide),
+        (
+            ("ids", "wide", "wide", "square", "square", "wide", "uw", "state"),
+            ("wide", "wide", "wide", "wide"),
+        ),
+        12 * unit, "span_query_grad",
     )
     dk, dv, dbeta = call(
-        kernel_e, (ids, k, v, beta, th, tl, update, dupdate, dkl, entering, back),
-        (wide16, wide16, jax.ShapeDtypeStruct((tokens, HEADS), F32)),
+        kernel_e, (ids, k, v, beta, z, update, dright, dkl, entering, back),
+        (wide16, wide16, jax.ShapeDtypeStruct((HEADS, tokens), F32)),
         (
-            ("ids", "wide", "wide", "beta", "square", "square", "wide", "wide", "wide", "state",
-             "state"),
+            ("ids", "wide", "wide", "beta", "z", "wide", "wide", "wide", "state", "state"),
             ("wide", "wide", "beta"),
         ),
         12 * unit, "span_key_grad",
     )
-    return (mixed[None], dq[None], dk[None], dv[None], dbeta[None], gain_total)
+    return (mixed[None], dq[None], dk[None], dv[None], jnp.transpose(dbeta)[None], gain_total)
 
 
 def solution(mesh):

time: 149 us -> 109 us (0.73)
  blocking collectives: 78.4 us -> 0 us
  starting transfers between devices: 9.74 us -> 48.7 us
  Pallas kernels: 41.8 us -> 28.4 us
  waiting for transfers between devices: 0.59 us -> 12.6 us
  local copies, waits for them, and re-layouts: 9.62 us -> 5.05 us
  matrix products: 5.99 us -> 8.24 us
  other arithmetic: 0.38 us -> 1.98 us
    psum x1 -> x0, blocking collectives: 78.4 us -> none  [local(): gain_total = lax.psum(dgain[0], ('seq', 'dp'))]
    ppermute x0 -> x5, starting transfers between devices: none -> 37.7 us  [exchange_sum(): lax.ppermute(value, axis, [(i, i ^ step) for i in range(size)])]
    pallas_call x5, Pallas kernels: 41.8 us -> 28.4 us  [call(): pl.pallas_call(kernel, grid=(HEADS // GROUP,), in_specs=[specs[kind] for...]
    ppermute x0 -> x5, waiting for transfers between devices: none -> 12.2 us  [exchange_sum(): lax.ppermute(value, axis, [(i, i ^ step) for i in range(size)])]
    unnamed x38 -> x26, local copies, waits for them, and re-layouts: 9.03 us -> 4.47 us
    dot_general x6, matrix products: 5.99 us -> 8.24 us  [advance(): lax.dot_general(matrix, state, dims, precision=HIGHEST, preferred_element...]
  transfers between devices with their start and end apart: 9 -> 14, of which waited for: 1 -> 5; matrix products, arithmetic and copies ran while one was open for 0% -> 2% of each run, Pallas kernels for 8% -> 11%
where the time goes in v2:
time: 109 us; the launch traced here: 107 us
  starting transfers between devices  48.7 us (45%)
  Pallas kernels  28.4 us (26%)
  waiting for transfers between devices  12.6 us (12%)
  matrix products  8.24 us (8%)
  local copies, waits for them, and re-layouts  5.05 us (5%)
  between operations  2.23 us (2%)
  other arithmetic  1.98 us (2%)
    ppermute x5, starting transfers between devices, exchange_sum(): lax.ppermute(value, axis, [(i, i ^ step) for i in range(size)])  37.7 us
    pallas_call x5, Pallas kernels, call(): pl.pallas_call(kernel, grid=(HEADS // GROUP,), in_specs=[specs[kind] for...  28.4 us
    ppermute x5, waiting for transfers between devices, exchange_sum(): lax.ppermute(value, axis, [(i, i ^ step) for i in range(size)])  12.2 us
    dot_general x6, matrix products, advance(): lax.dot_general(matrix, state, dims, precision=HIGHEST, preferred_element...  8.24 us
    ppermute x4, starting transfers between devices, local(): entering = entering + joined * lax.ppermute(outgoing, 'seq', pairs)  5.55 us
    unnamed x26, local copies, waits for them, and re-layouts  4.47 us
    ppermute x4, starting transfers between devices, local(): back = back + lax.ppermute(outgoing, 'seq', pairs)  3.6 us
  transfers between devices with their start and end apart: 14, of which 5 were waited for; matrix products, arithmetic and copies ran while one was open for 2% of the time, Pallas kernels for 11%

profile of v2, /device:TPU:0, one launch (start us, length us, event | category | flops | bytes accessed | tf_op | source)
XLA Modules:
  0.0 107.3 jit_solution(6477910670035282810)
XLA Ops:
  1.3 1.0 copy-done.5
  2.4 1.0 copy-done.7
  4.1 5.8 %span_state.1 = (f32[8,128,128]{2,1,0:T(8,128)S(1)}, f32[8,128,128]{2,1,0:T(8,128)S(1)}, bf16[8,256,256]{2,1,0:T(8,128)(2,1)S(1)}, bf16[8,256,256]{2,1,0:T(8,128)(2,1)S(1)}, f32[8,128,256]{2,1,0:T(8,128)S(1)}) custom-call(s32[1,256]{1,0:T(1,128)S(1)} %copy-done.2, bf16[256,1024]{1,0:T(8,128)(2,1)S(1)} %bitcast.33, bf16[256,1024]{1,0:T(8,128)(2,1)S(1)} %bitcast.37, ...), custom_call_target="tpu_custom_call" | custom-call | flops 5368709120 | bytes 4000000 | tf_op jit(solution)/shard_map/span_state/pallas_call | solution.py:317
  10.9 3.2 %collective-permute-start.1 = (f32[8,128,128]{2,1,0:T(8,128)S(1)}, f32[8,128,128]{2,1,0:T(8,128)}, u32[]{:S(2)}, u32[]{:S(2)}) collective-permute-start(f32[8,128,128]{2,1,0:T(8,128)S(1)} %get-tuple-element.29), channel_id=1, source_target_pairs={{0,4},{16,20},{20,24},{24,28},{1,5},{17,21},{21,25},{25,29},{2,6},... | collective-permute-start | bytes 1572872 | tf_op jit(solution)/shard_map/ppermute | solution.py:374
  14.7 1.8 %collective-permute-start = (s32[1,1]{1,0:T(1,128)}, s32[1,1]{1,0:T(1,128)}, u32[]{:S(2)}, u32[]{:S(2)}) collective-permute-start(s32[1,1]{1,0:T(1,128)} %get-tuple-element.45), channel_id=1, source_target_pairs={{0,4},{4,8},{8,12},{12,16},{16,20},{20,24},{24,28},{1,5},{5,9},{9,... | collective-permute-start | bytes 20 | tf_op jit(solution)/shard_map/ppermute | solution.py:347
  18.2 1.7 %convolution_add_fusion.5 = f32[8,128,128]{2,1,0:T(8,128)S(1)} fusion(f32[8,128,128]{2,1,0:T(8,128)S(1)} %get-tuple-element.29, f32[8,128,128]{2,1,0:T(8,128)S(1)} %get-tuple-element.30, f32[8,128,128]{2,1,0:T(8,128)} %collective-permute-done.1, f32[]{:T(128)} %bitcast.7), kind=kOutput, calls=%fused_computation.8 | convolution fusion | flops 201588736 | bytes 2097156 | tf_op jit(solution)/shard_map/dot_general | solution.py:363
  20.6 1.7 %convolution_add_fusion.4 = f32[8,128,128]{2,1,0:T(8,128)S(1)} fusion(f32[8,128,128]{2,1,0:T(8,128)S(1)} %get-tuple-element.29, f32[8,128,128]{2,1,0:T(8,128)S(1)} %get-tuple-element.30, f32[8,128,128]{2,1,0:T(8,128)S(1)} %collective-permute-done.2, f32[8,128,128]{2,1,0:T(8,128)} %collective-permute-done.1, f32[]{:T(128)} %bitcast.7), kind=kOutput, calls=%fused_computation.7 | convolution fusion | flops 201850880 | bytes 2621444 | tf_op jit(solution)/shard_map/dot_general | solution.py:363
  23.2 1.8 %convolution_add_fusion.3 = f32[8,128,128]{2,1,0:T(8,128)S(1)} fusion(f32[8,128,128]{2,1,0:T(8,128)S(1)} %get-tuple-element.29, f32[8,128,128]{2,1,0:T(8,128)S(1)} %get-tuple-element.30, f32[8,128,128]{2,1,0:T(8,128)S(1)} %collective-permute-done.3, f32[]{:T(128)} %bitcast.7, f32[8,128,128]{2,1,0:T(8,128)S(1)} %collective-permute-done.2, ...), kind=kOutput, calls=%fused_computation.6 | convolution fusion | flops 202113024 | bytes 3145732 | tf_op jit(solution)/shard_map/dot_general | solution.py:363
  25.9 3.4 %span_out.1 = (f32[256,1024]{1,0:T(8,128)S(1)}, f32[256,1024]{1,0:T(8,128)S(1)}, f32[8,256,256]{2,1,0:T(8,128)S(1)}) custom-call(s32[1,256]{1,0:T(1,128)S(1)} %copy-done.3, bf16[256,1024]{1,0:T(8,128)(2,1)S(1)} %bitcast.29, bf16[256,1024]{1,0:T(8,128)(2,1)S(1)} %bitcast.34, bf16[256,1024]{1,0:T(8,128)(2,1)S(1)} %bitcast.38, f32[8,256]{1,0:T(8,128)S(1)} %bitcast.41, ...), custom_call_target="tpu_custom_call" | custom-call | flops 2147483648 | bytes 4000000 | tf_op jit(solution)/shard_map/span_out/pallas_call | solution.py:317
  29.3 1.2 %multiply_add_fusion.s_ref = f32[8,128,128]{2,1,0:T(8,128)S(1)} fusion(f32[8,128,128]{2,1,0:T(8,128)S(1)} %collective-permute-done.4, f32[]{:T(128)} %bitcast.7, f32[8,128,128]{2,1,0:T(8,128)S(1)} %collective-permute-done.3, f32[8,128,128]{2,1,0:T(8,128)S(1)} %collective-permute-done.2, f32[8,128,128]{2,1,0:T(8,128)} %collective-permute-done.1), kind=kLoop, calls=%fused_computation.9 | loop fusion | flops 917504 | bytes 2621444 | tf_op jit(solution)/shard_map/add | solution.py:374
  30.6 2.8 %span_norm.1 = (bf16[256,1024]{1,0:T(8,128)(2,1)}, f32[256,1024]{1,0:T(8,128)S(1)}, f32[8,128,128]{2,1,0:T(8,128)S(1)}, f32[1,128]{1,0:T(1,128)S(1)}) custom-call(bf16[256,1024]{1,0:T(8,128)(2,1)S(1)} %bitcast.30, f32[256,1024]{1,0:T(8,128)S(1)} %get-tuple-element.27.o_ref, f32[256,1024]{1,0:T(8,128)S(1)} %get-tuple-element.28.e_ref, ...), custom_call_target="tpu_custom_call" | custom-call | flops 805306368 | bytes 4000000 | tf_op jit(solution)/shard_map/span_norm/pallas_call | solution.py:317
  34.1 1.0 fusion.2
  35.9 1.0 fusion.1
  37.7 12.0 %collective-permute-start.9 = (f32[1,128]{1,0:T(1,128)S(1)}, f32[1,128]{1,0:T(1,128)S(1)}, u32[]{:S(2)}, u32[]{:S(2)}) collective-permute-start(f32[1,128]{1,0:T(1,128)S(1)} %get-tuple-element.43), channel_id=1, source_target_pairs={{0,4},{4,0},{8,12},{12,8},{16,20},{20,16},{24,28},{28,24},{1,5},{5... | collective-permute-start | bytes 1544 | tf_op jit(solution)/shard_map/ppermute | solution.py:297
  50.5 21.5 %collective-permute-start.10 = (f32[1,128]{1,0:T(1,128)S(1)}, f32[1,128]{1,0:T(1,128)S(1)}, u32[]{:S(2)}, u32[]{:S(2)}) collective-permute-start(f32[1,128]{1,0:T(1,128)S(1)} %add.63), channel_id=1, source_target_pairs={{0,8},{4,12},{8,0},{12,4},{16,24},{20,28},{24,16},{28,20},{1,9},{5... | collective-permute-start | bytes 1544 | tf_op jit(solution)/shard_map/ppermute | solution.py:297
  72.1 5.9 %collective-permute-done.10 = f32[1,128]{1,0:T(1,128)S(1)} collective-permute-done((f32[1,128]{1,0:T(1,128)S(1)}, f32[1,128]{1,0:T(1,128)S(1)}, u32[]{:S(2)}, u32[]{:S(2)}) %collective-permute-start.10) | collective-permute-done | bytes 544 | tf_op jit(solution)/shard_map/ppermute | solution.py:297
  78.0 3.5 %collective-permute-done.11 = f32[1,128]{1,0:T(1,128)S(1)} collective-permute-done((f32[1,128]{1,0:T(1,128)S(1)}, f32[1,128]{1,0:T(1,128)S(1)}, u32[]{:S(2)}, u32[]{:S(2)}) %collective-permute-start.11) | collective-permute-done | bytes 544 | tf_op jit(solution)/shard_map/ppermute | solution.py:297
  81.5 1.6 %collective-permute-start.12 = (f32[1,128]{1,0:T(1,128)S(1)}, f32[1,128]{1,0:T(1,128)S(1)}, u32[]{:S(2)}, u32[]{:S(2)}) collective-permute-start(f32[1,128]{1,0:T(1,128)S(1)} %add.65), channel_id=1, source_target_pairs={{0,1},{1,0},{2,3},{3,2},{4,5},{5,4},{6,7},{7,6},{8,9},{9,8},{10,11... | collective-permute-start | bytes 1544 | tf_op jit(solution)/shard_map/ppermute | solution.py:297
  83.1 2.0 %collective-permute-done.12 = f32[1,128]{1,0:T(1,128)S(1)} collective-permute-done((f32[1,128]{1,0:T(1,128)S(1)}, f32[1,128]{1,0:T(1,128)S(1)}, u32[]{:S(2)}, u32[]{:S(2)}) %collective-permute-start.12) | collective-permute-done | bytes 544 | tf_op jit(solution)/shard_map/ppermute | solution.py:297
  85.1 2.6 %collective-permute-start.13 = (f32[1,128]{1,0:T(1,128)S(1)}, f32[1,128]{1,0:T(1,128)S(1)}, u32[]{:S(2)}, u32[]{:S(2)}) collective-permute-start(f32[1,128]{1,0:T(1,128)S(1)} %add.66), channel_id=1, source_target_pairs={{0,2},{1,3},{2,0},{3,1},{4,6},{5,7},{6,4},{7,5},{8,10},{9,11},{10,... | collective-permute-start | bytes 1544 | tf_op jit(solution)/shard_map/ppermute | solution.py:297
  87.7 1.0 fusion
  88.7 1.5 %collective-permute-start.8 = (f32[8,128,128]{2,1,0:T(8,128)S(1)}, f32[8,128,128]{2,1,0:T(8,128)S(1)}, u32[]{:S(2)}, u32[]{:S(2)}) collective-permute-start(f32[8,128,128]{2,1,0:T(8,128)S(1)} %fusion), channel_id=1, source_target_pairs={{4,0},{5,1},{6,2},{7,3}} | collective-permute-start | bytes 1572872 | tf_op jit(solution)/shard_map/ppermute | solution.py:392
  90.3 8.9 %span_query_grad.1 = (bf16[256,1024]{1,0:T(8,128)(2,1)}, f32[256,1024]{1,0:T(8,128)S(1)}, f32[256,1024]{1,0:T(8,128)S(1)}, f32[256,1024]{1,0:T(8,128)S(1)}) custom-call(s32[1,256]{1,0:T(1,128)S(1)} %copy-done.3, bf16[256,1024]{1,0:T(8,128)(2,1)S(1)} %bitcast.31, bf16[256,1024]{1,0:T(8,128)(2,1)S(1)} %bitcast.35, ...), custom_call_target="tpu_custom_call" | custom-call | flops 3221225472 | bytes 4000000 | tf_op jit(solution)/shard_map/span_query_grad/pallas_call | solution.py:317
  99.8 7.4 %span_key_grad.1 = (bf16[256,1024]{1,0:T(8,128)(2,1)}, bf16[256,1024]{1,0:T(8,128)(2,1)}, f32[8,256]{1,0:T(8,128)}) custom-call(s32[1,256]{1,0:T(1,128)S(1)} %copy-done.3, bf16[256,1024]{1,0:T(8,128)(2,1)S(1)} %bitcast.36, bf16[256,1024]{1,0:T(8,128)(2,1)S(1)} %bitcast.39, f32[8,256]{1,0:T(8,128)S(1)} %bitcast.42, f32[8,128,256]{2,1,0:T(8,128)S(1)} %copy-done.12, ...), custom_call_target="tpu_custom_call" | custom-call | flops 3221225472 | bytes 4000000 | tf_op jit(solution)/shard_map/span_key_grad/pallas_call | solution.py:317
  (52 shorter events, 9.4 us)
Async XLA Ops:
  1.3 1.0 copy-start.5
  2.4 1.0 copy-start.7
  10.9 7.2 %collective-permute-start.1 = (f32[8,128,128]{2,1,0:T(8,128)S(1)}, f32[8,128,128]{2,1,0:T(8,128)}, u32[]{:S(2)}, u32[]{:S(2)}) collective-permute-start(f32[8,128,128]{2,1,0:T(8,128)S(1)} %get-tuple-element.29), channel_id=1, source_target_pairs={{0,4},{16,20},{20,24},{24,28},{1,5},{17,21},{21,25},{25,29},{2,6},... | collective-permute-start | bytes 1572872 | tf_op jit(solution)/shard_map/ppermute | solution.py:374
  14.7 2.2 %collective-permute-start = (s32[1,1]{1,0:T(1,128)}, s32[1,1]{1,0:T(1,128)}, u32[]{:S(2)}, u32[]{:S(2)}) collective-permute-start(s32[1,1]{1,0:T(1,128)} %get-tuple-element.45), channel_id=1, source_target_pairs={{0,4},{4,8},{8,12},{12,16},{16,20},{20,24},{24,28},{1,5},{5,9},{9,... | collective-permute-start | bytes 20 | tf_op jit(solution)/shard_map/ppermute | solution.py:347
  19.9 0.7 collective-permute-start.2
  22.3 3.5 %copy-start.1 = (bf16[1,256,1024]{2,1,0:T(8,128)(2,1)S(1)}, bf16[1,256,1024]{2,1,0:T(8,128)(2,1)}, u32[]{:S(2)}) copy-start(bf16[1,256,1024]{2,1,0:T(8,128)(2,1)} %param.7) | copy-start | bytes 1572868
  22.3 3.5 %copy-start.3 = (s32[1,256]{1,0:T(1,128)S(1)}, s32[1,256]{1,0:T(1,128)}, u32[]{:S(2)}) copy-start(s32[1,256]{1,0:T(1,128)} %ids_ref.7) | copy-start | bytes 3076
  22.3 3.5 %copy-start.6 = (bf16[1,256,1024]{2,1,0:T(8,128)(2,1)S(1)}, bf16[1,256,1024]{2,1,0:T(8,128)(2,1)}, u32[]{:S(2)}) copy-start(bf16[1,256,1024]{2,1,0:T(8,128)(2,1)} %param.8) | copy-start | bytes 1572868
  22.3 3.5 %copy-start.8 = (bf16[1,256,1024]{2,1,0:T(8,128)(2,1)S(1)}, bf16[1,256,1024]{2,1,0:T(8,128)(2,1)}, u32[]{:S(2)}) copy-start(bf16[1,256,1024]{2,1,0:T(8,128)(2,1)} %param.9) | copy-start | bytes 1572868
  22.3 3.5 %copy-start.10 = (f32[1,256,8]{1,2,0:T(8,128)S(1)}, f32[1,256,8]{1,2,0:T(8,128)}, u32[]{:S(2)}) copy-start(f32[1,256,8]{1,2,0:T(8,128)} %param.10) | copy-start | bytes 24580
  22.4 0.8 collective-permute-start.3
  25.0 4.4 %collective-permute-start.4 = (f32[8,128,128]{2,1,0:T(8,128)S(1)}, f32[8,128,128]{2,1,0:T(8,128)S(1)}, u32[]{:S(2)}, u32[]{:S(2)}) collective-permute-start(f32[8,128,128]{2,1,0:T(8,128)S(1)} %convolution_add_fusion.3), channel_id=1, source_target_pairs={{12,16},{13,17},{14,18},{15,19}} | collective-permute-start | bytes 1572872 | tf_op jit(solution)/shard_map/ppermute | solution.py:374
  29.3 1.3 %copy-start = (bf16[1,256,1024]{2,1,0:T(8,128)(2,1)S(1)}, bf16[1,256,1024]{2,1,0:T(8,128)(2,1)}, u32[]{:S(2)}) copy-start(bf16[1,256,1024]{2,1,0:T(8,128)(2,1)} %param.12) | copy-start | bytes 1572868
  29.3 1.3 %copy-start.4 = (f32[128]{0:T(128)S(1)}, f32[128]{0:T(128)}, u32[]{:S(2)}) copy-start(f32[128]{0:T(128)} %param.13) | copy-start | bytes 1540
  33.4 0.7 collective-permute-start.5
  35.2 0.7 collective-permute-start.6
  37.0 50.7 %collective-permute-start.7 = (f32[8,128,128]{2,1,0:T(8,128)S(1)}, f32[8,128,128]{2,1,0:T(8,128)S(1)}, u32[]{:S(2)}, u32[]{:S(2)}) collective-permute-start(f32[8,128,128]{2,1,0:T(8,128)S(1)} %fusion.1), channel_id=1, source_target_pairs={{8,4},{9,5},{10,6},{11,7}} | collective-permute-start | bytes 1572872 | tf_op jit(solution)/shard_map/ppermute | solution.py:392
  37.7 12.9 %collective-permute-start.9 = (f32[1,128]{1,0:T(1,128)S(1)}, f32[1,128]{1,0:T(1,128)S(1)}, u32[]{:S(2)}, u32[]{:S(2)}) collective-permute-start(f32[1,128]{1,0:T(1,128)S(1)} %get-tuple-element.43), channel_id=1, source_target_pairs={{0,4},{4,0},{8,12},{12,8},{16,20},{20,16},{24,28},{28,24},{1,5},{5... | collective-permute-start | bytes 1544 | tf_op jit(solution)/shard_map/ppermute | solution.py:297
  50.5 27.4 %collective-permute-start.10 = (f32[1,128]{1,0:T(1,128)S(1)}, f32[1,128]{1,0:T(1,128)S(1)}, u32[]{:S(2)}, u32[]{:S(2)}) collective-permute-start(f32[1,128]{1,0:T(1,128)S(1)} %add.63), channel_id=1, source_target_pairs={{0,8},{4,12},{8,0},{12,4},{16,24},{20,28},{24,16},{28,20},{1,9},{5... | collective-permute-start | bytes 1544 | tf_op jit(solution)/shard_map/ppermute | solution.py:297
  78.0 3.5 %collective-permute-start.11 = (f32[1,128]{1,0:T(1,128)S(1)}, f32[1,128]{1,0:T(1,128)S(1)}, u32[]{:S(2)}, u32[]{:S(2)}) collective-permute-start(f32[1,128]{1,0:T(1,128)S(1)} %add.64), channel_id=1, source_target_pairs={{0,16},{4,20},{8,24},{12,28},{16,0},{20,4},{24,8},{28,12},{1,17},{... | collective-permute-start | bytes 1544 | tf_op jit(solution)/shard_map/ppermute | solution.py:297
  81.5 3.5 %collective-permute-start.12 = (f32[1,128]{1,0:T(1,128)S(1)}, f32[1,128]{1,0:T(1,128)S(1)}, u32[]{:S(2)}, u32[]{:S(2)}) collective-permute-start(f32[1,128]{1,0:T(1,128)S(1)} %add.65), channel_id=1, source_target_pairs={{0,1},{1,0},{2,3},{3,2},{4,5},{5,4},{6,7},{7,6},{8,9},{9,8},{10,11... | collective-permute-start | bytes 1544 | tf_op jit(solution)/shard_map/ppermute | solution.py:297
  85.1 14.1 %collective-permute-start.13 = (f32[1,128]{1,0:T(1,128)S(1)}, f32[1,128]{1,0:T(1,128)S(1)}, u32[]{:S(2)}, u32[]{:S(2)}) collective-permute-start(f32[1,128]{1,0:T(1,128)S(1)} %add.66), channel_id=1, source_target_pairs={{0,2},{1,3},{2,0},{3,1},{4,6},{5,7},{6,4},{7,5},{8,10},{9,11},{10,... | collective-permute-start | bytes 1544 | tf_op jit(solution)/shard_map/ppermute | solution.py:297
  88.7 11.0 %collective-permute-start.8 = (f32[8,128,128]{2,1,0:T(8,128)S(1)}, f32[8,128,128]{2,1,0:T(8,128)S(1)}, u32[]{:S(2)}, u32[]{:S(2)}) collective-permute-start(f32[8,128,128]{2,1,0:T(8,128)S(1)} %fusion), channel_id=1, source_target_pairs={{4,0},{5,1},{6,2},{7,3}} | collective-permute-start | bytes 1572872 | tf_op jit(solution)/shard_map/ppermute | solution.py:392
  90.3 9.5 %copy-start.12 = (f32[8,128,256]{2,1,0:T(8,128)S(1)}, f32[8,128,256]{2,1,0:T(8,128)}, u32[]{:S(2)}) copy-start(f32[8,128,256]{2,1,0:T(8,128)} %copy-done.11) | copy-start | bytes 3145732
  (3 other events, 2.4 us)

commit v3 on v2

--- a/solution.py
+++ b/solution.py
@@ -9,8 +9,9 @@
 
 HEADS = 8
 DIM = 128
-GROUP = 8
 BASE = 16
+ROWS = HEADS * DIM
+META = 8
 HIGHEST = lax.Precision.HIGHEST
 F32 = jnp.float32
 BF16 = jnp.bfloat16
@@ -59,6 +60,22 @@
     return ref[:, DIM * j : DIM * (j + 1)]
 
 
+def block(ref, j):
+    return ref.at[DIM * j : DIM * (j + 1)]
+
+
+def notes(*values):
+    lane = lax.broadcasted_iota(jnp.int32, (META, DIM), 1)
+    out = jnp.zeros((META, DIM), F32)
+    for at, value in enumerate(values):
+        out = jnp.where(lane == at, value, out)
+    return out
+
+
+def note(rows, at):
+    return rows[:1, at : at + 1]
+
+
 def put(ref, j, value):
     ref[:, DIM * j : DIM * (j + 1)] = value.astype(ref.dtype)
 
@@ -68,10 +85,9 @@
 
 
 def logit_of(beta_ref, j):
-    at = pl.program_id(0) * GROUP + j
     beta = jnp.transpose(beta_ref[...])
     lane = lax.broadcasted_iota(jnp.int32, beta.shape, 1)
-    return jnp.sum(jnp.where(lane == at, beta, 0.0), axis=1, keepdims=True)
+    return jnp.sum(jnp.where(lane == j, beta, 0.0), axis=1, keepdims=True)
 
 
 def base_inverses(blocks):
@@ -130,10 +146,10 @@
     return ts
 
 
-def kernel_a(ids_ref, k_ref, v_ref, beta_ref, at_ref, bt_ref, th_ref, tl_ref, z_ref):
+def kernel_a(ids_ref, k_ref, v_ref, beta_ref, ab_ref, th_ref, tl_ref, z_ref):
     same, ii, jj, keep, tail, through = id_masks(ids_ref)
     strict = same & (ii > jj)
-    heads = range(GROUP)
+    heads = range(HEADS)
     ks = [head(k_ref, j) for j in heads]
     k32 = [k.astype(F32) for k in ks]
     iks = [inv_norm(k) for k in k32]
@@ -170,11 +186,13 @@
     for j in heads:
         right = writes(head(v_ref, j).astype(F32), k32[j], rates[j], iks[j], keep)
         both = dot3(split(zs[j]), split(right))
-        bt_ref[j] = both[:, :DIM]
-        at_ref[j] = eye * through - both[:, DIM:]
+        block(ab_ref, j)[...] = eye * through - both[:, DIM:]
+        block(ab_ref, HEADS + j)[...] = both[:, :DIM]
         th_ref[j] = fulls[j][0]
         tl_ref[j] = fulls[j][1]
         z_ref[j] = zs[j]
+    row = ids_ref[...].astype(F32)
+    ab_ref[2 * ROWS :] = notes(row[:, :1], row[:, row.shape[1] - 1 :], 1.0)
 
 
 def writes(value, key, rate, ik, keep):
@@ -186,7 +204,7 @@
 ):
     same, ii, jj, keep, tail, through = id_masks(ids_ref)
     causal = same & (ii >= jj)
-    for j in range(GROUP):
+    for j in range(HEADS):
         q, k = head(q_ref, j), head(k_ref, j)
         k32 = k.astype(F32)
         rate = jax.nn.sigmoid(logit_of(beta_ref, j))
@@ -199,13 +217,70 @@
         uw_ref[j] = uw
 
 
-def kernel_c(q_ref, o_ref, e_ref, s_ref, cot_ref, gain_ref, y_ref, do_ref, c_ref, dg_ref):
+def kernel_join(ids_ref, ab_ref, prev_ref, both_ref, mid_ref, map_ref):
+    row = ids_ref[...].astype(F32)
+    last = row[:, row.shape[1] - 1 :]
+    before = prev_ref[2 * ROWS :]
+    joined = (note(before, 1) == row[:, :1]).astype(F32)
+    for j in range(HEADS):
+        right = jnp.concatenate(
+            [block(prev_ref, j)[...], block(prev_ref, HEADS + j)[...]], axis=1
+        )
+        made = joined * dot3(split(block(ab_ref, j)[...]), split(right))
+        matrix, offset = made[:, :DIM], made[:, DIM:] + block(ab_ref, HEADS + j)[...]
+        block(both_ref, j)[...] = matrix
+        block(map_ref, j)[...] = matrix
+        block(both_ref, HEADS + j)[...] = offset
+        block(mid_ref, j)[...] = offset
+    tail = notes(note(before, 0), last, 1.0)
+    both_ref[2 * ROWS :] = tail
+    mid_ref[ROWS:] = tail
+
+
+def kernel_c(
+    ids_ref, q_ref, o_ref, e_ref, p1_ref, p3_ref, m2_ref, m4_ref, m5_ref, cot_ref, gain_ref,
+    y_ref, do_ref, c_ref, s_ref, dg_ref,
+):
+    first = ids_ref[...].astype(F32)[:, :1]
+    before = p1_ref[2 * ROWS :] + p3_ref[2 * ROWS :]
+    middle = m2_ref[ROWS:] + m4_ref[ROWS:] + m5_ref[ROWS:]
+    known = note(before, 2)
+    inner = (note(middle, 1) == note(before, 0)).astype(F32)
+    direct = (1.0 - known) * (note(middle, 1) == first).astype(F32)
+    joined = known * (note(before, 1) == first).astype(F32)
+    states = []
+    for j in range(HEADS):
+        mid = block(m2_ref, j)[...] + block(m4_ref, j)[...] + block(m5_ref, j)[...]
+        matrix = block(p1_ref, j)[...] + block(p3_ref, j)[...]
+        offset = block(p1_ref, HEADS + j)[...] + block(p3_ref, HEADS + j)[...]
+        made = dot3(split(matrix), split(inner * mid)) + offset
+        states.append(joined * made + direct * mid)
+        s_ref[j] = states[j]
+    norm_part(
+        states, joined + direct, q_ref, o_ref, e_ref, cot_ref, gain_ref, y_ref, do_ref, c_ref,
+        dg_ref,
+    )
+
+
+def kernel_c_known(
+    joined_ref, q_ref, o_ref, e_ref, s_ref, cot_ref, gain_ref, y_ref, do_ref, c_ref, dg_ref
+):
+    states = [s_ref[j] for j in range(HEADS)]
+    norm_part(
+        states, joined_ref[...], q_ref, o_ref, e_ref, cot_ref, gain_ref, y_ref, do_ref, c_ref,
+        dg_ref,
+    )
+
+
+def norm_part(
+    states, joined, q_ref, o_ref, e_ref, cot_ref, gain_ref, y_ref, do_ref, c_ref, dg_ref
+):
     gain = gain_ref[...]
     dgain = jnp.zeros((1, DIM), F32)
-    for j in range(GROUP):
+    for j in range(HEADS):
         iq = inv_norm(head(q_ref, j).astype(F32))
         effective = split(head(e_ref, j))
-        raw = head(o_ref, j) + dot3(effective, split(s_ref[j]))
+        raw = head(o_ref, j) + dot3(effective, split(states[j]))
         out = raw * iq
         inv = lax.rsqrt(jnp.mean(out * out, axis=-1, keepdims=True) + 1e-05)
         unit = out * inv
@@ -216,13 +291,28 @@
         dout = inv * (pulled - unit * jnp.mean(pulled * unit, axis=-1, keepdims=True))
         draw = dout * iq
         put(do_ref, j, draw)
-        c_ref[j] = dot3(effective, split(draw), TN)
-
-    @pl.when(pl.program_id(0) == 0)
-    def _():
-        dg_ref[...] = jnp.zeros_like(dg_ref)
-
-    dg_ref[...] += dgain
+        block(c_ref, j)[...] = joined * dot3(effective, split(draw), TN)
+    c_ref[ROWS:] = notes(joined)
+    dg_ref[...] = dgain
+
+
+def kernel_back(ab_ref, c_ref, back_ref, out_ref):
+    joined = note(c_ref[ROWS:], 0)
+    for j in range(HEADS):
+        made = dot3(split(block(ab_ref, j)[...]), split(block(back_ref, j)[...]), TN)
+        block(out_ref, j)[...] = block(c_ref, j)[...] + joined * made
+    out_ref[ROWS:] = c_ref[ROWS:]
+
+
+def kernel_back_far(ab_ref, c_ref, map_ref, h_ref, far_ref, near_ref, g_ref, out_ref):
+    joined = note(c_ref[ROWS:], 0)
+    beyond = note(h_ref[ROWS:], 0)
+    for j in range(HEADS):
+        far = dot3(split(block(map_ref, j)[...]), split(block(far_ref, j)[...]), TN)
+        back = block(near_ref, j)[...] + block(h_ref, j)[...] + beyond * far
+        g_ref[j] = back
+        made = dot3(split(block(ab_ref, j)[...]), split(back), TN)
+        block(out_ref, j)[...] = block(c_ref, j)[...] + joined * made
 
 
 def kernel_d(
@@ -231,7 +321,7 @@
 ):
     same, ii, jj, keep, tail, through = id_masks(ids_ref)
     causal = same & (ii >= jj)
-    for j in range(GROUP):
+    for j in range(HEADS):
         q, k = head(q_ref, j), head(k_ref, j)
         q32 = q.astype(F32)
         state = split(s_ref[j])
@@ -252,7 +342,7 @@
 
 
 def kernel_e(
-    ids_ref, k_ref, v_ref, beta_ref, z_ref, u_ref, dr_ref, dkl_ref, s_ref, g_ref,
+    ids_ref, k_ref, v_ref, beta_ref, z_ref, u_ref, dr_ref, dkl_ref, s_ref, g_ref, h_ref,
     dk_ref, dv_ref, db_ref,
 ):
     same, ii, jj, keep, tail, through = id_masks(ids_ref)
@@ -260,7 +350,7 @@
     shape = (db_ref.shape[1], db_ref.shape[0])
     lane = lax.broadcasted_iota(jnp.int32, shape, 1)
     dbeta = jnp.zeros(shape, F32)
-    heads = range(GROUP)
+    heads = range(HEADS)
     for j in heads:
         k = head(k_ref, j)
         k32 = k.astype(F32)
@@ -269,12 +359,11 @@
         rate = jax.nn.sigmoid(logit)
         update = head(u_ref, j)
         updates = split(update)
-        back = split(g_ref[j])
+        back = split(g_ref[j] + block(h_ref, j)[...])
         dright = head(dr_ref, j) + dot3(split(z_ref[j]), back, TN)
         put(dv_ref, j, dright * (rate * ik))
-        at = pl.program_id(0) * GROUP + j
         dlogit = jax.nn.sigmoid(-logit) * jnp.sum(dright * update, axis=-1, keepdims=True)
-        dbeta = jnp.where(lane == at, dlogit, dbeta)
+        dbeta = jnp.where(lane == j, dlogit, dbeta)
         scaled = dright * (rate * ik * ik)
         inner = split(jnp.where(strict, -dot3(split(scaled), updates, NT), 0.0))
         dk = head(dkl_ref, j) + (dot2(inner, k) + dot2(inner, k, TN))
@@ -283,11 +372,7 @@
         dk = dk - k32 * (ik * ik * jnp.sum(k32 * dk, axis=-1, keepdims=True))
         put(dk_ref, j, dk)
 
-    @pl.when(pl.program_id(0) == 0)
-    def _():
-        db_ref[...] = jnp.zeros_like(db_ref)
-
-    db_ref[...] += jnp.transpose(dbeta)
+    db_ref[...] = jnp.transpose(dbeta)
 
 
 def exchange_sum(value, axis):
@@ -299,116 +384,130 @@
     return value
 
 
-def call(kernel, ins, outs, kinds, flops, name):
-    tokens = None
-    for kind, arg in zip(kinds[0], ins):
-        if kind == "wide":
-            tokens = arg.shape[0]
-    specs = {
-        "wide": pl.BlockSpec((tokens, GROUP * DIM), lambda h: (0, h)),
-        "state": pl.BlockSpec((GROUP, DIM, DIM), lambda h: (h, 0, 0)),
-        "square": pl.BlockSpec((GROUP, tokens, tokens), lambda h: (h, 0, 0)),
-        "z": pl.BlockSpec((GROUP, DIM, tokens), lambda h: (h, 0, 0)),
-        "uw": pl.BlockSpec((GROUP, tokens, 2 * DIM), lambda h: (h, 0, 0)),
-        "ids": pl.BlockSpec((1, tokens), lambda h: (0, 0)),
-        "beta": pl.BlockSpec((HEADS, tokens), lambda h: (0, 0)),
-        "row": pl.BlockSpec((1, DIM), lambda h: (0, 0)),
-    }
+def call(kernel, ins, outs, flops, name, limit=16):
     return pl.pallas_call(
         kernel,
-        grid=(HEADS // GROUP,),
-        in_specs=[specs[kind] for kind in kinds[0]],
-        out_specs=[specs[kind] for kind in kinds[1]],
         out_shape=outs,
-        compiler_params=pltpu.CompilerParams(vmem_limit_bytes=16 * 1024 * 1024),
+        compiler_params=pltpu.CompilerParams(vmem_limit_bytes=limit * 1024 * 1024),
         cost_estimate=pl.CostEstimate(flops=flops, bytes_accessed=4_000_000, transcendentals=0),
         name=name,
     )(*ins)
 
 
-def local(
-    query_heads, key_heads, value_heads, beta_logits, segment_ids, output_cotangent, norm_gain
-):
-    q, k, v = query_heads[0], key_heads[0], value_heads[0]
-    beta, ids, cot = jnp.transpose(beta_logits[0]), segment_ids, output_cotangent[0]
-    gain = norm_gain[None]
-    tokens = q.shape[0]
-    spans = lax.axis_size("seq")
-    here = lax.axis_index("seq")
+def shape(*sizes, dtype=F32):
+    return jax.ShapeDtypeStruct(sizes, dtype)
+
+
+def send(value, pairs):
+    return lax.ppermute(value, "seq", pairs)
+
+
+def relay_forward(ab, ids, spans):
     half = spans // 2
-
-    wide = jax.ShapeDtypeStruct((tokens, HEADS * DIM), F32)
-    wide16 = jax.ShapeDtypeStruct((tokens, HEADS * DIM), BF16)
-    states = jax.ShapeDtypeStruct((HEADS, DIM, DIM), F32)
-    square = jax.ShapeDtypeStruct((HEADS, tokens, tokens), BF16)
-    uw_shape = jax.ShapeDtypeStruct((HEADS, tokens, 2 * DIM), F32)
-    unit = 2 * HEADS * tokens**3
-
-    prior = lax.ppermute(ids[:, tokens - 1 :], "seq", [(s, s + 1) for s in range(spans - 1)])
-    joined = ((prior == ids[:, :1]) & (here > 0)).astype(F32)[:, :, None]
-
-    z_shape = jax.ShapeDtypeStruct((HEADS, DIM, tokens), F32)
-    at, bt, th, tl, z = call(
-        kernel_a, (ids, k, v, beta), (states, states, square, square, z_shape),
-        (("ids", "wide", "wide", "beta"), ("state", "state", "square", "square", "z")),
-        20 * unit, "span_state",
-    )
-    o0, eff, uw = call(
-        kernel_b, (ids, q, k, v, beta, th, tl), (wide, wide, uw_shape),
-        (("ids", "wide", "wide", "wide", "beta", "square", "square"), ("wide", "wide", "uw")),
-        8 * unit, "span_out",
-    )
-
-    def advance(matrix, state, dims):
-        return lax.dot_general(matrix, state, dims, precision=HIGHEST, preferred_element_type=F32)
-
-    FWD = (((2,), (1,)), ((0,), (0,)))
-    BWD = (((1,), (1,)), ((0,), (0,)))
-
+    at = ab[:ROWS].reshape(HEADS, DIM, DIM)
+    bt = ab[ROWS : 2 * ROWS].reshape(HEADS, DIM, DIM)
+    prior = send(ids[:, ids.shape[1] - 1 :], [(s, s + 1) for s in range(spans - 1)])
+    joined = (prior == ids[:, :1]).astype(F32)
     entering = jnp.zeros((HEADS, DIM, DIM), F32)
     outgoing = bt
     for turn in range(half):
         pairs = [(turn, turn + 1)]
         if turn == 0:
             pairs += [(s, s + 1) for s in range(half, spans - 1)]
-        entering = entering + joined * lax.ppermute(outgoing, "seq", pairs)
+        entering = entering + joined[:, :, None] * send(outgoing, pairs)
         if turn < half - 1:
-            outgoing = advance(at, entering, FWD) + bt
-
-    mixed, draw, cs, dgain = call(
-        kernel_c, (q, o0, eff, entering, cot, gain),
-        (wide16, wide, states, jax.ShapeDtypeStruct((1, DIM), F32)),
-        (("wide", "wide", "wide", "state", "wide", "row"), ("wide", "wide", "state", "row")),
-        3 * unit, "span_norm",
-    )
-    gain_total = exchange_sum(exchange_sum(dgain, "seq"), "dp")[0]
-
+            dims = (((2,), (1,)), ((0,), (0,)))
+            outgoing = lax.dot_general(at, entering, dims, precision=HIGHEST) + bt
+    return entering, joined
+
+
+def relay_backward(ab, c, spans):
+    half = spans // 2
+    at = ab[:ROWS].reshape(HEADS, DIM, DIM)
+    joined = c[ROWS : ROWS + 1, :1]
+    cs = c[:ROWS].reshape(HEADS, DIM, DIM)
     back = jnp.zeros((HEADS, DIM, DIM), F32)
-    outgoing = joined * cs
+    outgoing = cs
     for turn in range(half):
         pairs = [(half - turn, half - turn - 1)]
         if turn == 0:
             pairs += [(s, s - 1) for s in range(half + 1, spans)]
-        back = back + lax.ppermute(outgoing, "seq", pairs)
+        back = back + send(outgoing, pairs)
         if turn < half - 1:
-            outgoing = joined * (advance(at, back, BWD) + cs)
-
+            dims = (((1,), (1,)), ((0,), (0,)))
+            outgoing = lax.dot_general(at, back, dims, precision=HIGHEST) * joined + cs
+    return back
+
+
+def local(
+    query_heads, key_heads, value_heads, beta_logits, segment_ids, output_cotangent, norm_gain
+):
+    q, k, v = query_heads[0], key_heads[0], value_heads[0]
+    beta, ids, cot = jnp.transpose(beta_logits[0]), segment_ids, output_cotangent[0]
+    gain = norm_gain[None]
+    tokens = q.shape[0]
+    spans = lax.axis_size("seq")
+    short = spans == 8
+
+    wide, wide16 = shape(tokens, ROWS), shape(tokens, ROWS, dtype=BF16)
+    states = shape(HEADS, DIM, DIM)
+    square = shape(HEADS, tokens, tokens, dtype=BF16)
+    one, two = shape(ROWS + META, DIM), shape(2 * ROWS + META, DIM)
+    row = shape(1, DIM)
+    unit = 2 * HEADS * tokens**3
+
+    ab, th, tl, z = call(
+        kernel_a, (ids, k, v, beta), (two, square, square, shape(HEADS, DIM, tokens)),
+        20 * unit, "span_state", 60,
+    )
+    if short:
+        r1 = send(ab, [(0, 1), (2, 3), (4, 5), (5, 6), (6, 7)])
+        pair, mid, pair_map = call(
+            kernel_join, (ids, ab, r1), (two, one, shape(ROWS, DIM)), unit, "join"
+        )
+        r3 = send(pair, [(3, 4)])
+        r2 = send(mid, [(1, 4)])
+        r4 = send(mid, [(1, 2)])
+    o0, eff, uw = call(
+        kernel_b, (ids, q, k, v, beta, th, tl),
+        (wide, wide, shape(HEADS, tokens, 2 * DIM)), 8 * unit, "span_out",
+    )
+    if short:
+        r5 = send(r4, [(2, 3)])
+        far_map = send(pair_map, [(3, 1)])
+        mixed, draw, c, entering, dgain = call(
+            kernel_c, (ids, q, o0, eff, r1, r3, r2, r4, r5, cot, gain),
+            (wide16, wide, one, states, row), 4 * unit, "span_norm",
+        )
+        n1 = send(c, [(3, 2)])
+        n3 = send(c, [(4, 1)])
+        n4 = send(c, [(4, 3), (5, 4), (6, 5), (7, 6)])
+        h = call(kernel_back, (ab, c, n1), one, unit, "back")
+        n2 = send(h, [(2, 1)])
+    else:
+        entering, joined = relay_forward(ab, ids, spans)
+        mixed, draw, c, dgain = call(
+            kernel_c_known, (joined, q, o0, eff, entering, cot, gain),
+            (wide16, wide, one, row), 4 * unit, "span_norm",
+        )
     dq, update, dright, dkl = call(
         kernel_d, (ids, q, k, th, tl, draw, uw, entering), (wide16, wide, wide, wide),
-        (
-            ("ids", "wide", "wide", "square", "square", "wide", "uw", "state"),
-            ("wide", "wide", "wide", "wide"),
-        ),
         12 * unit, "span_query_grad",
     )
+    if short:
+        back, last = call(
+            kernel_back_far, (ab, c, far_map, n2, n3, n4), (states, shape(ROWS, DIM)), unit,
+            "back_far",
+        )
+        far = send(last, [(1, 0), (3, 2)])
+        last, dgain = lax.optimization_barrier((last, dgain))
+    else:
+        back = relay_backward(ab, c, spans)
+        far = jnp.zeros((ROWS, DIM), F32)
+    gain_total = exchange_sum(exchange_sum(dgain, "seq"), "dp")[0]
     dk, dv, dbeta = call(
-        kernel_e, (ids, k, v, beta, z, update, dright, dkl, entering, back),
-        (wide16, wide16, jax.ShapeDtypeStruct((HEADS, tokens), F32)),
-        (
-            ("ids", "wide", "wide", "beta", "z", "wide", "wide", "wide", "state", "state"),
-            ("wide", "wide", "beta"),
-        ),
-        12 * unit, "span_key_grad",
+        kernel_e, (ids, k, v, beta, z, update, dright, dkl, entering, back, far),
+        (wide16, wide16, shape(HEADS, tokens)), 12 * unit, "span_key_grad",
     )
     return (mixed[None], dq[None], dk[None], dv[None], jnp.transpose(dbeta)[None], gain_total)
 

time: 109 us -> 93.8 us (0.86); the launches traced: 107 us -> 93.4 us
  matrix products: 8.24 us -> 0 us
  Pallas kernels: 28.4 us -> 33.2 us
  starting transfers between devices: 48.7 us -> 44.3 us
  waiting for transfers between devices: 12.6 us -> 10.8 us
  other arithmetic: 1.98 us -> 0.53 us
  local copies, waits for them, and re-layouts: 5.05 us -> 3.71 us
  between operations: 2.23 us -> 0.93 us
    dot_general x6 -> x0, matrix products: 8.24 us -> none  [advance(): lax.dot_general(matrix, state, dims, precision=HIGHEST, preferred_element...]
    pallas_call x5 -> x8, Pallas kernels: 28.4 us -> 33.2 us  [call(): pl.pallas_call(kernel, out_shape=outs, compiler_params=pltpu.CompilerPara...]
    ppermute x5, starting transfers between devices: 37.7 us -> 33.8 us  [exchange_sum(): lax.ppermute(value, axis, [(i, i ^ step) for i in range(size)])]
    ppermute x5, waiting for transfers between devices: 12.2 us -> 8.34 us  [exchange_sum(): lax.ppermute(value, axis, [(i, i ^ step) for i in range(size)])]
    ppermute x9 -> x11, waiting for transfers between devices: 0.42 us -> 2.44 us  [send(): return lax.ppermute(value, 'seq', pairs)]
    add x4 -> x0, other arithmetic: 1.41 us -> none  [the longest x1 1.23 us: local(): entering = entering + joined * lax.ppermute(outgoing, 'seq', pairs)]
    unnamed x26 -> x28, local copies, waits for them, and re-layouts: 4.47 us -> 3.71 us
    ppermute x9 -> x11, starting transfers between devices: 11 us -> 10.5 us  [send(): return lax.ppermute(value, 'seq', pairs)]
  transfers between devices with their start and end apart: 14 -> 16, of which waited for: 5 -> 5; matrix products, arithmetic and copies ran while one was open for 2% -> 1% of each run, Pallas kernels for 11% -> 14%
where the time goes in v3:
time: 93.8 us; the launch traced here: 93.4 us
  starting transfers between devices  44.3 us (47%)
  Pallas kernels  33.2 us (35%)
  waiting for transfers between devices  10.8 us (12%)
  local copies, waits for them, and re-layouts  3.71 us (4%)
    ppermute x5, starting transfers between devices, exchange_sum(): lax.ppermute(value, axis, [(i, i ^ step) for i in range(size)])  33.8 us
    pallas_call x8, Pallas kernels, call(): pl.pallas_call(kernel, out_shape=outs, compiler_params=pltpu.CompilerPara...  33.2 us
    ppermute x11, starting transfers between devices, send(): return lax.ppermute(value, 'seq', pairs)  10.5 us
    ppermute x5, waiting for transfers between devices, exchange_sum(): lax.ppermute(value, axis, [(i, i ^ step) for i in range(size)])  8.34 us
    unnamed x28, local copies, waits for them, and re-layouts  3.71 us
    ppermute x11, waiting for transfers between devices, send(): return lax.ppermute(value, 'seq', pairs)  2.44 us
  transfers between devices with their start and end apart: 16, of which 5 were waited for; matrix products, arithmetic and copies ran while one was open for 1% of the time, Pallas kernels for 14%

profile of v3, /device:TPU:0, one launch (start us, length us, event | category | flops | bytes accessed | tf_op | source)
XLA Modules:
  0.0 93.4 jit_solution(9251581734246357147)
XLA Ops:
  0.6 8.3 %span_state.1 = (f32[2056,128]{1,0:T(8,128)}, bf16[8,256,256]{2,1,0:T(8,128)(2,1)}, bf16[8,256,256]{2,1,0:T(8,128)(2,1)}, f32[8,128,256]{2,1,0:T(8,128)}) custom-call(s32[1,256]{1,0:T(1,128)} %ids_ref.11, bf16[256,1024]{1,0:T(8,128)(2,1)} %bitcast.22, bf16[256,1024]{1,0:T(8,128)(2,1)} %bitcast.26, f32[8,256]{1,0:T(8,128)} %bitcast.29), custom_call_target="tpu_custom_call" | custom-call | flops 5368709120 | bytes 4000000 | tf_op jit(solution)/shard_map/span_state/pallas_call | solution.py:388
  8.9 2.4 %collective-permute-start = (f32[2056,128]{1,0:T(8,128)}, f32[2056,128]{1,0:T(8,128)S(1)}, u32[]{:S(2)}, u32[]{:S(2)}) collective-permute-start(f32[2056,128]{1,0:T(8,128)} %get-tuple-element.35.ab_ref), channel_id=1, source_target_pairs={{0,4},{8,12},{16,20},{20,24},{24,28},{1,5},{9,13},{17,21},{21,25},... | collective-permute-start | bytes 3158024 | tf_op jit(solution)/shard_map/ppermute | solution.py:402
  11.3 2.4 %collective-permute-done.prev_ref.p1_ref = f32[2056,128]{1,0:T(8,128)S(1)} collective-permute-done((f32[2056,128]{1,0:T(8,128)}, f32[2056,128]{1,0:T(8,128)S(1)}, u32[]{:S(2)}, u32[]{:S(2)}) %collective-permute-start) | collective-permute-done | bytes 1052704 | tf_op jit(solution)/shard_map/ppermute | solution.py:402
  13.8 1.2 %copy-done = f32[2056,128]{1,0:T(8,128)S(1)} copy-done((f32[2056,128]{1,0:T(8,128)S(1)}, f32[2056,128]{1,0:T(8,128)}, u32[]{:S(2)}) %copy-start) | copy-done | bytes 1052696
  15.6 0.7 collective-permute-start.3
  16.3 0.7 collective-permute-start.1
  17.1 0.7 collective-permute-start.2
  17.8 0.9 collective-permute-start.4
  18.7 1.2 %copy-done.9 = bf16[8,256,256]{2,1,0:T(8,128)(2,1)S(1)} copy-done((bf16[8,256,256]{2,1,0:T(8,128)(2,1)S(1)}, bf16[8,256,256]{2,1,0:T(8,128)(2,1)}, u32[]{:S(2)}) %copy-start.9) | copy-done | bytes 1048600
  19.9 1.2 %copy-done.11 = bf16[8,256,256]{2,1,0:T(8,128)(2,1)S(1)} copy-done((bf16[8,256,256]{2,1,0:T(8,128)(2,1)S(1)}, bf16[8,256,256]{2,1,0:T(8,128)(2,1)}, u32[]{:S(2)}) %copy-start.11) | copy-done | bytes 1048600
  21.2 3.5 %span_out.1 = (f32[256,1024]{1,0:T(8,128)S(1)}, f32[256,1024]{1,0:T(8,128)S(1)}, f32[8,256,256]{2,1,0:T(8,128)S(1)}) custom-call(s32[1,256]{1,0:T(1,128)S(1)} %copy-done.4, bf16[256,1024]{1,0:T(8,128)(2,1)S(1)} %bitcast.18, bf16[256,1024]{1,0:T(8,128)(2,1)S(1)} %bitcast.23, bf16[256,1024]{1,0:T(8,128)(2,1)S(1)} %bitcast.27, f32[8,256]{1,0:T(8,128)S(1)} %bitcast.30, ...), custom_call_target="tpu_custom_call" | custom-call | flops 2147483648 | bytes 4000000 | tf_op jit(solution)/shard_map/span_out/pallas_call | solution.py:388
  24.7 3.2 %span_norm.1 = (bf16[256,1024]{1,0:T(8,128)(2,1)}, f32[256,1024]{1,0:T(8,128)S(1)}, f32[1032,128]{1,0:T(8,128)S(1)}, f32[8,128,128]{2,1,0:T(8,128)S(1)}, f32[1,128]{1,0:T(1,128)S(1)}) custom-call(s32[1,256]{1,0:T(1,128)S(1)} %copy-done.4, bf16[256,1024]{1,0:T(8,128)(2,1)S(1)} %bitcast.19, f32[256,1024]{1,0:T(8,128)S(1)} %get-tuple-element.33.o_ref, ...), custom_call_target="tpu_custom_call" | custom-call | flops 1073741824 | bytes 4000000 | tf_op jit(solution)/shard_map/span_norm/pallas_call | solution.py:388
  29.4 0.7 collective-permute-start.8
  31.2 0.8 collective-permute-start.5
  32.1 0.8 back_far.1
  32.9 29.6 %collective-permute-start.11 = (f32[1,128]{1,0:T(1,128)S(1)}, f32[1,128]{1,0:T(1,128)S(1)}, u32[]{:S(2)}, u32[]{:S(2)}) collective-permute-start(f32[1,128]{1,0:T(1,128)S(1)} %get-tuple-element.55), channel_id=1, source_target_pairs={{0,4},{4,0},{8,12},{12,8},{16,20},{20,16},{24,28},{28,24},{1,5},{5... | collective-permute-start | bytes 1544 | tf_op jit(solution)/shard_map/ppermute | solution.py:382
  62.5 0.8 collective-permute-done.11
  63.3 3.5 %collective-permute-done.12 = f32[1,128]{1,0:T(1,128)S(1)} collective-permute-done((f32[1,128]{1,0:T(1,128)S(1)}, f32[1,128]{1,0:T(1,128)S(1)}, u32[]{:S(2)}, u32[]{:S(2)}) %collective-permute-start.12) | collective-permute-done | bytes 544 | tf_op jit(solution)/shard_map/ppermute | solution.py:382
  66.9 3.5 %collective-permute-done.13 = f32[1,128]{1,0:T(1,128)S(1)} collective-permute-done((f32[1,128]{1,0:T(1,128)S(1)}, f32[1,128]{1,0:T(1,128)S(1)}, u32[]{:S(2)}, u32[]{:S(2)}) %collective-permute-start.13) | collective-permute-done | bytes 544 | tf_op jit(solution)/shard_map/ppermute | solution.py:382
  70.4 1.6 %collective-permute-start.14 = (f32[1,128]{1,0:T(1,128)S(1)}, f32[1,128]{1,0:T(1,128)S(1)}, u32[]{:S(2)}, u32[]{:S(2)}) collective-permute-start(f32[1,128]{1,0:T(1,128)S(1)} %add.17), channel_id=1, source_target_pairs={{0,1},{1,0},{2,3},{3,2},{4,5},{5,4},{6,7},{7,6},{8,9},{9,8},{10,11... | collective-permute-start | bytes 1544 | tf_op jit(solution)/shard_map/ppermute | solution.py:382
  72.0 1.5 %collective-permute-start.10 = (f32[1024,128]{1,0:T(8,128)S(1)}, f32[1024,128]{1,0:T(8,128)S(1)}, u32[]{:S(2)}, u32[]{:S(2)}) collective-permute-start(f32[1024,128]{1,0:T(8,128)S(1)} %get-tuple-element.50), channel_id=1, source_target_pairs={{4,0},{12,8},{5,1},{13,9},{6,2},{14,10},{7,3},{15,11}} | collective-permute-start | bytes 1572872 | tf_op jit(solution)/shard_map/ppermute | solution.py:402
  74.0 2.6 %collective-permute-start.15 = (f32[1,128]{1,0:T(1,128)S(1)}, f32[1,128]{1,0:T(1,128)S(1)}, u32[]{:S(2)}, u32[]{:S(2)}) collective-permute-start(f32[1,128]{1,0:T(1,128)S(1)} %add.18), channel_id=1, source_target_pairs={{0,2},{1,3},{2,0},{3,1},{4,6},{5,7},{6,4},{7,5},{8,10},{9,11},{10,... | collective-permute-start | bytes 1544 | tf_op jit(solution)/shard_map/ppermute | solution.py:382
  76.5 8.9 %span_query_grad.1 = (bf16[256,1024]{1,0:T(8,128)(2,1)}, f32[256,1024]{1,0:T(8,128)S(1)}, f32[256,1024]{1,0:T(8,128)S(1)}, f32[256,1024]{1,0:T(8,128)S(1)}) custom-call(s32[1,256]{1,0:T(1,128)S(1)} %copy-done.4, bf16[256,1024]{1,0:T(8,128)(2,1)S(1)} %bitcast.20, bf16[256,1024]{1,0:T(8,128)(2,1)S(1)} %bitcast.24, bf16[8,256,256]{2,1,0:T(8,128)(2,1)S(1)} %copy-done.10, ...), custom_call_target="tpu_custom_call" | custom-call | flops 3221225472 | bytes 4000000 | tf_op jit(solution)/shard_map/span_query_grad/pallas_call | solution.py:388
  86.0 7.4 %span_key_grad.1 = (bf16[256,1024]{1,0:T(8,128)(2,1)}, bf16[256,1024]{1,0:T(8,128)(2,1)}, f32[8,256]{1,0:T(8,128)}) custom-call(s32[1,256]{1,0:T(1,128)S(1)} %copy-done.4, bf16[256,1024]{1,0:T(8,128)(2,1)S(1)} %bitcast.25, bf16[256,1024]{1,0:T(8,128)(2,1)S(1)} %bitcast.28, f32[8,256]{1,0:T(8,128)S(1)} %bitcast.31, f32[8,128,256]{2,1,0:T(8,128)S(1)} %copy-done.13, ...), custom_call_target="tpu_custom_call" | custom-call | flops 3221225472 | bytes 4000000 | tf_op jit(solution)/shard_map/span_key_grad/pallas_call | solution.py:388
  (49 shorter events, 4.2 us)
Async XLA Ops:
  0.6 13.1 %copy-start.4 = (s32[1,256]{1,0:T(1,128)S(1)}, s32[1,256]{1,0:T(1,128)}, u32[]{:S(2)}) copy-start(s32[1,256]{1,0:T(1,128)} %ids_ref.11) | copy-start | bytes 3076
  8.9 4.8 %collective-permute-start = (f32[2056,128]{1,0:T(8,128)}, f32[2056,128]{1,0:T(8,128)S(1)}, u32[]{:S(2)}, u32[]{:S(2)}) collective-permute-start(f32[2056,128]{1,0:T(8,128)} %get-tuple-element.35.ab_ref), channel_id=1, source_target_pairs={{0,4},{8,12},{16,20},{20,24},{24,28},{1,5},{9,13},{17,21},{21,25},... | collective-permute-start | bytes 3158024 | tf_op jit(solution)/shard_map/ppermute | solution.py:402
  15.0 3.7 %copy-start.6 = (bf16[1,256,1024]{2,1,0:T(8,128)(2,1)S(1)}, bf16[1,256,1024]{2,1,0:T(8,128)(2,1)}, u32[]{:S(2)}) copy-start(bf16[1,256,1024]{2,1,0:T(8,128)(2,1)} %param.8) | copy-start | bytes 1572868
  15.0 3.7 %copy-start.7 = (bf16[1,256,1024]{2,1,0:T(8,128)(2,1)S(1)}, bf16[1,256,1024]{2,1,0:T(8,128)(2,1)}, u32[]{:S(2)}) copy-start(bf16[1,256,1024]{2,1,0:T(8,128)(2,1)} %param.9) | copy-start | bytes 1572868
  15.0 3.7 %copy-start.8 = (f32[1,256,8]{1,2,0:T(8,128)S(1)}, f32[1,256,8]{1,2,0:T(8,128)}, u32[]{:S(2)}) copy-start(f32[1,256,8]{1,2,0:T(8,128)} %param.10) | copy-start | bytes 24580
  15.6 2.1 %collective-permute-start.3 = (f32[1032,128]{1,0:T(8,128)S(1)}, f32[1032,128]{1,0:T(8,128)S(1)}, u32[]{:S(2)}, u32[]{:S(2)}) collective-permute-start(f32[1032,128]{1,0:T(8,128)S(1)} %get-tuple-element.37), channel_id=1, source_target_pairs={{4,8},{5,9},{6,10},{7,11}} | collective-permute-start | bytes 1585160 | tf_op jit(solution)/shard_map/ppermute | solution.py:402
  16.3 8.3 %collective-permute-start.1 = (f32[2056,128]{1,0:T(8,128)S(1)}, f32[2056,128]{1,0:T(8,128)S(1)}, u32[]{:S(2)}, u32[]{:S(2)}) collective-permute-start(f32[2056,128]{1,0:T(8,128)S(1)} %get-tuple-element.36), channel_id=1, source_target_pairs={{12,16},{13,17},{14,18},{15,19}} | collective-permute-start | bytes 3158024 | tf_op jit(solution)/shard_map/ppermute | solution.py:402
  17.1 7.6 %collective-permute-start.2 = (f32[1032,128]{1,0:T(8,128)S(1)}, f32[1032,128]{1,0:T(8,128)S(1)}, u32[]{:S(2)}, u32[]{:S(2)}) collective-permute-start(f32[1032,128]{1,0:T(8,128)S(1)} %get-tuple-element.37), channel_id=1, source_target_pairs={{4,16},{5,17},{6,18},{7,19}} | collective-permute-start | bytes 1585160 | tf_op jit(solution)/shard_map/ppermute | solution.py:402
  17.8 6.9 %collective-permute-start.4 = (f32[1032,128]{1,0:T(8,128)S(1)}, f32[1032,128]{1,0:T(8,128)S(1)}, u32[]{:S(2)}, u32[]{:S(2)}) collective-permute-start(f32[1032,128]{1,0:T(8,128)S(1)} %collective-permute-done.3.m4_ref), channel_id=1, source_target_pairs={{8,12},{9,13},{10,14},{11,15}} | collective-permute-start | bytes 1585160 | tf_op jit(solution)/shard_map/ppermute | solution.py:402
  24.7 5.4 %copy-start.1 = (f32[2056,128]{1,0:T(8,128)S(1)}, f32[2056,128]{1,0:T(8,128)}, u32[]{:S(2)}) copy-start(f32[2056,128]{1,0:T(8,128)} %get-tuple-element.35.ab_ref) | copy-start | bytes 3158020
  28.0 2.1 %collective-permute-start.6 = (f32[1032,128]{1,0:T(8,128)S(1)}, f32[1032,128]{1,0:T(8,128)S(1)}, u32[]{:S(2)}, u32[]{:S(2)}) collective-permute-start(f32[1032,128]{1,0:T(8,128)S(1)} %get-tuple-element.47.c_ref), channel_id=1, source_target_pairs={{12,8},{13,9},{14,10},{15,11}} | collective-permute-start | bytes 1585160 | tf_op jit(solution)/shard_map/ppermute | solution.py:402
  28.7 3.4 %collective-permute-start.9 = (f32[1032,128]{1,0:T(8,128)S(1)}, f32[1032,128]{1,0:T(8,128)S(1)}, u32[]{:S(2)}, u32[]{:S(2)}) collective-permute-start(f32[1032,128]{1,0:T(8,128)S(1)} %get-tuple-element.47.c_ref), channel_id=1, source_target_pairs={{16,12},{20,16},{24,20},{28,24},{17,13},{21,17},{25,21},{29,25},{1... | collective-permute-start | bytes 1585160 | tf_op jit(solution)/shard_map/ppermute | solution.py:402
  29.4 2.7 %collective-permute-start.8 = (f32[1032,128]{1,0:T(8,128)S(1)}, f32[1032,128]{1,0:T(8,128)S(1)}, u32[]{:S(2)}, u32[]{:S(2)}) collective-permute-start(f32[1032,128]{1,0:T(8,128)S(1)} %get-tuple-element.47.c_ref), channel_id=1, source_target_pairs={{16,4},{17,5},{18,6},{19,7}} | collective-permute-start | bytes 1585160 | tf_op jit(solution)/shard_map/ppermute | solution.py:402
  30.5 1.6 %collective-permute-start.7 = (f32[1032,128]{1,0:T(8,128)S(1)}, f32[1032,128]{1,0:T(8,128)S(1)}, u32[]{:S(2)}, u32[]{:S(2)}) collective-permute-start(f32[1032,128]{1,0:T(8,128)S(1)} %back.1), channel_id=1, source_target_pairs={{8,4},{9,5},{10,6},{11,7}} | collective-permute-start | bytes 1585160 | tf_op jit(solution)/shard_map/ppermute | solution.py:402
  31.2 45.3 %copy-start.10 = (bf16[8,256,256]{2,1,0:T(8,128)(2,1)S(1)}, bf16[8,256,256]{2,1,0:T(8,128)(2,1)}, u32[]{:S(2)}) copy-start(bf16[8,256,256]{2,1,0:T(8,128)(2,1)} %get-tuple-element.31.th_ref) | copy-start | bytes 3145732
  31.2 45.3 %copy-start.12 = (bf16[8,256,256]{2,1,0:T(8,128)(2,1)S(1)}, bf16[8,256,256]{2,1,0:T(8,128)(2,1)}, u32[]{:S(2)}) copy-start(bf16[8,256,256]{2,1,0:T(8,128)(2,1)} %get-tuple-element.32.tl_ref) | copy-start | bytes 3145732
  31.2 0.8 collective-permute-start.5
  32.9 30.4 %collective-permute-start.11 = (f32[1,128]{1,0:T(1,128)S(1)}, f32[1,128]{1,0:T(1,128)S(1)}, u32[]{:S(2)}, u32[]{:S(2)}) collective-permute-start(f32[1,128]{1,0:T(1,128)S(1)} %get-tuple-element.55), channel_id=1, source_target_pairs={{0,4},{4,0},{8,12},{12,8},{16,20},{20,16},{24,28},{28,24},{1,5},{5... | collective-permute-start | bytes 1544 | tf_op jit(solution)/shard_map/ppermute | solution.py:382
  63.3 3.5 %collective-permute-start.12 = (f32[1,128]{1,0:T(1,128)S(1)}, f32[1,128]{1,0:T(1,128)S(1)}, u32[]{:S(2)}, u32[]{:S(2)}) collective-permute-start(f32[1,128]{1,0:T(1,128)S(1)} %add.15), channel_id=1, source_target_pairs={{0,8},{4,12},{8,0},{12,4},{16,24},{20,28},{24,16},{28,20},{1,9},{5... | collective-permute-start | bytes 1544 | tf_op jit(solution)/shard_map/ppermute | solution.py:382
  66.9 3.5 %collective-permute-start.13 = (f32[1,128]{1,0:T(1,128)S(1)}, f32[1,128]{1,0:T(1,128)S(1)}, u32[]{:S(2)}, u32[]{:S(2)}) collective-permute-start(f32[1,128]{1,0:T(1,128)S(1)} %add.16), channel_id=1, source_target_pairs={{0,16},{4,20},{8,24},{12,28},{16,0},{20,4},{24,8},{28,12},{1,17},{... | collective-permute-start | bytes 1544 | tf_op jit(solution)/shard_map/ppermute | solution.py:382
  70.4 3.5 %collective-permute-start.14 = (f32[1,128]{1,0:T(1,128)S(1)}, f32[1,128]{1,0:T(1,128)S(1)}, u32[]{:S(2)}, u32[]{:S(2)}) collective-permute-start(f32[1,128]{1,0:T(1,128)S(1)} %add.17), channel_id=1, source_target_pairs={{0,1},{1,0},{2,3},{3,2},{4,5},{5,4},{6,7},{7,6},{8,9},{9,8},{10,11... | collective-permute-start | bytes 1544 | tf_op jit(solution)/shard_map/ppermute | solution.py:382
  72.0 14.0 %collective-permute-start.10 = (f32[1024,128]{1,0:T(8,128)S(1)}, f32[1024,128]{1,0:T(8,128)S(1)}, u32[]{:S(2)}, u32[]{:S(2)}) collective-permute-start(f32[1024,128]{1,0:T(8,128)S(1)} %get-tuple-element.50), channel_id=1, source_target_pairs={{4,0},{12,8},{5,1},{13,9},{6,2},{14,10},{7,3},{15,11}} | collective-permute-start | bytes 1572872 | tf_op jit(solution)/shard_map/ppermute | solution.py:402
  74.0 11.5 %collective-permute-start.15 = (f32[1,128]{1,0:T(1,128)S(1)}, f32[1,128]{1,0:T(1,128)S(1)}, u32[]{:S(2)}, u32[]{:S(2)}) collective-permute-start(f32[1,128]{1,0:T(1,128)S(1)} %add.18), channel_id=1, source_target_pairs={{0,2},{1,3},{2,0},{3,1},{4,6},{5,7},{6,4},{7,5},{8,10},{9,11},{10,... | collective-permute-start | bytes 1544 | tf_op jit(solution)/shard_map/ppermute | solution.py:382
  76.5 9.5 %copy-start.13 = (f32[8,128,256]{2,1,0:T(8,128)S(1)}, f32[8,128,256]{2,1,0:T(8,128)}, u32[]{:S(2)}) copy-start(f32[8,128,256]{2,1,0:T(8,128)} %get-tuple-element.43.z_ref) | copy-start | bytes 3145732
  (6 other events, 14.4 us)

commit v4 on v3

--- a/solution.py
+++ b/solution.py
@@ -40,6 +40,33 @@
 
 def dot2r(a, b, dims=NN):
     return mm(a, b[0], dims) + mm(a, b[1], dims)
+
+
+def cat(parts, axis):
+    return jnp.concatenate(parts, axis=axis)
+
+
+def pack3(a, b):
+    left = cat([a[0], a[1]], 1)
+    right = cat([cat([b[0], b[1]], 1), cat([b[0], jnp.zeros_like(b[0])], 1)], 0)
+    out = mm(left, right)
+    return out[:, :DIM] + out[:, DIM:]
+
+
+def pack3_nt(a, b):
+    left = cat([a[0], a[1]], 1)
+    right = cat([cat([b[0], b[0]], 1), cat([b[1], jnp.zeros_like(b[1])], 1)], 0)
+    out = mm(left, right, NT)
+    return out[:, :DIM] + out[:, DIM:]
+
+
+def outer3(a, b):
+    return mm(cat([a[0], a[1]], 1), cat([b[0], b[0]], 1), NT) + mm(a[0], b[1], NT)
+
+
+def wide3(a, b, dims=NN):
+    out = mm(a[0], cat([b[0], b[1]], 1), dims)
+    return out[:, :DIM] + (out[:, DIM:] + mm(a[1], b[0], dims))
 
 
 def id_masks(ids_ref):
@@ -146,7 +173,20 @@
     return ts
 
 
-def kernel_a(ids_ref, k_ref, v_ref, beta_ref, ab_ref, th_ref, tl_ref, z_ref):
+def kernel_a(
+    ids_in, k_in, v_in, beta_in, ab_ref, th_ref, tl_ref, z_ref,
+    ids_ref, k_ref, v_ref, beta_ref, sems,
+):
+    copies = [
+        pltpu.make_async_copy(source, target, sems.at[at])
+        for at, (source, target) in enumerate(
+            ((ids_in, ids_ref), (k_in, k_ref), (beta_in, beta_ref), (v_in, v_ref))
+        )
+    ]
+    for copy in copies:
+        copy.start()
+    for copy in copies[:3]:
+        copy.wait()
     same, ii, jj, keep, tail, through = id_masks(ids_ref)
     strict = same & (ii > jj)
     heads = range(HEADS)
@@ -183,6 +223,7 @@
         == lax.broadcasted_iota(jnp.int32, (DIM, DIM), 1)
     ).astype(F32)
     zs = [dot2r((k * tail).astype(BF16), full, TN) for k, full in zip(k32, fulls)]
+    copies[3].wait()
     for j in heads:
         right = writes(head(v_ref, j).astype(F32), k32[j], rates[j], iks[j], keep)
         both = dot3(split(zs[j]), split(right))
@@ -200,7 +241,8 @@
 
 
 def kernel_b(
-    ids_ref, q_ref, k_ref, v_ref, beta_ref, th_ref, tl_ref, o_ref, e_ref, uw_ref
+    ids_ref, q_ref, k_ref, v_ref, beta_ref, th_ref, tl_ref, z_ref,
+    o_ref, e_ref, uw_ref, ph_ref, pl_ref, zh_ref, zl_ref,
 ):
     same, ii, jj, keep, tail, through = id_masks(ids_ref)
     causal = same & (ii >= jj)
@@ -208,53 +250,71 @@
         q, k = head(q_ref, j), head(k_ref, j)
         k32 = k.astype(F32)
         rate = jax.nn.sigmoid(logit_of(beta_ref, j))
-        right = writes(head(v_ref, j).astype(F32), k32, rate, inv_norm(k32), keep)
-        uw = dot3((th_ref[j], tl_ref[j]), split(right))
+        right = split(writes(head(v_ref, j).astype(F32), k32, rate, inv_norm(k32), keep))
+        solve = (th_ref[j], tl_ref[j])
+        uw_ref[j] = dot3(solve, right)
         scores = jnp.where(causal, mm(q, k, NT), 0.0)
-        both = dot3(split(scores), split(uw))
+        through_solve = split(dot3(split(scores), solve))
+        both = dot3(through_solve, right)
         put(o_ref, j, both[:, :DIM])
         put(e_ref, j, q.astype(F32) * keep - both[:, DIM:])
-        uw_ref[j] = uw
-
-
-def kernel_join(ids_ref, ab_ref, prev_ref, both_ref, mid_ref, map_ref):
+        ph_ref[j] = jnp.transpose(through_solve[0])
+        pl_ref[j] = jnp.transpose(through_solve[1])
+        ends = split(jnp.transpose(z_ref[j]))
+        put(zh_ref, j, ends[0])
+        put(zl_ref, j, ends[1])
+
+
+def kernel_join(ids_ref, ab_ref, prev_ref, both_ref, mid_ref, side_ref):
     row = ids_ref[...].astype(F32)
     last = row[:, row.shape[1] - 1 :]
     before = prev_ref[2 * ROWS :]
     joined = (note(before, 1) == row[:, :1]).astype(F32)
-    for j in range(HEADS):
-        right = jnp.concatenate(
-            [block(prev_ref, j)[...], block(prev_ref, HEADS + j)[...]], axis=1
-        )
+    maps = lax.axis_index("seq") == 3
+    for j in range(HEADS):
+        right = cat([block(prev_ref, j)[...], block(prev_ref, HEADS + j)[...]], 1)
         made = joined * dot3(split(block(ab_ref, j)[...]), split(right))
-        matrix, offset = made[:, :DIM], made[:, DIM:] + block(ab_ref, HEADS + j)[...]
-        block(both_ref, j)[...] = matrix
-        block(map_ref, j)[...] = matrix
+        block(both_ref, j)[...] = made[:, :DIM]
+        offset = made[:, DIM:] + block(ab_ref, HEADS + j)[...]
         block(both_ref, HEADS + j)[...] = offset
         block(mid_ref, j)[...] = offset
-    tail = notes(note(before, 0), last, 1.0)
-    both_ref[2 * ROWS :] = tail
-    mid_ref[ROWS:] = tail
+        block(side_ref, j)[...] = jnp.where(maps, made[:, :DIM], offset)
+    after = notes(note(before, 0), last, 1.0)
+    both_ref[2 * ROWS :] = after
+    mid_ref[ROWS:] = after
+    side_ref[ROWS:] = after
+
+
+def kernel_apply(both_ref, mid_ref, out_ref):
+    after, middle = both_ref[2 * ROWS :], mid_ref[ROWS:]
+    inner = (note(middle, 1) == note(after, 0)).astype(F32)
+    for j in range(HEADS):
+        made = pack3(split(block(both_ref, j)[...]), split(inner * block(mid_ref, j)[...]))
+        block(out_ref, j)[...] = made + block(both_ref, HEADS + j)[...]
+    out_ref[ROWS:] = after
 
 
 def kernel_c(
-    ids_ref, q_ref, o_ref, e_ref, p1_ref, p3_ref, m2_ref, m4_ref, m5_ref, cot_ref, gain_ref,
+    ids_ref, q_ref, o_ref, e_ref, prev_ref, m2_ref, m3_ref, m4_ref, cot_ref, gain_ref,
     y_ref, do_ref, c_ref, s_ref, dg_ref,
 ):
     first = ids_ref[...].astype(F32)[:, :1]
-    before = p1_ref[2 * ROWS :] + p3_ref[2 * ROWS :]
-    middle = m2_ref[ROWS:] + m4_ref[ROWS:] + m5_ref[ROWS:]
+    before = prev_ref[2 * ROWS :]
+    direct_side = lax.axis_index("seq") != 1
+
+    def side(rows):
+        return jnp.where(direct_side, rows, 0.0)
+
+    middle = side(m2_ref[ROWS:]) + m3_ref[ROWS:] + m4_ref[ROWS:]
     known = note(before, 2)
     inner = (note(middle, 1) == note(before, 0)).astype(F32)
     direct = (1.0 - known) * (note(middle, 1) == first).astype(F32)
     joined = known * (note(before, 1) == first).astype(F32)
     states = []
     for j in range(HEADS):
-        mid = block(m2_ref, j)[...] + block(m4_ref, j)[...] + block(m5_ref, j)[...]
-        matrix = block(p1_ref, j)[...] + block(p3_ref, j)[...]
-        offset = block(p1_ref, HEADS + j)[...] + block(p3_ref, HEADS + j)[...]
-        made = dot3(split(matrix), split(inner * mid)) + offset
-        states.append(joined * made + direct * mid)
+        mid = side(block(m2_ref, j)[...]) + block(m3_ref, j)[...] + block(m4_ref, j)[...]
+        made = pack3(split(block(prev_ref, j)[...]), split(inner * mid))
+        states.append(joined * (made + block(prev_ref, HEADS + j)[...]) + direct * mid)
         s_ref[j] = states[j]
     norm_part(
         states, joined + direct, q_ref, o_ref, e_ref, cot_ref, gain_ref, y_ref, do_ref, c_ref,
@@ -280,7 +340,7 @@
     for j in range(HEADS):
         iq = inv_norm(head(q_ref, j).astype(F32))
         effective = split(head(e_ref, j))
-        raw = head(o_ref, j) + dot3(effective, split(states[j]))
+        raw = head(o_ref, j) + pack3(effective, split(states[j]))
         out = raw * iq
         inv = lax.rsqrt(jnp.mean(out * out, axis=-1, keepdims=True) + 1e-05)
         unit = out * inv
@@ -291,7 +351,7 @@
         dout = inv * (pulled - unit * jnp.mean(pulled * unit, axis=-1, keepdims=True))
         draw = dout * iq
         put(do_ref, j, draw)
-        block(c_ref, j)[...] = joined * dot3(effective, split(draw), TN)
+        block(c_ref, j)[...] = joined * wide3(effective, split(draw), TN)
     c_ref[ROWS:] = notes(joined)
     dg_ref[...] = dgain
 
@@ -299,7 +359,7 @@
 def kernel_back(ab_ref, c_ref, back_ref, out_ref):
     joined = note(c_ref[ROWS:], 0)
     for j in range(HEADS):
-        made = dot3(split(block(ab_ref, j)[...]), split(block(back_ref, j)[...]), TN)
+        made = wide3(split(block(ab_ref, j)[...]), split(block(back_ref, j)[...]), TN)
         block(out_ref, j)[...] = block(c_ref, j)[...] + joined * made
     out_ref[ROWS:] = c_ref[ROWS:]
 
@@ -308,15 +368,15 @@
     joined = note(c_ref[ROWS:], 0)
     beyond = note(h_ref[ROWS:], 0)
     for j in range(HEADS):
-        far = dot3(split(block(map_ref, j)[...]), split(block(far_ref, j)[...]), TN)
+        far = wide3(split(block(map_ref, j)[...]), split(block(far_ref, j)[...]), TN)
         back = block(near_ref, j)[...] + block(h_ref, j)[...] + beyond * far
         g_ref[j] = back
-        made = dot3(split(block(ab_ref, j)[...]), split(back), TN)
+        made = wide3(split(block(ab_ref, j)[...]), split(back), TN)
         block(out_ref, j)[...] = block(c_ref, j)[...] + joined * made
 
 
 def kernel_d(
-    ids_ref, q_ref, k_ref, th_ref, tl_ref, do_ref, uw_ref, s_ref,
+    ids_ref, q_ref, k_ref, ph_ref, pl_ref, do_ref, uw_ref, s_ref,
     dq_ref, u_ref, dr_ref, dk_ref,
 ):
     same, ii, jj, keep, tail, through = id_masks(ids_ref)
@@ -326,23 +386,21 @@
         q32 = q.astype(F32)
         state = split(s_ref[j])
         uw = uw_ref[j]
-        update = uw[:, :DIM] - dot3(split(uw[:, DIM:]), state)
+        update = uw[:, :DIM] - pack3(split(uw[:, DIM:]), state)
         draw = head(do_ref, j)
         draws = split(draw)
-        scores = split(jnp.where(causal, mm(q, k, NT), 0.0))
-        weights = split(jnp.where(causal, dot3(draws, split(update), NT), 0.0))
-        dq = dot3(split(draw * keep), state, NT) + dot2(weights, k)
+        weights = split(jnp.where(causal, outer3(draws, split(update)), 0.0))
+        dq = keep * pack3_nt(draws, state) + dot2(weights, k)
         iq = inv_norm(q32)
         dq = dq - q32 * (iq * iq * jnp.sum(q32 * dq, axis=-1, keepdims=True))
         put(dq_ref, j, dq)
         put(u_ref, j, update)
-        dupdate = dot3(scores, draws, TN)
-        put(dr_ref, j, dot3((th_ref[j], tl_ref[j]), split(dupdate), TN))
+        put(dr_ref, j, wide3((ph_ref[j], pl_ref[j]), draws))
         put(dk_ref, j, dot2(weights, q, TN))
 
 
 def kernel_e(
-    ids_ref, k_ref, v_ref, beta_ref, z_ref, u_ref, dr_ref, dkl_ref, s_ref, g_ref, h_ref,
+    ids_ref, k_ref, v_ref, beta_ref, zh_ref, zl_ref, u_ref, dr_ref, dkl_ref, s_ref, g_ref, h_ref,
     dk_ref, dv_ref, db_ref,
 ):
     same, ii, jj, keep, tail, through = id_masks(ids_ref)
@@ -360,37 +418,29 @@
         update = head(u_ref, j)
         updates = split(update)
         back = split(g_ref[j] + block(h_ref, j)[...])
-        dright = head(dr_ref, j) + dot3(split(z_ref[j]), back, TN)
+        dright = head(dr_ref, j) + pack3((head(zh_ref, j), head(zl_ref, j)), back)
         put(dv_ref, j, dright * (rate * ik))
         dlogit = jax.nn.sigmoid(-logit) * jnp.sum(dright * update, axis=-1, keepdims=True)
         dbeta = jnp.where(lane == j, dlogit, dbeta)
         scaled = dright * (rate * ik * ik)
-        inner = split(jnp.where(strict, -dot3(split(scaled), updates, NT), 0.0))
+        inner = split(jnp.where(strict, outer3(split(-scaled), updates), 0.0))
         dk = head(dkl_ref, j) + (dot2(inner, k) + dot2(inner, k, TN))
-        dk = dk + tail * dot3(updates, back, NT)
-        dk = dk - dot3(split(scaled * keep), split(s_ref[j]), NT)
+        dk = dk + tail * pack3_nt(updates, back)
+        dk = dk - keep * pack3_nt(split(scaled), split(s_ref[j]))
         dk = dk - k32 * (ik * ik * jnp.sum(k32 * dk, axis=-1, keepdims=True))
         put(dk_ref, j, dk)
 
     db_ref[...] = jnp.transpose(dbeta)
 
 
-def exchange_sum(value, axis):
-    size = lax.axis_size(axis)
-    step = 1
-    while step < size:
-        value = value + lax.ppermute(value, axis, [(i, i ^ step) for i in range(size)])
-        step *= 2
-    return value
-
-
-def call(kernel, ins, outs, flops, name, limit=16):
+def call(kernel, ins, outs, flops, name, **extra):
     return pl.pallas_call(
         kernel,
         out_shape=outs,
-        compiler_params=pltpu.CompilerParams(vmem_limit_bytes=limit * 1024 * 1024),
+        compiler_params=pltpu.CompilerParams(vmem_limit_bytes=16 * 1024 * 1024),
         cost_estimate=pl.CostEstimate(flops=flops, bytes_accessed=4_000_000, transcendentals=0),
         name=name,
+        **extra,
     )(*ins)
 
 
@@ -458,32 +508,39 @@
 
     ab, th, tl, z = call(
         kernel_a, (ids, k, v, beta), (two, square, square, shape(HEADS, DIM, tokens)),
-        20 * unit, "span_state", 60,
+        20 * unit, "span_state",
+        in_specs=[pl.BlockSpec(memory_space=pltpu.HBM)] * 4,
+        scratch_shapes=[
+            pltpu.VMEM(ids.shape, ids.dtype),
+            pltpu.VMEM(k.shape, k.dtype),
+            pltpu.VMEM(v.shape, v.dtype),
+            pltpu.VMEM(beta.shape, beta.dtype),
+            pltpu.SemaphoreType.DMA((4,)),
+        ],
     )
     if short:
-        r1 = send(ab, [(0, 1), (2, 3), (4, 5), (5, 6), (6, 7)])
-        pair, mid, pair_map = call(
-            kernel_join, (ids, ab, r1), (two, one, shape(ROWS, DIM)), unit, "join"
-        )
-        r3 = send(pair, [(3, 4)])
-        r2 = send(mid, [(1, 4)])
-        r4 = send(mid, [(1, 2)])
-    o0, eff, uw = call(
-        kernel_b, (ids, q, k, v, beta, th, tl),
-        (wide, wide, shape(HEADS, tokens, 2 * DIM)), 8 * unit, "span_out",
+        r1 = send(ab, [(0, 1), (2, 3)])
+        pair, mid, side = call(kernel_join, (ids, ab, r1), (two, one, one), unit, "join")
+        m3 = send(mid, [(1, 3)])
+        side = send(side, [(1, 2), (3, 1), (4, 5), (5, 6), (6, 7)])
+    o0, eff, uw, ph, pl_, zh, zl = call(
+        kernel_b, (ids, q, k, v, beta, th, tl, z),
+        (
+            wide, wide, shape(HEADS, tokens, 2 * DIM), square, square, wide16, wide16,
+        ),
+        11 * unit, "span_out",
     )
     if short:
-        r5 = send(r4, [(2, 3)])
-        far_map = send(pair_map, [(3, 1)])
+        m3, side, o0 = lax.optimization_barrier((m3, side, o0))
+        m4 = send(call(kernel_apply, (pair, m3), one, unit, "apply"), [(3, 4)])
         mixed, draw, c, entering, dgain = call(
-            kernel_c, (ids, q, o0, eff, r1, r3, r2, r4, r5, cot, gain),
+            kernel_c, (ids, q, o0, eff, r1, side, m3, m4, cot, gain),
             (wide16, wide, one, states, row), 4 * unit, "span_norm",
         )
+        n3 = send(c, [(4, 1)])
+        n4 = send(c, [(4, 3)])
         n1 = send(c, [(3, 2)])
-        n3 = send(c, [(4, 1)])
-        n4 = send(c, [(4, 3), (5, 4), (6, 5), (7, 6)])
-        h = call(kernel_back, (ab, c, n1), one, unit, "back")
-        n2 = send(h, [(2, 1)])
+        n2 = send(call(kernel_back, (ab, c, n1), one, unit, "back"), [(2, 1)])
     else:
         entering, joined = relay_forward(ab, ids, spans)
         mixed, draw, c, dgain = call(
@@ -491,24 +548,27 @@
             (wide16, wide, one, row), 4 * unit, "span_norm",
         )
     dq, update, dright, dkl = call(
-        kernel_d, (ids, q, k, th, tl, draw, uw, entering), (wide16, wide, wide, wide),
+        kernel_d, (ids, q, k, ph, pl_, draw, uw, entering), (wide16, wide, wide, wide),
         12 * unit, "span_query_grad",
     )
     if short:
+        n3, n4, update = lax.optimization_barrier((n3, n4, update))
         back, last = call(
-            kernel_back_far, (ab, c, far_map, n2, n3, n4), (states, shape(ROWS, DIM)), unit,
+            kernel_back_far, (ab, c, side, n2, n3, n4), (states, shape(ROWS, DIM)), unit,
             "back_far",
         )
-        far = send(last, [(1, 0), (3, 2)])
-        last, dgain = lax.optimization_barrier((last, dgain))
+        far = send(last, [(1, 0), (3, 2), (5, 4), (6, 5), (7, 6)])
     else:
         back = relay_backward(ab, c, spans)
         far = jnp.zeros((ROWS, DIM), F32)
-    gain_total = exchange_sum(exchange_sum(dgain, "seq"), "dp")[0]
     dk, dv, dbeta = call(
-        kernel_e, (ids, k, v, beta, z, update, dright, dkl, entering, back, far),
+        kernel_e, (ids, k, v, beta, zh, zl, update, dright, dkl, entering, back, far),
         (wide16, wide16, shape(HEADS, tokens)), 12 * unit, "span_key_grad",
     )
+    dgain, dbeta = lax.optimization_barrier((dgain, dbeta))
+    devices = spans * lax.axis_size("dp")
+    copies = jnp.broadcast_to(dgain, (devices, DIM))[:, None]
+    gain_total = jnp.sum(lax.all_to_all(copies, ("seq", "dp"), 0, 0), axis=(0, 1))
     return (mixed[None], dq[None], dk[None], dv[None], jnp.transpose(dbeta)[None], gain_total)
 
 

time: 93.8 us -> 76.4 us (0.81)
  starting transfers between devices: 44.3 us -> 9.1 us
  blocking collectives: 0 us -> 12.7 us
  waiting for transfers between devices: 10.8 us -> 19.6 us
  Pallas kernels: 33.2 us -> 29.8 us
    ppermute x5 -> x0, starting transfers between devices: 33.8 us -> none  [exchange_sum(): lax.ppermute(value, axis, [(i, i ^ step) for i in range(size)])]
    ppermute x11 -> x9, waiting for transfers between devices: 2.44 us -> 19.6 us  [send(): return lax.ppermute(value, 'seq', pairs)]
    all_to_all x0 -> x1, blocking collectives: none -> 12.7 us  [local(): lax.all_to_all(copies, ('seq', 'dp'), 0, 0)]
    ppermute x5 -> x0, waiting for transfers between devices: 8.34 us -> none  [exchange_sum(): lax.ppermute(value, axis, [(i, i ^ step) for i in range(size)])]
    pallas_call x8 -> x9, Pallas kernels: 33.2 us -> 29.8 us  [call(): pl.pallas_call(kernel, out_shape=outs, compiler_params=pltpu.CompilerPara...]
    ppermute x11 -> x9, starting transfers between devices: 10.5 us -> 9.1 us  [send(): return lax.ppermute(value, 'seq', pairs)]
    unnamed x28 -> x16, local copies, waits for them, and re-layouts: 3.71 us -> 3.47 us
  transfers between devices with their start and end apart: 16 -> 9, of which waited for: 5 -> 2; matrix products, arithmetic and copies ran while one was open for 1% -> 0% of each run, Pallas kernels for 14% -> 15%
where the time goes in v4:
time: 76.4 us; the launch traced here: 76 us
  Pallas kernels  29.8 us (39%)
  waiting for transfers between devices  19.6 us (26%)
  blocking collectives  12.7 us (17%)
  starting transfers between devices  9.1 us (12%)
  local copies, waits for them, and re-layouts  3.48 us (5%)
  between operations  0.85 us (1%)
    pallas_call x9, Pallas kernels, call(): pl.pallas_call(kernel, out_shape=outs, compiler_params=pltpu.CompilerPara...  29.8 us
    ppermute x9, waiting for transfers between devices, send(): return lax.ppermute(value, 'seq', pairs)  19.6 us
    all_to_all x1, blocking collectives, local(): lax.all_to_all(copies, ('seq', 'dp'), 0, 0)  12.7 us
    ppermute x9, starting transfers between devices, send(): return lax.ppermute(value, 'seq', pairs)  9.1 us
    unnamed x16, local copies, waits for them, and re-layouts  3.47 us
  transfers between devices with their start and end apart: 9, of which 2 were waited for; matrix products, arithmetic and copies ran while one was open for 0% of the time, Pallas kernels for 15%

profile of v4, /device:TPU:0, one launch (start us, length us, event | category | flops | bytes accessed | tf_op | source)
XLA Modules:
  0.0 76.0 jit_solution(9015763840140631004)
XLA Ops:
  0.6 0.7 copy-done.2
  1.3 1.0 %copy-done.4 = bf16[1,256,1024]{2,1,0:T(8,128)(2,1)S(1)} copy-done((bf16[1,256,1024]{2,1,0:T(8,128)(2,1)S(1)}, bf16[1,256,1024]{2,1,0:T(8,128)(2,1)}, u32[]{:S(2)}) %copy-start.4) | copy-done | bytes 524312
  2.4 1.0 %copy-done.5 = bf16[1,256,1024]{2,1,0:T(8,128)(2,1)S(1)} copy-done((bf16[1,256,1024]{2,1,0:T(8,128)(2,1)S(1)}, bf16[1,256,1024]{2,1,0:T(8,128)(2,1)}, u32[]{:S(2)}) %copy-start.5) | copy-done | bytes 524312
  3.4 0.7 copy-done.6
  4.1 6.4 %span_state.1 = (f32[2056,128]{1,0:T(8,128)S(1)}, bf16[8,256,256]{2,1,0:T(8,128)(2,1)S(1)}, bf16[8,256,256]{2,1,0:T(8,128)(2,1)S(1)}, f32[8,128,256]{2,1,0:T(8,128)S(1)}) custom-call(s32[1,256]{1,0:T(1,128)S(1)} %copy-done.2, bf16[256,1024]{1,0:T(8,128)(2,1)S(1)} %bitcast.23, bf16[256,1024]{1,0:T(8,128)(2,1)S(1)} %bitcast.27, f32[8,256]{1,0:T(8,128)S(1)} %bitcast.30), custom_call_target="tpu_custom_call" | custom-call | flops 5368709120 | bytes 4000000 | tf_op jit(solution)/shard_map/span_state/pallas_call | solution.py:437
  10.6 2.6 %collective-permute-start = (f32[2056,128]{1,0:T(8,128)S(1)}, f32[2056,128]{1,0:T(8,128)S(1)}, u32[]{:S(2)}, u32[]{:S(2)}) collective-permute-start(f32[2056,128]{1,0:T(8,128)S(1)} %get-tuple-element.42.ab_ref), channel_id=1, source_target_pairs={{0,4},{8,12},{1,5},{9,13},{2,6},{10,14},{3,7},{11,15}} | collective-permute-start | bytes 3158024 | tf_op jit(solution)/shard_map/ppermute | solution.py:452
  13.1 2.2 %collective-permute-done.prev_ref = f32[2056,128]{1,0:T(8,128)S(1)} collective-permute-done((f32[2056,128]{1,0:T(8,128)S(1)}, f32[2056,128]{1,0:T(8,128)S(1)}, u32[]{:S(2)}, u32[]{:S(2)}) %collective-permute-start) | collective-permute-done | bytes 1052704 | tf_op jit(solution)/shard_map/ppermute | solution.py:452
  15.3 0.6 join.1
  16.0 0.7 collective-permute-start.1
  16.7 0.9 %collective-permute-start.2 = (f32[1032,128]{1,0:T(8,128)S(1)}, f32[1032,128]{1,0:T(8,128)S(1)}, u32[]{:S(2)}, u32[]{:S(2)}) collective-permute-start(f32[1032,128]{1,0:T(8,128)S(1)} %get-tuple-element.44), channel_id=1, source_target_pairs={{4,8},{12,4},{16,20},{20,24},{24,28},{5,9},{13,5},{17,21},{21,25},... | collective-permute-start | bytes 1585160 | tf_op jit(solution)/shard_map/ppermute | solution.py:452
  17.6 5.1 %span_out.1 = (f32[256,1024]{1,0:T(8,128)S(1)}, f32[256,1024]{1,0:T(8,128)S(1)}, f32[8,256,256]{2,1,0:T(8,128)S(1)}, bf16[8,256,256]{2,1,0:T(8,128)(2,1)S(1)}, b...) custom-call(s32[1,256]{1,0:T(1,128)S(1)} %copy-done.2, ...), custom_call_target="tpu_custom_call" | custom-call | flops 2952790016 | bytes 4000000 | tf_op jit(solution)/shard_map/span_out/pallas_call | solution.py:437
  23.2 0.7 collective-permute-start.3
  24.0 2.6 %span_norm.1 = (bf16[256,1024]{1,0:T(8,128)(2,1)}, f32[256,1024]{1,0:T(8,128)S(1)}, f32[1032,128]{1,0:T(8,128)S(1)}, f32[8,128,128]{2,1,0:T(8,128)S(1)}, f32[1,128]{1,0:T(1,128)S(1)}) custom-call(s32[1,256]{1,0:T(1,128)S(1)} %copy-done.2, bf16[256,1024]{1,0:T(8,128)(2,1)S(1)} %bitcast.19, f32[256,1024]{1,0:T(8,128)S(1)} %get-tuple-element.49.o_ref, ...), custom_call_target="tpu_custom_call" | custom-call | flops 1073741824 | bytes 4000000 | tf_op jit(solution)/shard_map/span_norm/pallas_call | solution.py:437
  26.6 0.7 collective-permute-start.6
  27.3 0.7 collective-permute-start.4
  28.0 0.7 collective-permute-start.5
  29.1 0.9 %collective-permute-start.7 = (f32[1032,128]{1,0:T(8,128)S(1)}, f32[1032,128]{1,0:T(8,128)S(1)}, u32[]{:S(2)}, u32[]{:S(2)}) collective-permute-start(f32[1032,128]{1,0:T(8,128)S(1)} %back.1), channel_id=1, source_target_pairs={{8,4},{9,5},{10,6},{11,7}} | collective-permute-start | bytes 1585160 | tf_op jit(solution)/shard_map/ppermute | solution.py:452
  30.1 6.0 %span_query_grad.1 = (bf16[256,1024]{1,0:T(8,128)(2,1)}, f32[256,1024]{1,0:T(8,128)S(1)}, f32[256,1024]{1,0:T(8,128)S(1)}, f32[256,1024]{1,0:T(8,128)S(1)}) custom-call(s32[1,256]{1,0:T(1,128)S(1)} %copy-done.2, bf16[256,1024]{1,0:T(8,128)(2,1)S(1)} %bitcast.20, bf16[256,1024]{1,0:T(8,128)(2,1)S(1)} %bitcast.25, ...), custom_call_target="tpu_custom_call" | custom-call | flops 3221225472 | bytes 4000000 | tf_op jit(solution)/shard_map/span_query_grad/pallas_call | solution.py:437
  36.1 1.7 %back_far.1 = (f32[8,128,128]{2,1,0:T(8,128)S(1)}, f32[1024,128]{1,0:T(8,128)S(1)}) custom-call(f32[2056,128]{1,0:T(8,128)S(1)} %get-tuple-element.42.ab_ref, f32[1032,128]{1,0:T(8,128)S(1)} %get-tuple-element.63.c_ref, f32[1032,128]{1,0:T(8,128)S(1)} %collective-permute-done.2.m2_ref.map_ref, f32[1032,128]{1,0:T(8,128)S(1)} %collective-permute-done.7.h_ref, ...), custom_call_target="tpu_custom_call" | custom-call | flops 268435456 | bytes 4000000 | tf_op jit(solution)/shard_map/back_far/pallas_call | solution.py:437
  37.9 1.3 %collective-permute-start.8 = (f32[1024,128]{1,0:T(8,128)S(1)}, f32[1024,128]{1,0:T(8,128)S(1)}, u32[]{:S(2)}, u32[]{:S(2)}) collective-permute-start(f32[1024,128]{1,0:T(8,128)S(1)} %get-tuple-element.71), channel_id=1, source_target_pairs={{4,0},{12,8},{20,16},{24,20},{28,24},{5,1},{13,9},{21,17},{25,21},... | collective-permute-start | bytes 1572872 | tf_op jit(solution)/shard_map/ppermute | solution.py:452
  39.2 17.3 %collective-permute-done.8.h_ref = f32[1024,128]{1,0:T(8,128)S(1)} collective-permute-done((f32[1024,128]{1,0:T(8,128)S(1)}, f32[1024,128]{1,0:T(8,128)S(1)}, u32[]{:S(2)}, u32[]{:S(2)}) %collective-permute-start.8) | collective-permute-done | bytes 524320 | tf_op jit(solution)/shard_map/ppermute | solution.py:452
  56.5 6.2 %span_key_grad.1 = (bf16[256,1024]{1,0:T(8,128)(2,1)}, bf16[256,1024]{1,0:T(8,128)(2,1)}, f32[8,256]{1,0:T(8,128)}) custom-call(s32[1,256]{1,0:T(1,128)S(1)} %copy-done.2, bf16[256,1024]{1,0:T(8,128)(2,1)S(1)} %bitcast.26, bf16[256,1024]{1,0:T(8,128)(2,1)S(1)} %bitcast.29, f32[8,256]{1,0:T(8,128)S(1)} %bitcast.32, ...), custom_call_target="tpu_custom_call" | custom-call | flops 3221225472 | bytes 4000000 | tf_op jit(solution)/shard_map/span_key_grad/pallas_call | solution.py:437
  62.8 12.7 %all_to_all.5 = f32[32,1,128]{2,1,0:T(1,128)S(1)} all-to-all(f32[32,1,128]{2,1,0:T(1,128)S(1)} %broadcast_in_dim_broadcast_in_dim.2), channel_id=1, replica_groups=mesh['seq'=8,'dp'=4] {'seq','dp'}, dimensions={0} | all-to-all | bytes 32768 | tf_op jit(solution)/shard_map/all_to_all | solution.py:571
  75.5 0.5 reduce_sum.9
  (22 shorter events, 1.0 us)
Async XLA Ops:
  0.6 0.7 copy-start.2
  1.3 1.0 %copy-start.4 = (bf16[1,256,1024]{2,1,0:T(8,128)(2,1)S(1)}, bf16[1,256,1024]{2,1,0:T(8,128)(2,1)}, u32[]{:S(2)}) copy-start(bf16[1,256,1024]{2,1,0:T(8,128)(2,1)} %param.8) | copy-start | bytes 1572868
  2.4 1.0 %copy-start.5 = (bf16[1,256,1024]{2,1,0:T(8,128)(2,1)S(1)}, bf16[1,256,1024]{2,1,0:T(8,128)(2,1)}, u32[]{:S(2)}) copy-start(bf16[1,256,1024]{2,1,0:T(8,128)(2,1)} %param.9) | copy-start | bytes 1572868
  3.4 0.7 copy-start.6
  10.6 7.0 %copy-start.1 = (bf16[1,256,1024]{2,1,0:T(8,128)(2,1)S(1)}, bf16[1,256,1024]{2,1,0:T(8,128)(2,1)}, u32[]{:S(2)}) copy-start(bf16[1,256,1024]{2,1,0:T(8,128)(2,1)} %param.7) | copy-start | bytes 1572868
  10.6 4.8 %collective-permute-start = (f32[2056,128]{1,0:T(8,128)S(1)}, f32[2056,128]{1,0:T(8,128)S(1)}, u32[]{:S(2)}, u32[]{:S(2)}) collective-permute-start(f32[2056,128]{1,0:T(8,128)S(1)} %get-tuple-element.42.ab_ref), channel_id=1, source_target_pairs={{0,4},{8,12},{1,5},{9,13},{2,6},{10,14},{3,7},{11,15}} | collective-permute-start | bytes 3158024 | tf_op jit(solution)/shard_map/ppermute | solution.py:452
  16.0 6.7 %collective-permute-start.1 = (f32[1032,128]{1,0:T(8,128)S(1)}, f32[1032,128]{1,0:T(8,128)S(1)}, u32[]{:S(2)}, u32[]{:S(2)}) collective-permute-start(f32[1032,128]{1,0:T(8,128)S(1)} %get-tuple-element.43), channel_id=1, source_target_pairs={{4,12},{5,13},{6,14},{7,15}} | collective-permute-start | bytes 1585160 | tf_op jit(solution)/shard_map/ppermute | solution.py:452
  16.7 6.1 %collective-permute-start.2 = (f32[1032,128]{1,0:T(8,128)S(1)}, f32[1032,128]{1,0:T(8,128)S(1)}, u32[]{:S(2)}, u32[]{:S(2)}) collective-permute-start(f32[1032,128]{1,0:T(8,128)S(1)} %get-tuple-element.44), channel_id=1, source_target_pairs={{4,8},{12,4},{16,20},{20,24},{24,28},{5,9},{13,5},{17,21},{21,25},... | collective-permute-start | bytes 1585160 | tf_op jit(solution)/shard_map/ppermute | solution.py:452
  22.7 1.2 %copy-start = (bf16[1,256,1024]{2,1,0:T(8,128)(2,1)S(1)}, bf16[1,256,1024]{2,1,0:T(8,128)(2,1)}, u32[]{:S(2)}) copy-start(bf16[1,256,1024]{2,1,0:T(8,128)(2,1)} %param.12) | copy-start | bytes 1572868
  22.7 1.2 %copy-start.3 = (f32[128]{0:T(128)S(1)}, f32[128]{0:T(128)}, u32[]{:S(2)}) copy-start(f32[128]{0:T(128)} %param.13) | copy-start | bytes 1540
  23.2 0.7 collective-permute-start.3
  26.6 2.1 %collective-permute-start.6 = (f32[1032,128]{1,0:T(8,128)S(1)}, f32[1032,128]{1,0:T(8,128)S(1)}, u32[]{:S(2)}, u32[]{:S(2)}) collective-permute-start(f32[1032,128]{1,0:T(8,128)S(1)} %get-tuple-element.63.c_ref), channel_id=1, source_target_pairs={{12,8},{13,9},{14,10},{15,11}} | collective-permute-start | bytes 1585160 | tf_op jit(solution)/shard_map/ppermute | solution.py:452
  27.3 8.8 %collective-permute-start.4 = (f32[1032,128]{1,0:T(8,128)S(1)}, f32[1032,128]{1,0:T(8,128)S(1)}, u32[]{:S(2)}, u32[]{:S(2)}) collective-permute-start(f32[1032,128]{1,0:T(8,128)S(1)} %get-tuple-element.63.c_ref), channel_id=1, source_target_pairs={{16,4},{17,5},{18,6},{19,7}} | collective-permute-start | bytes 1585160 | tf_op jit(solution)/shard_map/ppermute | solution.py:452
  28.0 8.1 %collective-permute-start.5 = (f32[1032,128]{1,0:T(8,128)S(1)}, f32[1032,128]{1,0:T(8,128)S(1)}, u32[]{:S(2)}, u32[]{:S(2)}) collective-permute-start(f32[1032,128]{1,0:T(8,128)S(1)} %get-tuple-element.63.c_ref), channel_id=1, source_target_pairs={{16,12},{17,13},{18,14},{19,15}} | collective-permute-start | bytes 1585160 | tf_op jit(solution)/shard_map/ppermute | solution.py:452
  29.1 7.0 %collective-permute-start.7 = (f32[1032,128]{1,0:T(8,128)S(1)}, f32[1032,128]{1,0:T(8,128)S(1)}, u32[]{:S(2)}, u32[]{:S(2)}) collective-permute-start(f32[1032,128]{1,0:T(8,128)S(1)} %back.1), channel_id=1, source_target_pairs={{8,4},{9,5},{10,6},{11,7}} | collective-permute-start | bytes 1585160 | tf_op jit(solution)/shard_map/ppermute | solution.py:452
  36.1 20.4 %copy-start.7 = (f32[1,256,8]{1,2,0:T(8,128)S(1)}, f32[1,256,8]{1,2,0:T(8,128)}, u32[]{:S(2)}) copy-start(f32[1,256,8]{1,2,0:T(8,128)} %param.10) | copy-start | bytes 24580
  37.9 18.6 %collective-permute-start.8 = (f32[1024,128]{1,0:T(8,128)S(1)}, f32[1024,128]{1,0:T(8,128)S(1)}, u32[]{:S(2)}, u32[]{:S(2)}) collective-permute-start(f32[1024,128]{1,0:T(8,128)S(1)} %get-tuple-element.71), channel_id=1, source_target_pairs={{4,0},{12,8},{20,16},{24,20},{28,24},{5,1},{13,9},{21,17},{25,21},... | collective-permute-start | bytes 1572872 | tf_op jit(solution)/shard_map/ppermute | solution.py:452

commit v5 on v4

--- a/solution.py
+++ b/solution.py
@@ -174,7 +174,7 @@
 
 
 def kernel_a(
-    ids_in, k_in, v_in, beta_in, ab_ref, th_ref, tl_ref, z_ref,
+    ids_in, k_in, v_in, beta_in, ab_ref, b_ref, th_ref, tl_ref, z_ref,
     ids_ref, k_ref, v_ref, beta_ref, sems,
 ):
     copies = [
@@ -229,11 +229,14 @@
         both = dot3(split(zs[j]), split(right))
         block(ab_ref, j)[...] = eye * through - both[:, DIM:]
         block(ab_ref, HEADS + j)[...] = both[:, :DIM]
+        block(b_ref, j)[...] = both[:, :DIM]
         th_ref[j] = fulls[j][0]
         tl_ref[j] = fulls[j][1]
         z_ref[j] = zs[j]
     row = ids_ref[...].astype(F32)
-    ab_ref[2 * ROWS :] = notes(row[:, :1], row[:, row.shape[1] - 1 :], 1.0)
+    after = notes(row[:, :1], row[:, row.shape[1] - 1 :], 1.0)
+    ab_ref[2 * ROWS :] = after
+    b_ref[ROWS:] = after
 
 
 def writes(value, key, rate, ik, keep):
@@ -265,24 +268,27 @@
         put(zl_ref, j, ends[1])
 
 
-def kernel_join(ids_ref, ab_ref, prev_ref, both_ref, mid_ref, side_ref):
+def kernel_step(ids_ref, ab_ref, prev_ref, out_ref):
+    row = ids_ref[...].astype(F32)
+    joined = (note(prev_ref[ROWS:], 1) == row[:, :1]).astype(F32)
+    for j in range(HEADS):
+        made = pack3(split(block(ab_ref, j)[...]), split(block(prev_ref, j)[...]))
+        block(out_ref, j)[...] = joined * made + block(ab_ref, HEADS + j)[...]
+    out_ref[ROWS:] = ab_ref[2 * ROWS :]
+
+
+def kernel_join(ids_ref, ab_ref, prev_ref, both_ref, map_ref):
     row = ids_ref[...].astype(F32)
     last = row[:, row.shape[1] - 1 :]
     before = prev_ref[2 * ROWS :]
     joined = (note(before, 1) == row[:, :1]).astype(F32)
-    maps = lax.axis_index("seq") == 3
     for j in range(HEADS):
         right = cat([block(prev_ref, j)[...], block(prev_ref, HEADS + j)[...]], 1)
         made = joined * dot3(split(block(ab_ref, j)[...]), split(right))
+        block(map_ref, j)[...] = made[:, :DIM]
         block(both_ref, j)[...] = made[:, :DIM]
-        offset = made[:, DIM:] + block(ab_ref, HEADS + j)[...]
-        block(both_ref, HEADS + j)[...] = offset
-        block(mid_ref, j)[...] = offset
-        block(side_ref, j)[...] = jnp.where(maps, made[:, :DIM], offset)
-    after = notes(note(before, 0), last, 1.0)
-    both_ref[2 * ROWS :] = after
-    mid_ref[ROWS:] = after
-    side_ref[ROWS:] = after
+        block(both_ref, HEADS + j)[...] = made[:, DIM:] + block(ab_ref, HEADS + j)[...]
+    both_ref[2 * ROWS :] = notes(note(before, 0), last, 1.0)
 
 
 def kernel_apply(both_ref, mid_ref, out_ref):
@@ -295,24 +301,20 @@
 
 
 def kernel_c(
-    ids_ref, q_ref, o_ref, e_ref, prev_ref, m2_ref, m3_ref, m4_ref, cot_ref, gain_ref,
+    ids_ref, q_ref, o_ref, e_ref, prev_ref, m1_ref, m2_ref, m3_ref, m4_ref, cot_ref, gain_ref,
     y_ref, do_ref, c_ref, s_ref, dg_ref,
 ):
     first = ids_ref[...].astype(F32)[:, :1]
     before = prev_ref[2 * ROWS :]
-    direct_side = lax.axis_index("seq") != 1
-
-    def side(rows):
-        return jnp.where(direct_side, rows, 0.0)
-
-    middle = side(m2_ref[ROWS:]) + m3_ref[ROWS:] + m4_ref[ROWS:]
+    parts = (m1_ref, m2_ref, m3_ref, m4_ref)
+    middle = sum(part[ROWS:] for part in parts)
     known = note(before, 2)
     inner = (note(middle, 1) == note(before, 0)).astype(F32)
     direct = (1.0 - known) * (note(middle, 1) == first).astype(F32)
     joined = known * (note(before, 1) == first).astype(F32)
     states = []
     for j in range(HEADS):
-        mid = side(block(m2_ref, j)[...]) + block(m3_ref, j)[...] + block(m4_ref, j)[...]
+        mid = sum(block(part, j)[...] for part in parts)
         made = pack3(split(block(prev_ref, j)[...]), split(inner * mid))
         states.append(joined * (made + block(prev_ref, HEADS + j)[...]) + direct * mid)
         s_ref[j] = states[j]
@@ -367,11 +369,13 @@
 def kernel_back_far(ab_ref, c_ref, map_ref, h_ref, far_ref, near_ref, g_ref, out_ref):
     joined = note(c_ref[ROWS:], 0)
     beyond = note(h_ref[ROWS:], 0)
+    backs = []
     for j in range(HEADS):
         far = wide3(split(block(map_ref, j)[...]), split(block(far_ref, j)[...]), TN)
-        back = block(near_ref, j)[...] + block(h_ref, j)[...] + beyond * far
-        g_ref[j] = back
-        made = wide3(split(block(ab_ref, j)[...]), split(back), TN)
+        backs.append(block(near_ref, j)[...] + block(h_ref, j)[...] + beyond * far)
+        g_ref[j] = backs[j]
+    for j in range(HEADS):
+        made = wide3(split(block(ab_ref, j)[...]), split(backs[j]), TN)
         block(out_ref, j)[...] = block(c_ref, j)[...] + joined * made
 
 
@@ -506,8 +510,8 @@
     row = shape(1, DIM)
     unit = 2 * HEADS * tokens**3
 
-    ab, th, tl, z = call(
-        kernel_a, (ids, k, v, beta), (two, square, square, shape(HEADS, DIM, tokens)),
+    ab, bm, th, tl, z = call(
+        kernel_a, (ids, k, v, beta), (two, one, square, square, shape(HEADS, DIM, tokens)),
         20 * unit, "span_state",
         in_specs=[pl.BlockSpec(memory_space=pltpu.HBM)] * 4,
         scratch_shapes=[
@@ -519,10 +523,16 @@
         ],
     )
     if short:
-        r1 = send(ab, [(0, 1), (2, 3)])
-        pair, mid, side = call(kernel_join, (ids, ab, r1), (two, one, one), unit, "join")
+        r1 = send(bm, [(0, 1)])
+        r3 = send(ab, [(2, 3)])
+        mid = call(kernel_step, (ids, ab, r1), one, unit, "step")
         m3 = send(mid, [(1, 3)])
-        side = send(side, [(1, 2), (3, 1), (4, 5), (5, 6), (6, 7)])
+        r3, mid = lax.optimization_barrier((r3, mid))
+        pair, pair_map = call(
+            kernel_join, (ids, ab, r3), (two, shape(ROWS, DIM)), unit, "join"
+        )
+        far_map = send(pair_map, [(3, 1)])
+        th, pair = lax.optimization_barrier((th, pair))
     o0, eff, uw, ph, pl_, zh, zl = call(
         kernel_b, (ids, q, k, v, beta, th, tl, z),
         (
@@ -531,16 +541,19 @@
         11 * unit, "span_out",
     )
     if short:
-        m3, side, o0 = lax.optimization_barrier((m3, side, o0))
+        mid, o0 = lax.optimization_barrier((mid, o0))
+        m3, far_map, o0 = lax.optimization_barrier((m3, far_map, o0))
+        m2 = send(mid, [(1, 2), (4, 5), (5, 6), (6, 7)])
         m4 = send(call(kernel_apply, (pair, m3), one, unit, "apply"), [(3, 4)])
         mixed, draw, c, entering, dgain = call(
-            kernel_c, (ids, q, o0, eff, r1, side, m3, m4, cot, gain),
+            kernel_c, (ids, q, o0, eff, r3, r1, m2, m3, m4, cot, gain),
             (wide16, wide, one, states, row), 4 * unit, "span_norm",
         )
         n3 = send(c, [(4, 1)])
         n4 = send(c, [(4, 3)])
         n1 = send(c, [(3, 2)])
-        n2 = send(call(kernel_back, (ab, c, n1), one, unit, "back"), [(2, 1)])
+        h = call(kernel_back, (ab, c, n1), one, unit, "back")
+        n2 = send(h, [(2, 1)])
     else:
         entering, joined = relay_forward(ab, ids, spans)
         mixed, draw, c, dgain = call(
@@ -554,7 +567,7 @@
     if short:
         n3, n4, update = lax.optimization_barrier((n3, n4, update))
         back, last = call(
-            kernel_back_far, (ab, c, side, n2, n3, n4), (states, shape(ROWS, DIM)), unit,
+            kernel_back_far, (ab, c, far_map, n2, n3, n4), (states, shape(ROWS, DIM)), unit,
             "back_far",
         )
         far = send(last, [(1, 0), (3, 2), (5, 4), (6, 5), (7, 6)])

time: 76.4 us -> 73.8 us (0.966)
  waiting for transfers between devices: 19.6 us -> 15.6 us
  starting transfers between devices: 9.1 us -> 10.6 us
  Pallas kernels: 29.8 us -> 28.9 us
    ppermute x9 -> x11, waiting for transfers between devices: 19.6 us -> 15.6 us  [send(): return lax.ppermute(value, 'seq', pairs)]
    ppermute x9 -> x11, starting transfers between devices: 9.1 us -> 10.6 us  [send(): return lax.ppermute(value, 'seq', pairs)]
    pallas_call x9 -> x10, Pallas kernels: 29.8 us -> 28.9 us  [call(): pl.pallas_call(kernel, out_shape=outs, compiler_params=pltpu.CompilerPara...]
  transfers between devices with their start and end apart: 9 -> 11, of which waited for: 2 -> 2; matrix products, arithmetic and copies ran while one was open for 0% -> 0% of each run, Pallas kernels for 15% -> 18%
where the time goes in v5:
time: 73.8 us; the launch traced here: 73.4 us
  Pallas kernels  28.9 us (39%)
  waiting for transfers between devices  15.6 us (21%)
  blocking collectives  13.4 us (18%)
  starting transfers between devices  10.6 us (14%)
  local copies, waits for them, and re-layouts  3.48 us (5%)
  between operations  0.89 us (1%)
    pallas_call x10, Pallas kernels, call(): pl.pallas_call(kernel, out_shape=outs, compiler_params=pltpu.CompilerPara...  28.9 us
    ppermute x11, waiting for transfers between devices, send(): return lax.ppermute(value, 'seq', pairs)  15.6 us
    all_to_all x1, blocking collectives, local(): lax.all_to_all(copies, ('seq', 'dp'), 0, 0)  13.4 us
    ppermute x11, starting transfers between devices, send(): return lax.ppermute(value, 'seq', pairs)  10.6 us
    unnamed x16, local copies, waits for them, and re-layouts  3.47 us
  transfers between devices with their start and end apart: 11, of which 2 were waited for; matrix products, arithmetic and copies ran while one was open for 0% of the time, Pallas kernels for 18%

profile of v5, /device:TPU:0, one launch (start us, length us, event | category | flops | bytes accessed | tf_op | source)
XLA Modules:
  0.0 73.4 jit_solution(1434763425310562895)
XLA Ops:
  0.6 0.7 copy-done.2
  1.3 1.0 %copy-done.4 = bf16[1,256,1024]{2,1,0:T(8,128)(2,1)S(1)} copy-done((bf16[1,256,1024]{2,1,0:T(8,128)(2,1)S(1)}, bf16[1,256,1024]{2,1,0:T(8,128)(2,1)}, u32[]{:S(2)}) %copy-start.4) | copy-done | bytes 524312
  2.4 1.0 %copy-done.5 = bf16[1,256,1024]{2,1,0:T(8,128)(2,1)S(1)} copy-done((bf16[1,256,1024]{2,1,0:T(8,128)(2,1)S(1)}, bf16[1,256,1024]{2,1,0:T(8,128)(2,1)}, u32[]{:S(2)}) %copy-start.5) | copy-done | bytes 524312
  3.4 0.7 copy-done.6
  4.1 6.4 %span_state.1 = (f32[2056,128]{1,0:T(8,128)S(1)}, f32[1032,128]{1,0:T(8,128)S(1)}, bf16[8,256,256]{2,1,0:T(8,128)(2,1)S(1)}, bf16[8,256,256]{2,1,0:T(8,128)(2,1)S(1)}, f32[8,128,256]{2,1,0:T(8,128)S(1)}) custom-call(s32[1,256]{1,0:T(1,128)S(1)} %copy-done.2, bf16[256,1024]{1,0:T(8,128)(2,1)S(1)} %bitcast.23, bf16[256,1024]{1,0:T(8,128)(2,1)S(1)} %bitcast.27, ...), custom_call_target="tpu_custom_call" | custom-call | flops 5368709120 | bytes 4000000 | tf_op jit(solution)/shard_map/span_state/pallas_call | solution.py:441
  10.5 0.7 collective-permute-start.2
  11.3 2.4 %collective-permute-start = (f32[1032,128]{1,0:T(8,128)S(1)}, f32[1032,128]{1,0:T(8,128)S(1)}, u32[]{:S(2)}, u32[]{:S(2)}) collective-permute-start(f32[1032,128]{1,0:T(8,128)S(1)} %get-tuple-element.49), channel_id=1, source_target_pairs={{0,4},{1,5},{2,6},{3,7}} | collective-permute-start | bytes 1585160 | tf_op jit(solution)/shard_map/ppermute | solution.py:456
  13.7 1.5 %collective-permute-done.prev_ref.m1_ref = f32[1032,128]{1,0:T(8,128)S(1)} collective-permute-done((f32[1032,128]{1,0:T(8,128)S(1)}, f32[1032,128]{1,0:T(8,128)S(1)}, u32[]{:S(2)}, u32[]{:S(2)}) %collective-permute-start) | collective-permute-done | bytes 528416 | tf_op jit(solution)/shard_map/ppermute | solution.py:456
  15.5 0.8 %collective-permute-start.1 = (f32[1032,128]{1,0:T(8,128)S(1)}, f32[1032,128]{1,0:T(8,128)S(1)}, u32[]{:S(2)}, u32[]{:S(2)}) collective-permute-start(f32[1032,128]{1,0:T(8,128)S(1)} %step.1), channel_id=1, source_target_pairs={{4,12},{5,13},{6,14},{7,15}} | collective-permute-start | bytes 1585160 | tf_op jit(solution)/shard_map/ppermute | solution.py:456
  17.0 0.9 %collective-permute-start.3 = (f32[1024,128]{1,0:T(8,128)S(1)}, f32[1024,128]{1,0:T(8,128)S(1)}, u32[]{:S(2)}, u32[]{:S(2)}) collective-permute-start(f32[1024,128]{1,0:T(8,128)S(1)} %get-tuple-element.51), channel_id=1, source_target_pairs={{12,4},{13,5},{14,6},{15,7}} | collective-permute-start | bytes 1572872 | tf_op jit(solution)/shard_map/ppermute | solution.py:456
  17.8 5.1 %span_out.1 = (f32[256,1024]{1,0:T(8,128)S(1)}, f32[256,1024]{1,0:T(8,128)S(1)}, f32[8,256,256]{2,1,0:T(8,128)S(1)}, bf16[8,256,256]{2,1,0:T(8,128)(2,1)S(1)}, b...) custom-call(s32[1,256]{1,0:T(1,128)S(1)} %copy-done.2, ...), custom_call_target="tpu_custom_call" | custom-call | flops 2952790016 | bytes 4000000 | tf_op jit(solution)/shard_map/span_out/pallas_call | solution.py:441
  22.9 0.8 %collective-permute-start.4 = (f32[1032,128]{1,0:T(8,128)S(1)}, f32[1032,128]{1,0:T(8,128)S(1)}, u32[]{:S(2)}, u32[]{:S(2)}) collective-permute-start(f32[1032,128]{1,0:T(8,128)S(1)} %step.1), channel_id=1, source_target_pairs={{4,8},{16,20},{20,24},{24,28},{5,9},{17,21},{21,25},{25,29},{6,10}... | collective-permute-start | bytes 1585160 | tf_op jit(solution)/shard_map/ppermute | solution.py:456
  24.3 0.7 collective-permute-start.5
  25.0 2.6 %span_norm.1 = (bf16[256,1024]{1,0:T(8,128)(2,1)}, f32[256,1024]{1,0:T(8,128)S(1)}, f32[1032,128]{1,0:T(8,128)S(1)}, f32[8,128,128]{2,1,0:T(8,128)S(1)}, f32[1,128]{1,0:T(1,128)S(1)}) custom-call(s32[1,256]{1,0:T(1,128)S(1)} %copy-done.2, bf16[256,1024]{1,0:T(8,128)(2,1)S(1)} %bitcast.19, f32[256,1024]{1,0:T(8,128)S(1)} %get-tuple-element.60.o_ref, ...), custom_call_target="tpu_custom_call" | custom-call | flops 1073741824 | bytes 4000000 | tf_op jit(solution)/shard_map/span_norm/pallas_call | solution.py:441
  27.6 0.7 collective-permute-start.8
  28.3 0.7 collective-permute-start.6
  29.0 0.7 collective-permute-start.7
  30.2 0.9 %collective-permute-start.9 = (f32[1032,128]{1,0:T(8,128)S(1)}, f32[1032,128]{1,0:T(8,128)S(1)}, u32[]{:S(2)}, u32[]{:S(2)}) collective-permute-start(f32[1032,128]{1,0:T(8,128)S(1)} %back.1), channel_id=1, source_target_pairs={{8,4},{9,5},{10,6},{11,7}} | collective-permute-start | bytes 1585160 | tf_op jit(solution)/shard_map/ppermute | solution.py:456
  31.1 6.0 %span_query_grad.1 = (bf16[256,1024]{1,0:T(8,128)(2,1)}, f32[256,1024]{1,0:T(8,128)S(1)}, f32[256,1024]{1,0:T(8,128)S(1)}, f32[256,1024]{1,0:T(8,128)S(1)}) custom-call(s32[1,256]{1,0:T(1,128)S(1)} %copy-done.2, bf16[256,1024]{1,0:T(8,128)(2,1)S(1)} %bitcast.20, bf16[256,1024]{1,0:T(8,128)(2,1)S(1)} %bitcast.25, ...), custom_call_target="tpu_custom_call" | custom-call | flops 3221225472 | bytes 4000000 | tf_op jit(solution)/shard_map/span_query_grad/pallas_call | solution.py:441
  37.1 0.7 back_far.1
  37.8 1.3 %collective-permute-start.10 = (f32[1024,128]{1,0:T(8,128)S(1)}, f32[1024,128]{1,0:T(8,128)S(1)}, u32[]{:S(2)}, u32[]{:S(2)}) collective-permute-start(f32[1024,128]{1,0:T(8,128)S(1)} %get-tuple-element.83), channel_id=1, source_target_pairs={{4,0},{12,8},{20,16},{24,20},{28,24},{5,1},{13,9},{21,17},{25,21},... | collective-permute-start | bytes 1572872 | tf_op jit(solution)/shard_map/ppermute | solution.py:456
  39.1 14.1 %collective-permute-done.10.h_ref = f32[1024,128]{1,0:T(8,128)S(1)} collective-permute-done((f32[1024,128]{1,0:T(8,128)S(1)}, f32[1024,128]{1,0:T(8,128)S(1)}, u32[]{:S(2)}, u32[]{:S(2)}) %collective-permute-start.10) | collective-permute-done | bytes 524320 | tf_op jit(solution)/shard_map/ppermute | solution.py:456
  53.2 6.3 %span_key_grad.1 = (bf16[256,1024]{1,0:T(8,128)(2,1)}, bf16[256,1024]{1,0:T(8,128)(2,1)}, f32[8,256]{1,0:T(8,128)}) custom-call(s32[1,256]{1,0:T(1,128)S(1)} %copy-done.2, bf16[256,1024]{1,0:T(8,128)(2,1)S(1)} %bitcast.26, bf16[256,1024]{1,0:T(8,128)(2,1)S(1)} %bitcast.29, f32[8,256]{1,0:T(8,128)S(1)} %bitcast.32, ...), custom_call_target="tpu_custom_call" | custom-call | flops 3221225472 | bytes 4000000 | tf_op jit(solution)/shard_map/span_key_grad/pallas_call | solution.py:441
  59.5 13.4 %all_to_all.5 = f32[32,1,128]{2,1,0:T(1,128)S(1)} all-to-all(f32[32,1,128]{2,1,0:T(1,128)S(1)} %broadcast_in_dim_broadcast_in_dim.2), channel_id=1, replica_groups=mesh['seq'=8,'dp'=4] {'seq','dp'}, dimensions={0} | all-to-all | bytes 32768 | tf_op jit(solution)/shard_map/all_to_all | solution.py:584
  (27 shorter events, 2.4 us)
Async XLA Ops:
  0.6 0.7 copy-start.2
  1.3 1.0 %copy-start.4 = (bf16[1,256,1024]{2,1,0:T(8,128)(2,1)S(1)}, bf16[1,256,1024]{2,1,0:T(8,128)(2,1)}, u32[]{:S(2)}) copy-start(bf16[1,256,1024]{2,1,0:T(8,128)(2,1)} %param.8) | copy-start | bytes 1572868
  2.4 1.0 %copy-start.5 = (bf16[1,256,1024]{2,1,0:T(8,128)(2,1)S(1)}, bf16[1,256,1024]{2,1,0:T(8,128)(2,1)}, u32[]{:S(2)}) copy-start(bf16[1,256,1024]{2,1,0:T(8,128)(2,1)} %param.9) | copy-start | bytes 1572868
  3.4 0.7 copy-start.6
  10.5 5.8 %collective-permute-start.2 = (f32[2056,128]{1,0:T(8,128)S(1)}, f32[2056,128]{1,0:T(8,128)S(1)}, u32[]{:S(2)}, u32[]{:S(2)}) collective-permute-start(f32[2056,128]{1,0:T(8,128)S(1)} %get-tuple-element.48.ab_ref), channel_id=1, source_target_pairs={{8,12},{9,13},{10,14},{11,15}} | collective-permute-start | bytes 3158024 | tf_op jit(solution)/shard_map/ppermute | solution.py:456
  11.3 3.9 %collective-permute-start = (f32[1032,128]{1,0:T(8,128)S(1)}, f32[1032,128]{1,0:T(8,128)S(1)}, u32[]{:S(2)}, u32[]{:S(2)}) collective-permute-start(f32[1032,128]{1,0:T(8,128)S(1)} %get-tuple-element.49), channel_id=1, source_target_pairs={{0,4},{1,5},{2,6},{3,7}} | collective-permute-start | bytes 1585160 | tf_op jit(solution)/shard_map/ppermute | solution.py:456
  15.5 2.4 %copy-start.1 = (bf16[1,256,1024]{2,1,0:T(8,128)(2,1)S(1)}, bf16[1,256,1024]{2,1,0:T(8,128)(2,1)}, u32[]{:S(2)}) copy-start(bf16[1,256,1024]{2,1,0:T(8,128)(2,1)} %param.7) | copy-start | bytes 1572868
  15.5 8.3 %collective-permute-start.1 = (f32[1032,128]{1,0:T(8,128)S(1)}, f32[1032,128]{1,0:T(8,128)S(1)}, u32[]{:S(2)}, u32[]{:S(2)}) collective-permute-start(f32[1032,128]{1,0:T(8,128)S(1)} %step.1), channel_id=1, source_target_pairs={{4,12},{5,13},{6,14},{7,15}} | collective-permute-start | bytes 1585160 | tf_op jit(solution)/shard_map/ppermute | solution.py:456
  17.0 6.8 %collective-permute-start.3 = (f32[1024,128]{1,0:T(8,128)S(1)}, f32[1024,128]{1,0:T(8,128)S(1)}, u32[]{:S(2)}, u32[]{:S(2)}) collective-permute-start(f32[1024,128]{1,0:T(8,128)S(1)} %get-tuple-element.51), channel_id=1, source_target_pairs={{12,4},{13,5},{14,6},{15,7}} | collective-permute-start | bytes 1572872 | tf_op jit(solution)/shard_map/ppermute | solution.py:456
  22.9 2.1 %copy-start = (bf16[1,256,1024]{2,1,0:T(8,128)(2,1)S(1)}, bf16[1,256,1024]{2,1,0:T(8,128)(2,1)}, u32[]{:S(2)}) copy-start(bf16[1,256,1024]{2,1,0:T(8,128)(2,1)} %param.12) | copy-start | bytes 1572868
  22.9 2.1 %copy-start.3 = (f32[128]{0:T(128)S(1)}, f32[128]{0:T(128)}, u32[]{:S(2)}) copy-start(f32[128]{0:T(128)} %param.13) | copy-start | bytes 1540
  22.9 2.1 %collective-permute-start.4 = (f32[1032,128]{1,0:T(8,128)S(1)}, f32[1032,128]{1,0:T(8,128)S(1)}, u32[]{:S(2)}, u32[]{:S(2)}) collective-permute-start(f32[1032,128]{1,0:T(8,128)S(1)} %step.1), channel_id=1, source_target_pairs={{4,8},{16,20},{20,24},{24,28},{5,9},{17,21},{21,25},{25,29},{6,10}... | collective-permute-start | bytes 1585160 | tf_op jit(solution)/shard_map/ppermute | solution.py:456
  24.3 0.7 collective-permute-start.5
  27.6 2.1 %collective-permute-start.8 = (f32[1032,128]{1,0:T(8,128)S(1)}, f32[1032,128]{1,0:T(8,128)S(1)}, u32[]{:S(2)}, u32[]{:S(2)}) collective-permute-start(f32[1032,128]{1,0:T(8,128)S(1)} %get-tuple-element.74.c_ref), channel_id=1, source_target_pairs={{12,8},{13,9},{14,10},{15,11}} | collective-permute-start | bytes 1585160 | tf_op jit(solution)/shard_map/ppermute | solution.py:456
  28.3 8.8 %collective-permute-start.6 = (f32[1032,128]{1,0:T(8,128)S(1)}, f32[1032,128]{1,0:T(8,128)S(1)}, u32[]{:S(2)}, u32[]{:S(2)}) collective-permute-start(f32[1032,128]{1,0:T(8,128)S(1)} %get-tuple-element.74.c_ref), channel_id=1, source_target_pairs={{16,4},{17,5},{18,6},{19,7}} | collective-permute-start | bytes 1585160 | tf_op jit(solution)/shard_map/ppermute | solution.py:456
  29.0 8.1 %collective-permute-start.7 = (f32[1032,128]{1,0:T(8,128)S(1)}, f32[1032,128]{1,0:T(8,128)S(1)}, u32[]{:S(2)}, u32[]{:S(2)}) collective-permute-start(f32[1032,128]{1,0:T(8,128)S(1)} %get-tuple-element.74.c_ref), channel_id=1, source_target_pairs={{16,12},{17,13},{18,14},{19,15}} | collective-permute-start | bytes 1585160 | tf_op jit(solution)/shard_map/ppermute | solution.py:456
  30.2 7.0 %collective-permute-start.9 = (f32[1032,128]{1,0:T(8,128)S(1)}, f32[1032,128]{1,0:T(8,128)S(1)}, u32[]{:S(2)}, u32[]{:S(2)}) collective-permute-start(f32[1032,128]{1,0:T(8,128)S(1)} %back.1), channel_id=1, source_target_pairs={{8,4},{9,5},{10,6},{11,7}} | collective-permute-start | bytes 1585160 | tf_op jit(solution)/shard_map/ppermute | solution.py:456
  37.1 16.1 %copy-start.7 = (f32[1,256,8]{1,2,0:T(8,128)S(1)}, f32[1,256,8]{1,2,0:T(8,128)}, u32[]{:S(2)}) copy-start(f32[1,256,8]{1,2,0:T(8,128)} %param.10) | copy-start | bytes 24580
  37.8 15.4 %collective-permute-start.10 = (f32[1024,128]{1,0:T(8,128)S(1)}, f32[1024,128]{1,0:T(8,128)S(1)}, u32[]{:S(2)}, u32[]{:S(2)}) collective-permute-start(f32[1024,128]{1,0:T(8,128)S(1)} %get-tuple-element.83), channel_id=1, source_target_pairs={{4,0},{12,8},{20,16},{24,20},{28,24},{5,1},{13,9},{21,17},{25,21},... | collective-permute-start | bytes 1572872 | tf_op jit(solution)/shard_map/ppermute | solution.py:456

commit v6 on v5

--- a/solution.py
+++ b/solution.py
@@ -10,6 +10,7 @@
 HEADS = 8
 DIM = 128
 BASE = 16
+TOGETHER = 4
 ROWS = HEADS * DIM
 META = 8
 HIGHEST = lax.Precision.HIGHEST
@@ -249,23 +250,36 @@
 ):
     same, ii, jj, keep, tail, through = id_masks(ids_ref)
     causal = same & (ii >= jj)
-    for j in range(HEADS):
-        q, k = head(q_ref, j), head(k_ref, j)
-        k32 = k.astype(F32)
-        rate = jax.nn.sigmoid(logit_of(beta_ref, j))
-        right = split(writes(head(v_ref, j).astype(F32), k32, rate, inv_norm(k32), keep))
-        solve = (th_ref[j], tl_ref[j])
-        uw_ref[j] = dot3(solve, right)
-        scores = jnp.where(causal, mm(q, k, NT), 0.0)
-        through_solve = split(dot3(split(scores), solve))
-        both = dot3(through_solve, right)
-        put(o_ref, j, both[:, :DIM])
-        put(e_ref, j, q.astype(F32) * keep - both[:, DIM:])
-        ph_ref[j] = jnp.transpose(through_solve[0])
-        pl_ref[j] = jnp.transpose(through_solve[1])
-        ends = split(jnp.transpose(z_ref[j]))
-        put(zh_ref, j, ends[0])
-        put(zl_ref, j, ends[1])
+    for start in range(0, HEADS, TOGETHER):
+        heads = range(start, start + TOGETHER)
+        solve = [(th_ref[j], tl_ref[j]) for j in heads]
+        right = []
+        for j in heads:
+            k32 = head(k_ref, j).astype(F32)
+            rate = jax.nn.sigmoid(logit_of(beta_ref, j))
+            value = head(v_ref, j).astype(F32)
+            right.append(split(writes(value, k32, rate, inv_norm(k32), keep)))
+        scores = [
+            split(jnp.where(causal, mm(head(q_ref, j), head(k_ref, j), NT), 0.0)) for j in heads
+        ]
+        solved = [split(lower3(x, t)) for x, t in zip(scores, solve)]
+        for at, j in enumerate(heads):
+            both = dot3(solved[at], right[at])
+            put(o_ref, j, both[:, :DIM])
+            put(e_ref, j, head(q_ref, j).astype(F32) * keep - both[:, DIM:])
+            uw_ref[j] = dot3(solve[at], right[at])
+            ph_ref[j] = jnp.transpose(solved[at][0])
+            pl_ref[j] = jnp.transpose(solved[at][1])
+            ends = split(jnp.transpose(z_ref[j]))
+            put(zh_ref, j, ends[0])
+            put(zl_ref, j, ends[1])
+
+
+def lower3(a, b):
+    n = a[0].shape[0] // 2
+    top = pack3([p[:n, :n] for p in a], [p[:n, :n] for p in b])
+    low = dot3([p[n:] for p in a], b)
+    return cat([cat([top, jnp.zeros_like(top)], 1), low], 0)
 
 
 def kernel_step(ids_ref, ab_ref, prev_ref, out_ref):
@@ -339,21 +353,29 @@
 ):
     gain = gain_ref[...]
     dgain = jnp.zeros((1, DIM), F32)
-    for j in range(HEADS):
-        iq = inv_norm(head(q_ref, j).astype(F32))
-        effective = split(head(e_ref, j))
-        raw = head(o_ref, j) + pack3(effective, split(states[j]))
-        out = raw * iq
-        inv = lax.rsqrt(jnp.mean(out * out, axis=-1, keepdims=True) + 1e-05)
-        unit = out * inv
-        put(y_ref, j, unit * gain)
-        cot = head(cot_ref, j).astype(F32)
-        dgain = dgain + jnp.sum(cot * unit, axis=0, keepdims=True)
-        pulled = cot * gain
-        dout = inv * (pulled - unit * jnp.mean(pulled * unit, axis=-1, keepdims=True))
-        draw = dout * iq
-        put(do_ref, j, draw)
-        block(c_ref, j)[...] = joined * wide3(effective, split(draw), TN)
+    for start in range(0, HEADS, TOGETHER):
+        heads = range(start, start + TOGETHER)
+        iq = [inv_norm(head(q_ref, j).astype(F32)) for j in heads]
+        effective = [split(head(e_ref, j)) for j in heads]
+        out = [
+            i * (head(o_ref, j) + pack3(e, split(states[j])))
+            for j, e, i in zip(heads, effective, iq)
+        ]
+        inv = [
+            lax.rsqrt(jnp.mean(x * x, axis=-1, keepdims=True) + 1e-05) for x in out
+        ]
+        unit = [x * i for x, i in zip(out, inv)]
+        cot = [head(cot_ref, j).astype(F32) for j in heads]
+        pulled = [x * gain for x in cot]
+        means = [jnp.mean(p * u, axis=-1, keepdims=True) for p, u in zip(pulled, unit)]
+        draw = [
+            (i * r) * (p - u * m) for i, r, p, u, m in zip(inv, iq, pulled, unit, means)
+        ]
+        for at, j in enumerate(heads):
+            put(do_ref, j, draw[at])
+            block(c_ref, j)[...] = joined * wide3(effective[at], split(draw[at]), TN)
+            put(y_ref, j, unit[at] * gain)
+            dgain = dgain + jnp.sum(cot[at] * unit[at], axis=0, keepdims=True)
     c_ref[ROWS:] = notes(joined)
     dg_ref[...] = dgain
 
@@ -385,22 +407,27 @@
 ):
     same, ii, jj, keep, tail, through = id_masks(ids_ref)
     causal = same & (ii >= jj)
-    for j in range(HEADS):
-        q, k = head(q_ref, j), head(k_ref, j)
-        q32 = q.astype(F32)
-        state = split(s_ref[j])
-        uw = uw_ref[j]
-        update = uw[:, :DIM] - pack3(split(uw[:, DIM:]), state)
-        draw = head(do_ref, j)
-        draws = split(draw)
-        weights = split(jnp.where(causal, outer3(draws, split(update)), 0.0))
-        dq = keep * pack3_nt(draws, state) + dot2(weights, k)
-        iq = inv_norm(q32)
-        dq = dq - q32 * (iq * iq * jnp.sum(q32 * dq, axis=-1, keepdims=True))
-        put(dq_ref, j, dq)
-        put(u_ref, j, update)
-        put(dr_ref, j, wide3((ph_ref[j], pl_ref[j]), draws))
-        put(dk_ref, j, dot2(weights, q, TN))
+    for start in range(0, HEADS, TOGETHER):
+        heads = range(start, start + TOGETHER)
+        state = [split(s_ref[j]) for j in heads]
+        update = [
+            uw_ref[j, :, :DIM] - pack3(split(uw_ref[j, :, DIM:]), x)
+            for j, x in zip(heads, state)
+        ]
+        draws = [split(head(do_ref, j)) for j in heads]
+        weights = [
+            split(jnp.where(causal, outer3(d, split(u)), 0.0)) for d, u in zip(draws, update)
+        ]
+        for at, j in enumerate(heads):
+            q, k = head(q_ref, j), head(k_ref, j)
+            q32 = q.astype(F32)
+            dq = keep * pack3_nt(draws[at], state[at]) + dot2(weights[at], k)
+            iq = inv_norm(q32)
+            dq = dq - q32 * (iq * iq * jnp.sum(q32 * dq, axis=-1, keepdims=True))
+            put(dq_ref, j, dq)
+            put(u_ref, j, update[at])
+            put(dr_ref, j, wide3((ph_ref[j], pl_ref[j]), draws[at]))
+            put(dk_ref, j, dot2(weights[at], q, TN))
 
 
 def kernel_e(
@@ -412,28 +439,41 @@
     shape = (db_ref.shape[1], db_ref.shape[0])
     lane = lax.broadcasted_iota(jnp.int32, shape, 1)
     dbeta = jnp.zeros(shape, F32)
-    heads = range(HEADS)
-    for j in heads:
-        k = head(k_ref, j)
-        k32 = k.astype(F32)
-        ik = inv_norm(k32)
-        logit = logit_of(beta_ref, j)
-        rate = jax.nn.sigmoid(logit)
-        update = head(u_ref, j)
-        updates = split(update)
-        back = split(g_ref[j] + block(h_ref, j)[...])
-        dright = head(dr_ref, j) + pack3((head(zh_ref, j), head(zl_ref, j)), back)
-        put(dv_ref, j, dright * (rate * ik))
-        dlogit = jax.nn.sigmoid(-logit) * jnp.sum(dright * update, axis=-1, keepdims=True)
-        dbeta = jnp.where(lane == j, dlogit, dbeta)
-        scaled = dright * (rate * ik * ik)
-        inner = split(jnp.where(strict, outer3(split(-scaled), updates), 0.0))
-        dk = head(dkl_ref, j) + (dot2(inner, k) + dot2(inner, k, TN))
-        dk = dk + tail * pack3_nt(updates, back)
-        dk = dk - keep * pack3_nt(split(scaled), split(s_ref[j]))
-        dk = dk - k32 * (ik * ik * jnp.sum(k32 * dk, axis=-1, keepdims=True))
-        put(dk_ref, j, dk)
-
+    for start in range(0, HEADS, TOGETHER):
+        heads = range(start, start + TOGETHER)
+        k32 = [head(k_ref, j).astype(F32) for j in heads]
+        ik = [inv_norm(k) for k in k32]
+        logit = [logit_of(beta_ref, j) for j in heads]
+        rate = [jax.nn.sigmoid(x) for x in logit]
+        back = [split(g_ref[j] + block(h_ref, j)[...]) for j in heads]
+        dright = [
+            head(dr_ref, j) + pack3((head(zh_ref, j), head(zl_ref, j)), g)
+            for j, g in zip(heads, back)
+        ]
+        update = [head(u_ref, j) for j in heads]
+        updates = [split(u) for u in update]
+        scaled = [split(d * (-r * i * i)) for d, r, i in zip(dright, rate, ik)]
+        inner = []
+        for x, u in zip(scaled, updates):
+            top = outer3([p[:DIM] for p in x], [p[:DIM] for p in u])
+            low = outer3([p[DIM:] for p in x], u)
+            top = jnp.where(strict[:DIM, :DIM], top, 0.0)
+            low = jnp.where(strict[DIM:], low, 0.0)
+            left, right = low[:, :DIM], low[:, DIM:]
+            top = cat([top + jnp.transpose(top), jnp.transpose(left)], 1)
+            low = cat([left, right + jnp.transpose(right)], 1)
+            inner.append(split(cat([top, low], 0)))
+        for at, j in enumerate(heads):
+            put(dv_ref, j, dright[at] * (rate[at] * ik[at]))
+            dlogit = jax.nn.sigmoid(-logit[at]) * jnp.sum(
+                dright[at] * update[at], axis=-1, keepdims=True
+            )
+            dbeta = jnp.where(lane == j, dlogit, dbeta)
+            dk = head(dkl_ref, j) + dot2(inner[at], head(k_ref, j))
+            dk = dk + tail * pack3_nt(updates[at], back[at])
+            dk = dk + keep * pack3_nt(scaled[at], split(s_ref[j]))
+            dk = dk - k32[at] * (ik[at] * ik[at] * jnp.sum(k32[at] * dk, axis=-1, keepdims=True))
+            put(dk_ref, j, dk)
     db_ref[...] = jnp.transpose(dbeta)
 
 
@@ -560,10 +600,18 @@
             kernel_c_known, (joined, q, o0, eff, entering, cot, gain),
             (wide16, wide, one, row), 4 * unit, "span_norm",
         )
+    rows = lax.axis_size("dp")
+    got = lax.ppermute(dgain, "dp", [(i, i ^ 1) for i in range(rows)])
     dq, update, dright, dkl = call(
         kernel_d, (ids, q, k, ph, pl_, draw, uw, entering), (wide16, wide, wide, wide),
         12 * unit, "span_query_grad",
     )
+    got, update = lax.optimization_barrier((got, update))
+    dgain = dgain + got
+    step = 2
+    while step < rows:
+        dgain = dgain + lax.ppermute(dgain, "dp", [(i, i ^ step) for i in range(rows)])
+        step *= 2
     if short:
         n3, n4, update = lax.optimization_barrier((n3, n4, update))
         back, last = call(
@@ -579,9 +627,8 @@
         (wide16, wide16, shape(HEADS, tokens)), 12 * unit, "span_key_grad",
     )
     dgain, dbeta = lax.optimization_barrier((dgain, dbeta))
-    devices = spans * lax.axis_size("dp")
-    copies = jnp.broadcast_to(dgain, (devices, DIM))[:, None]
-    gain_total = jnp.sum(lax.all_to_all(copies, ("seq", "dp"), 0, 0), axis=(0, 1))
+    copies = jnp.broadcast_to(dgain, (spans, DIM))[:, None]
+    gain_total = jnp.sum(lax.all_to_all(copies, "seq", 0, 0), axis=(0, 1))
     return (mixed[None], dq[None], dk[None], dv[None], jnp.transpose(dbeta)[None], gain_total)
 
 

time: 73.8 us -> 68.5 us (0.928)
  Pallas kernels: 28.9 us -> 22.7 us
  starting transfers between devices: 10.6 us -> 15.5 us
  blocking collectives: 13.4 us -> 10.2 us
  waiting for transfers between devices: 15.6 us -> 14.7 us
    pallas_call x10, Pallas kernels: 28.9 us -> 22.7 us  [call(): pl.pallas_call(kernel, out_shape=outs, compiler_params=pltpu.CompilerPara...]
    ppermute x0 -> x2, starting transfers between devices: none -> 5.11 us  [the longest x1 2.65 us: local(): lax.ppermute(dgain, 'dp', [(i, i ^ step) for i in range(rows)])]
    all_to_all x1, blocking collectives: 13.4 us -> 10.2 us  [local(): gain_total = jnp.sum(lax.all_to_all(copies, 'seq', 0, 0), axis=(0, 1))]
    ppermute x11, waiting for transfers between devices: 15.6 us -> 12.9 us  [send(): return lax.ppermute(value, 'seq', pairs)]
    ppermute x0 -> x2, waiting for transfers between devices: none -> 1.85 us  [the longest x1 1.85 us: local(): lax.ppermute(dgain, 'dp', [(i, i ^ step) for i in range(rows)])]
  transfers between devices with their start and end apart: 11 -> 13, of which waited for: 2 -> 3; matrix products, arithmetic and copies ran while one was open for 0% -> 0% of each run, Pallas kernels for 18% -> 13%
where the time goes in v6:
time: 68.5 us; the launch traced here: 68.1 us
  Pallas kernels  22.7 us (33%)
  starting transfers between devices  15.5 us (23%)
  waiting for transfers between devices  14.7 us (21%)
  blocking collectives  10.2 us (15%)
  local copies, waits for them, and re-layouts  3.48 us (5%)
  between operations  0.9 us (1%)
    pallas_call x10, Pallas kernels, call(): pl.pallas_call(kernel, out_shape=outs, compiler_params=pltpu.CompilerPara...  22.7 us
    ppermute x11, waiting for transfers between devices, send(): return lax.ppermute(value, 'seq', pairs)  12.9 us
    ppermute x11, starting transfers between devices, send(): return lax.ppermute(value, 'seq', pairs)  10.4 us
    all_to_all x1, blocking collectives, local(): gain_total = jnp.sum(lax.all_to_all(copies, 'seq', 0, 0), axis=(0, 1))  10.2 us
    unnamed x16, local copies, waits for them, and re-layouts  3.47 us
    ppermute x1, starting transfers between devices, local(): lax.ppermute(dgain, 'dp', [(i, i ^ step) for i in range(rows)])  2.65 us
    ppermute x1, starting transfers between devices, local(): got = lax.ppermute(dgain, 'dp', [(i, i ^ 1) for i in range(rows)])  2.46 us
    ppermute x1, waiting for transfers between devices, local(): lax.ppermute(dgain, 'dp', [(i, i ^ step) for i in range(rows)])  1.85 us
  transfers between devices with their start and end apart: 13, of which 3 were waited for; matrix products, arithmetic and copies ran while one was open for 0% of the time, Pallas kernels for 13%

profile of v6, /device:TPU:0, one launch (start us, length us, event | category | flops | bytes accessed | tf_op | source)
XLA Modules:
  0.0 68.1 jit_solution(18083153418452626037)
XLA Ops:
  1.3 1.0 %copy-done.4 = bf16[1,256,1024]{2,1,0:T(8,128)(2,1)S(1)} copy-done((bf16[1,256,1024]{2,1,0:T(8,128)(2,1)S(1)}, bf16[1,256,1024]{2,1,0:T(8,128)(2,1)}, u32[]{:S(2)}) %copy-start.4) | copy-done | bytes 524312
  2.4 1.0 %copy-done.5 = bf16[1,256,1024]{2,1,0:T(8,128)(2,1)S(1)} copy-done((bf16[1,256,1024]{2,1,0:T(8,128)(2,1)S(1)}, bf16[1,256,1024]{2,1,0:T(8,128)(2,1)}, u32[]{:S(2)}) %copy-start.5) | copy-done | bytes 524312
  3.4 0.7 %copy-done.6 = f32[1,256,8]{1,2,0:T(8,128)S(1)} copy-done((f32[1,256,8]{1,2,0:T(8,128)S(1)}, f32[1,256,8]{1,2,0:T(8,128)}, u32[]{:S(2)}) %copy-start.6) | copy-done | bytes 8216
  4.1 6.4 %span_state.1 = (f32[2056,128]{1,0:T(8,128)S(1)}, f32[1032,128]{1,0:T(8,128)S(1)}, bf16[8,256,256]{2,1,0:T(8,128)(2,1)S(1)}, bf16[8,256,256]{2,1,0:T(8,128)(2,1)S(1)}, f32[8,128,256]{2,1,0:T(8,128)S(1)}) custom-call(s32[1,256]{1,0:T(1,128)S(1)} %copy-done.2, bf16[256,1024]{1,0:T(8,128)(2,1)S(1)} %bitcast.22, bf16[256,1024]{1,0:T(8,128)(2,1)S(1)} %bitcast.26, ...), custom_call_target="tpu_custom_call" | custom-call | flops 5368709120 | bytes 4000000 | tf_op jit(solution)/shard_map/span_state/pallas_call | solution.py:481
  10.5 0.7 %collective-permute-start.2 = (f32[2056,128]{1,0:T(8,128)S(1)}, f32[2056,128]{1,0:T(8,128)S(1)}, u32[]{:S(2)}, u32[]{:S(2)}) collective-permute-start(f32[2056,128]{1,0:T(8,128)S(1)} %get-tuple-element.50.ab_ref), channel_id=1, source_target_pairs={{8,12},{9,13},{10,14},{11,15}} | collective-permute-start | bytes 3158024 | tf_op jit(solution)/shard_map/ppermute | solution.py:496
  11.3 2.4 %collective-permute-start = (f32[1032,128]{1,0:T(8,128)S(1)}, f32[1032,128]{1,0:T(8,128)S(1)}, u32[]{:S(2)}, u32[]{:S(2)}) collective-permute-start(f32[1032,128]{1,0:T(8,128)S(1)} %get-tuple-element.51), channel_id=1, source_target_pairs={{0,4},{1,5},{2,6},{3,7}} | collective-permute-start | bytes 1585160 | tf_op jit(solution)/shard_map/ppermute | solution.py:496
  13.7 1.5 %collective-permute-done.prev_ref.m1_ref = f32[1032,128]{1,0:T(8,128)S(1)} collective-permute-done((f32[1032,128]{1,0:T(8,128)S(1)}, f32[1032,128]{1,0:T(8,128)S(1)}, u32[]{:S(2)}, u32[]{:S(2)}) %collective-permute-start) | collective-permute-done | bytes 528416 | tf_op jit(solution)/shard_map/ppermute | solution.py:496
  15.5 0.8 %collective-permute-start.1 = (f32[1032,128]{1,0:T(8,128)S(1)}, f32[1032,128]{1,0:T(8,128)S(1)}, u32[]{:S(2)}, u32[]{:S(2)}) collective-permute-start(f32[1032,128]{1,0:T(8,128)S(1)} %step.1), channel_id=1, source_target_pairs={{4,12},{5,13},{6,14},{7,15}} | collective-permute-start | bytes 1585160 | tf_op jit(solution)/shard_map/ppermute | solution.py:496
  17.0 0.7 %collective-permute-start.3 = (f32[1024,128]{1,0:T(8,128)S(1)}, f32[1024,128]{1,0:T(8,128)S(1)}, u32[]{:S(2)}, u32[]{:S(2)}) collective-permute-start(f32[1024,128]{1,0:T(8,128)S(1)} %get-tuple-element.53), channel_id=1, source_target_pairs={{12,4},{13,5},{14,6},{15,7}} | collective-permute-start | bytes 1572872 | tf_op jit(solution)/shard_map/ppermute | solution.py:496
  17.7 3.0 %span_out.1 = (f32[256,1024]{1,0:T(8,128)S(1)}, f32[256,1024]{1,0:T(8,128)S(1)}, f32[8,256,256]{2,1,0:T(8,128)S(1)}, bf16[8,256,256]{2,1,0:T(8,128)(2,1)S(1)}, b...) custom-call(s32[1,256]{1,0:T(1,128)S(1)} %copy-done.2, ...), custom_call_target="tpu_custom_call" | custom-call | flops 2952790016 | bytes 4000000 | tf_op jit(solution)/shard_map/span_out/pallas_call | solution.py:481
  20.7 0.8 %collective-permute-start.4 = (f32[1032,128]{1,0:T(8,128)S(1)}, f32[1032,128]{1,0:T(8,128)S(1)}, u32[]{:S(2)}, u32[]{:S(2)}) collective-permute-start(f32[1032,128]{1,0:T(8,128)S(1)} %step.1), channel_id=1, source_target_pairs={{4,8},{16,20},{20,24},{24,28},{5,9},{17,21},{21,25},{25,29},{6,10}... | collective-permute-start | bytes 1585160 | tf_op jit(solution)/shard_map/ppermute | solution.py:496
  22.1 0.9 %collective-permute-start.5 = (f32[1032,128]{1,0:T(8,128)S(1)}, f32[1032,128]{1,0:T(8,128)S(1)}, u32[]{:S(2)}, u32[]{:S(2)}) collective-permute-start(f32[1032,128]{1,0:T(8,128)S(1)} %apply.1), channel_id=1, source_target_pairs={{12,16},{13,17},{14,18},{15,19}} | collective-permute-start | bytes 1585160 | tf_op jit(solution)/shard_map/ppermute | solution.py:496
  23.0 2.5 %span_norm.1 = (bf16[256,1024]{1,0:T(8,128)(2,1)}, f32[256,1024]{1,0:T(8,128)S(1)}, f32[1032,128]{1,0:T(8,128)S(1)}, f32[8,128,128]{2,1,0:T(8,128)S(1)}, f32[1,128]{1,0:T(1,128)S(1)}) custom-call(s32[1,256]{1,0:T(1,128)S(1)} %copy-done.2, bf16[256,1024]{1,0:T(8,128)(2,1)S(1)} %bitcast.19, f32[256,1024]{1,0:T(8,128)S(1)} %get-tuple-element.62.o_ref, ...), custom_call_target="tpu_custom_call" | custom-call | flops 1073741824 | bytes 4000000 | tf_op jit(solution)/shard_map/span_norm/pallas_call | solution.py:481
  26.2 0.7 %collective-permute-start.6 = (f32[1032,128]{1,0:T(8,128)S(1)}, f32[1032,128]{1,0:T(8,128)S(1)}, u32[]{:S(2)}, u32[]{:S(2)}) collective-permute-start(f32[1032,128]{1,0:T(8,128)S(1)} %get-tuple-element.76.c_ref), channel_id=1, source_target_pairs={{16,4},{17,5},{18,6},{19,7}} | collective-permute-start | bytes 1585160 | tf_op jit(solution)/shard_map/ppermute | solution.py:496
  26.9 0.7 %collective-permute-start.7 = (f32[1032,128]{1,0:T(8,128)S(1)}, f32[1032,128]{1,0:T(8,128)S(1)}, u32[]{:S(2)}, u32[]{:S(2)}) collective-permute-start(f32[1032,128]{1,0:T(8,128)S(1)} %get-tuple-element.76.c_ref), channel_id=1, source_target_pairs={{16,12},{17,13},{18,14},{19,15}} | collective-permute-start | bytes 1585160 | tf_op jit(solution)/shard_map/ppermute | solution.py:496
  28.0 0.7 %collective-permute-start.10 = (f32[1032,128]{1,0:T(8,128)S(1)}, f32[1032,128]{1,0:T(8,128)S(1)}, u32[]{:S(2)}, u32[]{:S(2)}) collective-permute-start(f32[1032,128]{1,0:T(8,128)S(1)} %back.1), channel_id=1, source_target_pairs={{8,4},{9,5},{10,6},{11,7}} | collective-permute-start | bytes 1585160 | tf_op jit(solution)/shard_map/ppermute | solution.py:496
  28.7 2.5 %collective-permute-start.8 = (f32[1,128]{1,0:T(1,128)S(1)}, f32[1,128]{1,0:T(1,128)S(1)}, u32[]{:S(2)}, u32[]{:S(2)}) collective-permute-start(f32[1,128]{1,0:T(1,128)S(1)} %get-tuple-element.77), channel_id=1, source_target_pairs={{0,1},{1,0},{2,3},{3,2},{4,5},{5,4},{6,7},{7,6},{8,9},{9,8},{10,11... | collective-permute-start | bytes 1544 | tf_op jit(solution)/shard_map/ppermute | solution.py:604
  31.2 4.0 %span_query_grad.1 = (bf16[256,1024]{1,0:T(8,128)(2,1)}, f32[256,1024]{1,0:T(8,128)S(1)}, f32[256,1024]{1,0:T(8,128)S(1)}, f32[256,1024]{1,0:T(8,128)S(1)}) custom-call(s32[1,256]{1,0:T(1,128)S(1)} %copy-done.2, bf16[256,1024]{1,0:T(8,128)(2,1)S(1)} %bitcast.20, bf16[256,1024]{1,0:T(8,128)(2,1)S(1)} %bitcast.24, ...), custom_call_target="tpu_custom_call" | custom-call | flops 3221225472 | bytes 4000000 | tf_op jit(solution)/shard_map/span_query_grad/pallas_call | solution.py:481
  35.8 1.3 %collective-permute-start.11 = (f32[1024,128]{1,0:T(8,128)S(1)}, f32[1024,128]{1,0:T(8,128)S(1)}, u32[]{:S(2)}, u32[]{:S(2)}) collective-permute-start(f32[1024,128]{1,0:T(8,128)S(1)} %get-tuple-element.87), channel_id=1, source_target_pairs={{4,0},{12,8},{20,16},{24,20},{28,24},{5,1},{13,9},{21,17},{25,21},... | collective-permute-start | bytes 1572872 | tf_op jit(solution)/shard_map/ppermute | solution.py:496
  37.2 2.7 %collective-permute-start.12 = (f32[1,128]{1,0:T(1,128)S(1)}, f32[1,128]{1,0:T(1,128)S(1)}, u32[]{:S(2)}, u32[]{:S(2)}) collective-permute-start(f32[1,128]{1,0:T(1,128)S(1)} %add.6), channel_id=1, source_target_pairs={{0,2},{1,3},{2,0},{3,1},{4,6},{5,7},{6,4},{7,5},{8,10},{9,11},{10,... | collective-permute-start | bytes 1544 | tf_op jit(solution)/shard_map/ppermute | solution.py:613
  39.8 1.9 %collective-permute-done.12 = f32[1,128]{1,0:T(1,128)S(1)} collective-permute-done((f32[1,128]{1,0:T(1,128)S(1)}, f32[1,128]{1,0:T(1,128)S(1)}, u32[]{:S(2)}, u32[]{:S(2)}) %collective-permute-start.12) | collective-permute-done | bytes 544 | tf_op jit(solution)/shard_map/ppermute | solution.py:613
  41.7 11.4 %collective-permute-done.11.h_ref = f32[1024,128]{1,0:T(8,128)S(1)} collective-permute-done((f32[1024,128]{1,0:T(8,128)S(1)}, f32[1024,128]{1,0:T(8,128)S(1)}, u32[]{:S(2)}, u32[]{:S(2)}) %collective-permute-start.11) | collective-permute-done | bytes 524320 | tf_op jit(solution)/shard_map/ppermute | solution.py:496
  53.0 4.3 %span_key_grad.1 = (bf16[256,1024]{1,0:T(8,128)(2,1)}, bf16[256,1024]{1,0:T(8,128)(2,1)}, f32[8,256]{1,0:T(8,128)}) custom-call(s32[1,256]{1,0:T(1,128)S(1)} %copy-done.2, bf16[256,1024]{1,0:T(8,128)(2,1)S(1)} %bitcast.25, bf16[256,1024]{1,0:T(8,128)(2,1)S(1)} %bitcast.28, f32[8,256]{1,0:T(8,128)S(1)} %bitcast.31, ...), custom_call_target="tpu_custom_call" | custom-call | flops 3221225472 | bytes 4000000 | tf_op jit(solution)/shard_map/span_key_grad/pallas_call | solution.py:481
  57.4 10.2 %all_to_all.5 = f32[8,1,128]{2,1,0:T(1,128)S(1)} all-to-all(f32[8,1,128]{2,1,0:T(1,128)S(1)} %broadcast_in_dim_broadcast_in_dim.2), channel_id=1, replica_groups=mesh['seq'=8,'dp'=4] {'seq'}, dimensions={0} | all-to-all | bytes 8192 | tf_op jit(solution)/shard_map/all_to_all | solution.py:631
  (33 shorter events, 4.4 us)
Async XLA Ops:
  0.6 0.7 copy-start.2
  1.3 1.0 %copy-start.4 = (bf16[1,256,1024]{2,1,0:T(8,128)(2,1)S(1)}, bf16[1,256,1024]{2,1,0:T(8,128)(2,1)}, u32[]{:S(2)}) copy-start(bf16[1,256,1024]{2,1,0:T(8,128)(2,1)} %param.8) | copy-start | bytes 1572868
  2.4 1.0 %copy-start.5 = (bf16[1,256,1024]{2,1,0:T(8,128)(2,1)S(1)}, bf16[1,256,1024]{2,1,0:T(8,128)(2,1)}, u32[]{:S(2)}) copy-start(bf16[1,256,1024]{2,1,0:T(8,128)(2,1)} %param.9) | copy-start | bytes 1572868
  3.4 0.7 %copy-start.6 = (f32[1,256,8]{1,2,0:T(8,128)S(1)}, f32[1,256,8]{1,2,0:T(8,128)}, u32[]{:S(2)}) copy-start(f32[1,256,8]{1,2,0:T(8,128)} %param.10) | copy-start | bytes 24580
  10.5 5.8 %collective-permute-start.2 = (f32[2056,128]{1,0:T(8,128)S(1)}, f32[2056,128]{1,0:T(8,128)S(1)}, u32[]{:S(2)}, u32[]{:S(2)}) collective-permute-start(f32[2056,128]{1,0:T(8,128)S(1)} %get-tuple-element.50.ab_ref), channel_id=1, source_target_pairs={{8,12},{9,13},{10,14},{11,15}} | collective-permute-start | bytes 3158024 | tf_op jit(solution)/shard_map/ppermute | solution.py:496
  11.3 3.9 %collective-permute-start = (f32[1032,128]{1,0:T(8,128)S(1)}, f32[1032,128]{1,0:T(8,128)S(1)}, u32[]{:S(2)}, u32[]{:S(2)}) collective-permute-start(f32[1032,128]{1,0:T(8,128)S(1)} %get-tuple-element.51), channel_id=1, source_target_pairs={{0,4},{1,5},{2,6},{3,7}} | collective-permute-start | bytes 1585160 | tf_op jit(solution)/shard_map/ppermute | solution.py:496
  15.5 2.2 %copy-start.1 = (bf16[1,256,1024]{2,1,0:T(8,128)(2,1)S(1)}, bf16[1,256,1024]{2,1,0:T(8,128)(2,1)}, u32[]{:S(2)}) copy-start(bf16[1,256,1024]{2,1,0:T(8,128)(2,1)} %param.7) | copy-start | bytes 1572868
  15.5 6.1 %collective-permute-start.1 = (f32[1032,128]{1,0:T(8,128)S(1)}, f32[1032,128]{1,0:T(8,128)S(1)}, u32[]{:S(2)}, u32[]{:S(2)}) collective-permute-start(f32[1032,128]{1,0:T(8,128)S(1)} %step.1), channel_id=1, source_target_pairs={{4,12},{5,13},{6,14},{7,15}} | collective-permute-start | bytes 1585160 | tf_op jit(solution)/shard_map/ppermute | solution.py:496
  17.0 4.6 %collective-permute-start.3 = (f32[1024,128]{1,0:T(8,128)S(1)}, f32[1024,128]{1,0:T(8,128)S(1)}, u32[]{:S(2)}, u32[]{:S(2)}) collective-permute-start(f32[1024,128]{1,0:T(8,128)S(1)} %get-tuple-element.53), channel_id=1, source_target_pairs={{12,4},{13,5},{14,6},{15,7}} | collective-permute-start | bytes 1572872 | tf_op jit(solution)/shard_map/ppermute | solution.py:496
  20.7 2.3 %copy-start = (bf16[1,256,1024]{2,1,0:T(8,128)(2,1)S(1)}, bf16[1,256,1024]{2,1,0:T(8,128)(2,1)}, u32[]{:S(2)}) copy-start(bf16[1,256,1024]{2,1,0:T(8,128)(2,1)} %param.12) | copy-start | bytes 1572868
  20.7 2.3 %copy-start.3 = (f32[128]{0:T(128)S(1)}, f32[128]{0:T(128)}, u32[]{:S(2)}) copy-start(f32[128]{0:T(128)} %param.13) | copy-start | bytes 1540
  20.7 2.2 %collective-permute-start.4 = (f32[1032,128]{1,0:T(8,128)S(1)}, f32[1032,128]{1,0:T(8,128)S(1)}, u32[]{:S(2)}, u32[]{:S(2)}) collective-permute-start(f32[1032,128]{1,0:T(8,128)S(1)} %step.1), channel_id=1, source_target_pairs={{4,8},{16,20},{20,24},{24,28},{5,9},{17,21},{21,25},{25,29},{6,10}... | collective-permute-start | bytes 1585160 | tf_op jit(solution)/shard_map/ppermute | solution.py:496
  22.1 0.9 %collective-permute-start.5 = (f32[1032,128]{1,0:T(8,128)S(1)}, f32[1032,128]{1,0:T(8,128)S(1)}, u32[]{:S(2)}, u32[]{:S(2)}) collective-permute-start(f32[1032,128]{1,0:T(8,128)S(1)} %apply.1), channel_id=1, source_target_pairs={{12,16},{13,17},{14,18},{15,19}} | collective-permute-start | bytes 1585160 | tf_op jit(solution)/shard_map/ppermute | solution.py:496
  25.5 2.1 %collective-permute-start.9 = (f32[1032,128]{1,0:T(8,128)S(1)}, f32[1032,128]{1,0:T(8,128)S(1)}, u32[]{:S(2)}, u32[]{:S(2)}) collective-permute-start(f32[1032,128]{1,0:T(8,128)S(1)} %get-tuple-element.76.c_ref), channel_id=1, source_target_pairs={{12,8},{13,9},{14,10},{15,11}} | collective-permute-start | bytes 1585160 | tf_op jit(solution)/shard_map/ppermute | solution.py:496
  26.2 9.0 %collective-permute-start.6 = (f32[1032,128]{1,0:T(8,128)S(1)}, f32[1032,128]{1,0:T(8,128)S(1)}, u32[]{:S(2)}, u32[]{:S(2)}) collective-permute-start(f32[1032,128]{1,0:T(8,128)S(1)} %get-tuple-element.76.c_ref), channel_id=1, source_target_pairs={{16,4},{17,5},{18,6},{19,7}} | collective-permute-start | bytes 1585160 | tf_op jit(solution)/shard_map/ppermute | solution.py:496
  26.9 8.3 %collective-permute-start.7 = (f32[1032,128]{1,0:T(8,128)S(1)}, f32[1032,128]{1,0:T(8,128)S(1)}, u32[]{:S(2)}, u32[]{:S(2)}) collective-permute-start(f32[1032,128]{1,0:T(8,128)S(1)} %get-tuple-element.76.c_ref), channel_id=1, source_target_pairs={{16,12},{17,13},{18,14},{19,15}} | collective-permute-start | bytes 1585160 | tf_op jit(solution)/shard_map/ppermute | solution.py:496
  28.0 7.1 %collective-permute-start.10 = (f32[1032,128]{1,0:T(8,128)S(1)}, f32[1032,128]{1,0:T(8,128)S(1)}, u32[]{:S(2)}, u32[]{:S(2)}) collective-permute-start(f32[1032,128]{1,0:T(8,128)S(1)} %back.1), channel_id=1, source_target_pairs={{8,4},{9,5},{10,6},{11,7}} | collective-permute-start | bytes 1585160 | tf_op jit(solution)/shard_map/ppermute | solution.py:496
  28.7 6.4 %collective-permute-start.8 = (f32[1,128]{1,0:T(1,128)S(1)}, f32[1,128]{1,0:T(1,128)S(1)}, u32[]{:S(2)}, u32[]{:S(2)}) collective-permute-start(f32[1,128]{1,0:T(1,128)S(1)} %get-tuple-element.77), channel_id=1, source_target_pairs={{0,1},{1,0},{2,3},{3,2},{4,5},{5,4},{6,7},{7,6},{8,9},{9,8},{10,11... | collective-permute-start | bytes 1544 | tf_op jit(solution)/shard_map/ppermute | solution.py:604
  35.1 17.9 %copy-start.7 = (f32[1,256,8]{1,2,0:T(8,128)S(1)}, f32[1,256,8]{1,2,0:T(8,128)}, u32[]{:S(2)}) copy-start(f32[1,256,8]{1,2,0:T(8,128)} %param.10) | copy-start | bytes 24580
  35.8 17.2 %collective-permute-start.11 = (f32[1024,128]{1,0:T(8,128)S(1)}, f32[1024,128]{1,0:T(8,128)S(1)}, u32[]{:S(2)}, u32[]{:S(2)}) collective-permute-start(f32[1024,128]{1,0:T(8,128)S(1)} %get-tuple-element.87), channel_id=1, source_target_pairs={{4,0},{12,8},{20,16},{24,20},{28,24},{5,1},{13,9},{21,17},{25,21},... | collective-permute-start | bytes 1572872 | tf_op jit(solution)/shard_map/ppermute | solution.py:496
  37.2 4.5 %collective-permute-start.12 = (f32[1,128]{1,0:T(1,128)S(1)}, f32[1,128]{1,0:T(1,128)S(1)}, u32[]{:S(2)}, u32[]{:S(2)}) collective-permute-start(f32[1,128]{1,0:T(1,128)S(1)} %add.6), channel_id=1, source_target_pairs={{0,2},{1,3},{2,0},{3,1},{4,6},{5,7},{6,4},{7,5},{8,10},{9,11},{10,... | collective-permute-start | bytes 1544 | tf_op jit(solution)/shard_map/ppermute | solution.py:613

commit v7 on v6

--- a/solution.py
+++ b/solution.py
@@ -174,20 +174,7 @@
     return ts
 
 
-def kernel_a(
-    ids_in, k_in, v_in, beta_in, ab_ref, b_ref, th_ref, tl_ref, z_ref,
-    ids_ref, k_ref, v_ref, beta_ref, sems,
-):
-    copies = [
-        pltpu.make_async_copy(source, target, sems.at[at])
-        for at, (source, target) in enumerate(
-            ((ids_in, ids_ref), (k_in, k_ref), (beta_in, beta_ref), (v_in, v_ref))
-        )
-    ]
-    for copy in copies:
-        copy.start()
-    for copy in copies[:3]:
-        copy.wait()
+def kernel_a(ids_ref, k_ref, v_ref, beta_ref, ab_ref, b_ref, th_ref, tl_ref, z_ref):
     same, ii, jj, keep, tail, through = id_masks(ids_ref)
     strict = same & (ii > jj)
     heads = range(HEADS)
@@ -224,7 +211,6 @@
         == lax.broadcasted_iota(jnp.int32, (DIM, DIM), 1)
     ).astype(F32)
     zs = [dot2r((k * tail).astype(BF16), full, TN) for k, full in zip(k32, fulls)]
-    copies[3].wait()
     for j in heads:
         right = writes(head(v_ref, j).astype(F32), k32[j], rates[j], iks[j], keep)
         both = dot3(split(zs[j]), split(right))
@@ -553,14 +539,6 @@
     ab, bm, th, tl, z = call(
         kernel_a, (ids, k, v, beta), (two, one, square, square, shape(HEADS, DIM, tokens)),
         20 * unit, "span_state",
-        in_specs=[pl.BlockSpec(memory_space=pltpu.HBM)] * 4,
-        scratch_shapes=[
-            pltpu.VMEM(ids.shape, ids.dtype),
-            pltpu.VMEM(k.shape, k.dtype),
-            pltpu.VMEM(v.shape, v.dtype),
-            pltpu.VMEM(beta.shape, beta.dtype),
-            pltpu.SemaphoreType.DMA((4,)),
-        ],
     )
     if short:
         r1 = send(bm, [(0, 1)])
@@ -609,9 +587,10 @@
     got, update = lax.optimization_barrier((got, update))
     dgain = dgain + got
     step = 2
-    while step < rows:
+    while 2 * step < rows:
         dgain = dgain + lax.ppermute(dgain, "dp", [(i, i ^ step) for i in range(rows)])
         step *= 2
+    got = lax.ppermute(dgain, "dp", [(i, i ^ step) for i in range(rows)])
     if short:
         n3, n4, update = lax.optimization_barrier((n3, n4, update))
         back, last = call(
@@ -626,7 +605,8 @@
         kernel_e, (ids, k, v, beta, zh, zl, update, dright, dkl, entering, back, far),
         (wide16, wide16, shape(HEADS, tokens)), 12 * unit, "span_key_grad",
     )
-    dgain, dbeta = lax.optimization_barrier((dgain, dbeta))
+    got, dbeta = lax.optimization_barrier((got, dbeta))
+    dgain = dgain + got
     copies = jnp.broadcast_to(dgain, (spans, DIM))[:, None]
     gain_total = jnp.sum(lax.all_to_all(copies, "seq", 0, 0), axis=(0, 1))
     return (mixed[None], dq[None], dk[None], dv[None], jnp.transpose(dbeta)[None], gain_total)

time: 68.5 us -> 67 us (0.978)
  blocking collectives: 10.2 us -> 9.3 us
    ppermute x1, waiting for transfers between devices: 1.85 us -> 0.01 us  [local(): got = lax.ppermute(dgain, 'dp', [(i, i ^ step) for i in range(rows)])]
    ppermute x11, waiting for transfers between devices: 12.9 us -> 14.7 us  [send(): return lax.ppermute(value, 'seq', pairs)]
    all_to_all x1, blocking collectives: 10.2 us -> 9.3 us  [local(): gain_total = jnp.sum(lax.all_to_all(copies, 'seq', 0, 0), axis=(0, 1))]
  transfers between devices with their start and end apart: 13 -> 13, of which waited for: 3 -> 2; matrix products, arithmetic and copies ran while one was open for 0% -> 0% of each run, Pallas kernels for 13% -> 20%
where the time goes in v7:
time: 67 us; the launch traced here: 66.6 us
  Pallas kernels  22.1 us (33%)
  starting transfers between devices  15.5 us (23%)
  waiting for transfers between devices  14.7 us (22%)
  blocking collectives  9.3 us (14%)
  local copies, waits for them, and re-layouts  3.48 us (5%)
  between operations  0.9 us (1%)
    pallas_call x10, Pallas kernels, call(): pl.pallas_call(kernel, out_shape=outs, compiler_params=pltpu.CompilerPara...  22.1 us
    ppermute x11, waiting for transfers between devices, send(): return lax.ppermute(value, 'seq', pairs)  14.7 us
    ppermute x11, starting transfers between devices, send(): return lax.ppermute(value, 'seq', pairs)  10.4 us
    all_to_all x1, blocking collectives, local(): gain_total = jnp.sum(lax.all_to_all(copies, 'seq', 0, 0), axis=(0, 1))  9.3 us
    unnamed x16, local copies, waits for them, and re-layouts  3.47 us
    ppermute x1, starting transfers between devices, local(): got = lax.ppermute(dgain, 'dp', [(i, i ^ step) for i in range(rows)])  2.64 us
    ppermute x1, starting transfers between devices, local(): got = lax.ppermute(dgain, 'dp', [(i, i ^ 1) for i in range(rows)])  2.49 us
  transfers between devices with their start and end apart: 13, of which 2 were waited for; matrix products, arithmetic and copies ran while one was open for 0% of the time, Pallas kernels for 20%

profile of v7, /device:TPU:0, one launch (start us, length us, event | category | flops | bytes accessed | tf_op | source)
XLA Modules:
  0.0 66.6 jit_solution(4353842850655811689)
XLA Ops:
  1.3 1.0 %copy-done.4 = bf16[1,256,1024]{2,1,0:T(8,128)(2,1)S(1)} copy-done((bf16[1,256,1024]{2,1,0:T(8,128)(2,1)S(1)}, bf16[1,256,1024]{2,1,0:T(8,128)(2,1)}, u32[]{:S(2)}) %copy-start.4) | copy-done | bytes 524312
  2.4 1.0 %copy-done.5 = bf16[1,256,1024]{2,1,0:T(8,128)(2,1)S(1)} copy-done((bf16[1,256,1024]{2,1,0:T(8,128)(2,1)S(1)}, bf16[1,256,1024]{2,1,0:T(8,128)(2,1)}, u32[]{:S(2)}) %copy-start.5) | copy-done | bytes 524312
  3.4 0.7 %copy-done.6 = f32[1,256,8]{1,2,0:T(8,128)S(1)} copy-done((f32[1,256,8]{1,2,0:T(8,128)S(1)}, f32[1,256,8]{1,2,0:T(8,128)}, u32[]{:S(2)}) %copy-start.6) | copy-done | bytes 8216
  4.1 5.8 %span_state.1 = (f32[2056,128]{1,0:T(8,128)S(1)}, f32[1032,128]{1,0:T(8,128)S(1)}, bf16[8,256,256]{2,1,0:T(8,128)(2,1)S(1)}, bf16[8,256,256]{2,1,0:T(8,128)(2,1)S(1)}, f32[8,128,256]{2,1,0:T(8,128)S(1)}) custom-call(s32[1,256]{1,0:T(1,128)S(1)} %copy-done.2, bf16[256,1024]{1,0:T(8,128)(2,1)S(1)} %bitcast.23, bf16[256,1024]{1,0:T(8,128)(2,1)S(1)} %bitcast.27, ...), custom_call_target="tpu_custom_call" | custom-call | flops 5368709120 | bytes 4000000 | tf_op jit(solution)/shard_map/span_state/pallas_call | solution.py:467
  9.9 0.7 %collective-permute-start.2 = (f32[2056,128]{1,0:T(8,128)S(1)}, f32[2056,128]{1,0:T(8,128)S(1)}, u32[]{:S(2)}, u32[]{:S(2)}) collective-permute-start(f32[2056,128]{1,0:T(8,128)S(1)} %get-tuple-element.50.ab_ref), channel_id=1, source_target_pairs={{8,12},{9,13},{10,14},{11,15}} | collective-permute-start | bytes 3158024 | tf_op jit(solution)/shard_map/ppermute | solution.py:482
  10.7 2.4 %collective-permute-start = (f32[1032,128]{1,0:T(8,128)S(1)}, f32[1032,128]{1,0:T(8,128)S(1)}, u32[]{:S(2)}, u32[]{:S(2)}) collective-permute-start(f32[1032,128]{1,0:T(8,128)S(1)} %get-tuple-element.51), channel_id=1, source_target_pairs={{0,4},{1,5},{2,6},{3,7}} | collective-permute-start | bytes 1585160 | tf_op jit(solution)/shard_map/ppermute | solution.py:482
  13.1 1.5 %collective-permute-done.prev_ref.m1_ref = f32[1032,128]{1,0:T(8,128)S(1)} collective-permute-done((f32[1032,128]{1,0:T(8,128)S(1)}, f32[1032,128]{1,0:T(8,128)S(1)}, u32[]{:S(2)}, u32[]{:S(2)}) %collective-permute-start) | collective-permute-done | bytes 528416 | tf_op jit(solution)/shard_map/ppermute | solution.py:482
  14.9 0.8 %collective-permute-start.1 = (f32[1032,128]{1,0:T(8,128)S(1)}, f32[1032,128]{1,0:T(8,128)S(1)}, u32[]{:S(2)}, u32[]{:S(2)}) collective-permute-start(f32[1032,128]{1,0:T(8,128)S(1)} %step.1), channel_id=1, source_target_pairs={{4,12},{5,13},{6,14},{7,15}} | collective-permute-start | bytes 1585160 | tf_op jit(solution)/shard_map/ppermute | solution.py:482
  16.4 0.7 %collective-permute-start.3 = (f32[1024,128]{1,0:T(8,128)S(1)}, f32[1024,128]{1,0:T(8,128)S(1)}, u32[]{:S(2)}, u32[]{:S(2)}) collective-permute-start(f32[1024,128]{1,0:T(8,128)S(1)} %get-tuple-element.53), channel_id=1, source_target_pairs={{12,4},{13,5},{14,6},{15,7}} | collective-permute-start | bytes 1572872 | tf_op jit(solution)/shard_map/ppermute | solution.py:482
  17.1 3.0 %span_out.1 = (f32[256,1024]{1,0:T(8,128)S(1)}, f32[256,1024]{1,0:T(8,128)S(1)}, f32[8,256,256]{2,1,0:T(8,128)S(1)}, bf16[8,256,256]{2,1,0:T(8,128)(2,1)S(1)}, b...) custom-call(s32[1,256]{1,0:T(1,128)S(1)} %copy-done.2, ...), custom_call_target="tpu_custom_call" | custom-call | flops 2952790016 | bytes 4000000 | tf_op jit(solution)/shard_map/span_out/pallas_call | solution.py:467
  20.1 0.8 %collective-permute-start.4 = (f32[1032,128]{1,0:T(8,128)S(1)}, f32[1032,128]{1,0:T(8,128)S(1)}, u32[]{:S(2)}, u32[]{:S(2)}) collective-permute-start(f32[1032,128]{1,0:T(8,128)S(1)} %step.1), channel_id=1, source_target_pairs={{4,8},{16,20},{20,24},{24,28},{5,9},{17,21},{21,25},{25,29},{6,10}... | collective-permute-start | bytes 1585160 | tf_op jit(solution)/shard_map/ppermute | solution.py:482
  21.5 0.9 %collective-permute-start.5 = (f32[1032,128]{1,0:T(8,128)S(1)}, f32[1032,128]{1,0:T(8,128)S(1)}, u32[]{:S(2)}, u32[]{:S(2)}) collective-permute-start(f32[1032,128]{1,0:T(8,128)S(1)} %apply.1), channel_id=1, source_target_pairs={{12,16},{13,17},{14,18},{15,19}} | collective-permute-start | bytes 1585160 | tf_op jit(solution)/shard_map/ppermute | solution.py:482
  22.4 2.5 %span_norm.1 = (bf16[256,1024]{1,0:T(8,128)(2,1)}, f32[256,1024]{1,0:T(8,128)S(1)}, f32[1032,128]{1,0:T(8,128)S(1)}, f32[8,128,128]{2,1,0:T(8,128)S(1)}, f32[1,128]{1,0:T(1,128)S(1)}) custom-call(s32[1,256]{1,0:T(1,128)S(1)} %copy-done.2, bf16[256,1024]{1,0:T(8,128)(2,1)S(1)} %bitcast.20, f32[256,1024]{1,0:T(8,128)S(1)} %get-tuple-element.62.o_ref, ...), custom_call_target="tpu_custom_call" | custom-call | flops 1073741824 | bytes 4000000 | tf_op jit(solution)/shard_map/span_norm/pallas_call | solution.py:467
  24.9 0.7 %collective-permute-start.9 = (f32[1032,128]{1,0:T(8,128)S(1)}, f32[1032,128]{1,0:T(8,128)S(1)}, u32[]{:S(2)}, u32[]{:S(2)}) collective-permute-start(f32[1032,128]{1,0:T(8,128)S(1)} %get-tuple-element.76.c_ref), channel_id=1, source_target_pairs={{12,8},{13,9},{14,10},{15,11}} | collective-permute-start | bytes 1585160 | tf_op jit(solution)/shard_map/ppermute | solution.py:482
  25.6 0.7 %collective-permute-start.6 = (f32[1032,128]{1,0:T(8,128)S(1)}, f32[1032,128]{1,0:T(8,128)S(1)}, u32[]{:S(2)}, u32[]{:S(2)}) collective-permute-start(f32[1032,128]{1,0:T(8,128)S(1)} %get-tuple-element.76.c_ref), channel_id=1, source_target_pairs={{16,4},{17,5},{18,6},{19,7}} | collective-permute-start | bytes 1585160 | tf_op jit(solution)/shard_map/ppermute | solution.py:482
  26.3 0.7 %collective-permute-start.7 = (f32[1032,128]{1,0:T(8,128)S(1)}, f32[1032,128]{1,0:T(8,128)S(1)}, u32[]{:S(2)}, u32[]{:S(2)}) collective-permute-start(f32[1032,128]{1,0:T(8,128)S(1)} %get-tuple-element.76.c_ref), channel_id=1, source_target_pairs={{16,12},{17,13},{18,14},{19,15}} | collective-permute-start | bytes 1585160 | tf_op jit(solution)/shard_map/ppermute | solution.py:482
  27.4 0.7 %collective-permute-start.10 = (f32[1032,128]{1,0:T(8,128)S(1)}, f32[1032,128]{1,0:T(8,128)S(1)}, u32[]{:S(2)}, u32[]{:S(2)}) collective-permute-start(f32[1032,128]{1,0:T(8,128)S(1)} %back.1), channel_id=1, source_target_pairs={{8,4},{9,5},{10,6},{11,7}} | collective-permute-start | bytes 1585160 | tf_op jit(solution)/shard_map/ppermute | solution.py:482
  28.1 2.5 %collective-permute-start.8 = (f32[1,128]{1,0:T(1,128)S(1)}, f32[1,128]{1,0:T(1,128)S(1)}, u32[]{:S(2)}, u32[]{:S(2)}) collective-permute-start(f32[1,128]{1,0:T(1,128)S(1)} %get-tuple-element.77), channel_id=1, source_target_pairs={{0,1},{1,0},{2,3},{3,2},{4,5},{5,4},{6,7},{7,6},{8,9},{9,8},{10,11... | collective-permute-start | bytes 1544 | tf_op jit(solution)/shard_map/ppermute | solution.py:582
  30.6 4.0 %span_query_grad.1 = (bf16[256,1024]{1,0:T(8,128)(2,1)}, f32[256,1024]{1,0:T(8,128)S(1)}, f32[256,1024]{1,0:T(8,128)S(1)}, f32[256,1024]{1,0:T(8,128)S(1)}) custom-call(s32[1,256]{1,0:T(1,128)S(1)} %copy-done.2, bf16[256,1024]{1,0:T(8,128)(2,1)S(1)} %bitcast.21, bf16[256,1024]{1,0:T(8,128)(2,1)S(1)} %bitcast.25, ...), custom_call_target="tpu_custom_call" | custom-call | flops 3221225472 | bytes 4000000 | tf_op jit(solution)/shard_map/span_query_grad/pallas_call | solution.py:467
  35.3 1.3 %collective-permute-start.11 = (f32[1024,128]{1,0:T(8,128)S(1)}, f32[1024,128]{1,0:T(8,128)S(1)}, u32[]{:S(2)}, u32[]{:S(2)}) collective-permute-start(f32[1024,128]{1,0:T(8,128)S(1)} %get-tuple-element.87), channel_id=1, source_target_pairs={{4,0},{12,8},{20,16},{24,20},{28,24},{5,1},{13,9},{21,17},{25,21},... | collective-permute-start | bytes 1572872 | tf_op jit(solution)/shard_map/ppermute | solution.py:482
  36.6 2.6 %collective-permute-start.12 = (f32[1,128]{1,0:T(1,128)S(1)}, f32[1,128]{1,0:T(1,128)S(1)}, u32[]{:S(2)}, u32[]{:S(2)}) collective-permute-start(f32[1,128]{1,0:T(1,128)S(1)} %add.8), channel_id=1, source_target_pairs={{0,2},{1,3},{2,0},{3,1},{4,6},{5,7},{6,4},{7,5},{8,10},{9,11},{10,... | collective-permute-start | bytes 1544 | tf_op jit(solution)/shard_map/ppermute | solution.py:593
  39.2 13.2 %collective-permute-done.11.h_ref = f32[1024,128]{1,0:T(8,128)S(1)} collective-permute-done((f32[1024,128]{1,0:T(8,128)S(1)}, f32[1024,128]{1,0:T(8,128)S(1)}, u32[]{:S(2)}, u32[]{:S(2)}) %collective-permute-start.11) | collective-permute-done | bytes 524320 | tf_op jit(solution)/shard_map/ppermute | solution.py:482
  52.4 4.3 %span_key_grad.1 = (bf16[256,1024]{1,0:T(8,128)(2,1)}, bf16[256,1024]{1,0:T(8,128)(2,1)}, f32[8,256]{1,0:T(8,128)}) custom-call(s32[1,256]{1,0:T(1,128)S(1)} %copy-done.2, bf16[256,1024]{1,0:T(8,128)(2,1)S(1)} %bitcast.26, bf16[256,1024]{1,0:T(8,128)(2,1)S(1)} %bitcast.29, f32[8,256]{1,0:T(8,128)S(1)} %bitcast.32, ...), custom_call_target="tpu_custom_call" | custom-call | flops 3221225472 | bytes 4000000 | tf_op jit(solution)/shard_map/span_key_grad/pallas_call | solution.py:467
  56.8 9.3 %all_to_all.5 = f32[8,1,128]{2,1,0:T(1,128)S(1)} all-to-all(f32[8,1,128]{2,1,0:T(1,128)S(1)} %broadcast_in_dim_broadcast_in_dim.2), channel_id=1, replica_groups=mesh['seq'=8,'dp'=4] {'seq'}, dimensions={0} | all-to-all | bytes 8192 | tf_op jit(solution)/shard_map/all_to_all | solution.py:611
  (33 shorter events, 3.8 us)
Async XLA Ops:
  0.6 0.7 %copy-start.2 = (s32[1,256]{1,0:T(1,128)S(1)}, s32[1,256]{1,0:T(1,128)}, u32[]{:S(2)}) copy-start(s32[1,256]{1,0:T(1,128)} %ids_ref.13) | copy-start | bytes 3076
  1.3 1.0 %copy-start.4 = (bf16[1,256,1024]{2,1,0:T(8,128)(2,1)S(1)}, bf16[1,256,1024]{2,1,0:T(8,128)(2,1)}, u32[]{:S(2)}) copy-start(bf16[1,256,1024]{2,1,0:T(8,128)(2,1)} %param.8) | copy-start | bytes 1572868
  2.4 1.0 %copy-start.5 = (bf16[1,256,1024]{2,1,0:T(8,128)(2,1)S(1)}, bf16[1,256,1024]{2,1,0:T(8,128)(2,1)}, u32[]{:S(2)}) copy-start(bf16[1,256,1024]{2,1,0:T(8,128)(2,1)} %param.9) | copy-start | bytes 1572868
  3.4 0.7 %copy-start.6 = (f32[1,256,8]{1,2,0:T(8,128)S(1)}, f32[1,256,8]{1,2,0:T(8,128)}, u32[]{:S(2)}) copy-start(f32[1,256,8]{1,2,0:T(8,128)} %param.10) | copy-start | bytes 24580
  9.9 5.8 %collective-permute-start.2 = (f32[2056,128]{1,0:T(8,128)S(1)}, f32[2056,128]{1,0:T(8,128)S(1)}, u32[]{:S(2)}, u32[]{:S(2)}) collective-permute-start(f32[2056,128]{1,0:T(8,128)S(1)} %get-tuple-element.50.ab_ref), channel_id=1, source_target_pairs={{8,12},{9,13},{10,14},{11,15}} | collective-permute-start | bytes 3158024 | tf_op jit(solution)/shard_map/ppermute | solution.py:482
  10.7 3.9 %collective-permute-start = (f32[1032,128]{1,0:T(8,128)S(1)}, f32[1032,128]{1,0:T(8,128)S(1)}, u32[]{:S(2)}, u32[]{:S(2)}) collective-permute-start(f32[1032,128]{1,0:T(8,128)S(1)} %get-tuple-element.51), channel_id=1, source_target_pairs={{0,4},{1,5},{2,6},{3,7}} | collective-permute-start | bytes 1585160 | tf_op jit(solution)/shard_map/ppermute | solution.py:482
  14.9 2.2 %copy-start.1 = (bf16[1,256,1024]{2,1,0:T(8,128)(2,1)S(1)}, bf16[1,256,1024]{2,1,0:T(8,128)(2,1)}, u32[]{:S(2)}) copy-start(bf16[1,256,1024]{2,1,0:T(8,128)(2,1)} %param.7) | copy-start | bytes 1572868
  14.9 6.1 %collective-permute-start.1 = (f32[1032,128]{1,0:T(8,128)S(1)}, f32[1032,128]{1,0:T(8,128)S(1)}, u32[]{:S(2)}, u32[]{:S(2)}) collective-permute-start(f32[1032,128]{1,0:T(8,128)S(1)} %step.1), channel_id=1, source_target_pairs={{4,12},{5,13},{6,14},{7,15}} | collective-permute-start | bytes 1585160 | tf_op jit(solution)/shard_map/ppermute | solution.py:482
  16.4 4.6 %collective-permute-start.3 = (f32[1024,128]{1,0:T(8,128)S(1)}, f32[1024,128]{1,0:T(8,128)S(1)}, u32[]{:S(2)}, u32[]{:S(2)}) collective-permute-start(f32[1024,128]{1,0:T(8,128)S(1)} %get-tuple-element.53), channel_id=1, source_target_pairs={{12,4},{13,5},{14,6},{15,7}} | collective-permute-start | bytes 1572872 | tf_op jit(solution)/shard_map/ppermute | solution.py:482
  20.1 2.3 %copy-start = (bf16[1,256,1024]{2,1,0:T(8,128)(2,1)S(1)}, bf16[1,256,1024]{2,1,0:T(8,128)(2,1)}, u32[]{:S(2)}) copy-start(bf16[1,256,1024]{2,1,0:T(8,128)(2,1)} %param.12) | copy-start | bytes 1572868
  20.1 2.3 %copy-start.3 = (f32[128]{0:T(128)S(1)}, f32[128]{0:T(128)}, u32[]{:S(2)}) copy-start(f32[128]{0:T(128)} %param.13) | copy-start | bytes 1540
  20.1 2.2 %collective-permute-start.4 = (f32[1032,128]{1,0:T(8,128)S(1)}, f32[1032,128]{1,0:T(8,128)S(1)}, u32[]{:S(2)}, u32[]{:S(2)}) collective-permute-start(f32[1032,128]{1,0:T(8,128)S(1)} %step.1), channel_id=1, source_target_pairs={{4,8},{16,20},{20,24},{24,28},{5,9},{17,21},{21,25},{25,29},{6,10}... | collective-permute-start | bytes 1585160 | tf_op jit(solution)/shard_map/ppermute | solution.py:482
  21.5 0.9 %collective-permute-start.5 = (f32[1032,128]{1,0:T(8,128)S(1)}, f32[1032,128]{1,0:T(8,128)S(1)}, u32[]{:S(2)}, u32[]{:S(2)}) collective-permute-start(f32[1032,128]{1,0:T(8,128)S(1)} %apply.1), channel_id=1, source_target_pairs={{12,16},{13,17},{14,18},{15,19}} | collective-permute-start | bytes 1585160 | tf_op jit(solution)/shard_map/ppermute | solution.py:482
  24.9 2.1 %collective-permute-start.9 = (f32[1032,128]{1,0:T(8,128)S(1)}, f32[1032,128]{1,0:T(8,128)S(1)}, u32[]{:S(2)}, u32[]{:S(2)}) collective-permute-start(f32[1032,128]{1,0:T(8,128)S(1)} %get-tuple-element.76.c_ref), channel_id=1, source_target_pairs={{12,8},{13,9},{14,10},{15,11}} | collective-permute-start | bytes 1585160 | tf_op jit(solution)/shard_map/ppermute | solution.py:482
  25.6 9.0 %collective-permute-start.6 = (f32[1032,128]{1,0:T(8,128)S(1)}, f32[1032,128]{1,0:T(8,128)S(1)}, u32[]{:S(2)}, u32[]{:S(2)}) collective-permute-start(f32[1032,128]{1,0:T(8,128)S(1)} %get-tuple-element.76.c_ref), channel_id=1, source_target_pairs={{16,4},{17,5},{18,6},{19,7}} | collective-permute-start | bytes 1585160 | tf_op jit(solution)/shard_map/ppermute | solution.py:482
  26.3 8.3 %collective-permute-start.7 = (f32[1032,128]{1,0:T(8,128)S(1)}, f32[1032,128]{1,0:T(8,128)S(1)}, u32[]{:S(2)}, u32[]{:S(2)}) collective-permute-start(f32[1032,128]{1,0:T(8,128)S(1)} %get-tuple-element.76.c_ref), channel_id=1, source_target_pairs={{16,12},{17,13},{18,14},{19,15}} | collective-permute-start | bytes 1585160 | tf_op jit(solution)/shard_map/ppermute | solution.py:482
  27.4 7.2 %collective-permute-start.10 = (f32[1032,128]{1,0:T(8,128)S(1)}, f32[1032,128]{1,0:T(8,128)S(1)}, u32[]{:S(2)}, u32[]{:S(2)}) collective-permute-start(f32[1032,128]{1,0:T(8,128)S(1)} %back.1), channel_id=1, source_target_pairs={{8,4},{9,5},{10,6},{11,7}} | collective-permute-start | bytes 1585160 | tf_op jit(solution)/shard_map/ppermute | solution.py:482
  28.1 6.5 %collective-permute-start.8 = (f32[1,128]{1,0:T(1,128)S(1)}, f32[1,128]{1,0:T(1,128)S(1)}, u32[]{:S(2)}, u32[]{:S(2)}) collective-permute-start(f32[1,128]{1,0:T(1,128)S(1)} %get-tuple-element.77), channel_id=1, source_target_pairs={{0,1},{1,0},{2,3},{3,2},{4,5},{5,4},{6,7},{7,6},{8,9},{9,8},{10,11... | collective-permute-start | bytes 1544 | tf_op jit(solution)/shard_map/ppermute | solution.py:582
  34.6 17.9 %copy-start.7 = (f32[1,256,8]{1,2,0:T(8,128)S(1)}, f32[1,256,8]{1,2,0:T(8,128)}, u32[]{:S(2)}) copy-start(f32[1,256,8]{1,2,0:T(8,128)} %param.10) | copy-start | bytes 24580
  35.3 17.2 %collective-permute-start.11 = (f32[1024,128]{1,0:T(8,128)S(1)}, f32[1024,128]{1,0:T(8,128)S(1)}, u32[]{:S(2)}, u32[]{:S(2)}) collective-permute-start(f32[1024,128]{1,0:T(8,128)S(1)} %get-tuple-element.87), channel_id=1, source_target_pairs={{4,0},{12,8},{20,16},{24,20},{28,24},{5,1},{13,9},{21,17},{25,21},... | collective-permute-start | bytes 1572872 | tf_op jit(solution)/shard_map/ppermute | solution.py:482
  36.6 20.2 %collective-permute-start.12 = (f32[1,128]{1,0:T(1,128)S(1)}, f32[1,128]{1,0:T(1,128)S(1)}, u32[]{:S(2)}, u32[]{:S(2)}) collective-permute-start(f32[1,128]{1,0:T(1,128)S(1)} %add.8), channel_id=1, source_target_pairs={{0,2},{1,3},{2,0},{3,1},{4,6},{5,7},{6,4},{7,5},{8,10},{9,11},{10,... | collective-permute-start | bytes 1544 | tf_op jit(solution)/shard_map/ppermute | solution.py:593

commit v8 on v7

--- a/solution.py
+++ b/solution.py
@@ -167,9 +167,9 @@
     while s < n:
         offs = [split(off(b, s)) for b in blocks]
         tss = [split(t) for t in ts]
-        mids = [dot3(o, t) for o, t in zip(offs, tss)]
+        mids = [pack3(o, t) for o, t in zip(offs, tss)]
         mids = [split(m) for m in mids]
-        ts = [t - dot3(p, m) for t, p, m in zip(ts, tss, mids)]
+        ts = [t - pack3(p, m) for t, p, m in zip(ts, tss, mids)]
         s *= 2
     return ts
 
@@ -190,8 +190,8 @@
     ts = inverse(blocks)
     t1s = [split(t) for t in ts[0::2]]
     t2s = [split(t) for t in ts[1::2]]
-    mids = [split(dot3(split(n[DIM:, :DIM]), t)) for n, t in zip(ns, t1s)]
-    lows = [split(-dot3(t, m)) for t, m in zip(t2s, mids)]
+    mids = [split(pack3(split(n[DIM:, :DIM]), t)) for n, t in zip(ns, t1s)]
+    lows = [split(-pack3(t, m)) for t, m in zip(t2s, mids)]
     zero = jnp.zeros((DIM, DIM), BF16)
     fulls = [
         tuple(

time: 67 us -> 66.4 us (level)
  Pallas kernels: 22.1 us -> 21.3 us
    pallas_call x10, Pallas kernels: 22.1 us -> 21.3 us  [call(): pl.pallas_call(kernel, out_shape=outs, compiler_params=pltpu.CompilerPara...]
where the time goes in v8:
time: 66.4 us; the launch traced here: 66 us
  Pallas kernels  21.3 us (32%)
  starting transfers between devices  15.5 us (23%)
  waiting for transfers between devices  14.7 us (22%)
  blocking collectives  9.44 us (14%)
  local copies, waits for them, and re-layouts  3.48 us (5%)
  between operations  0.9 us (1%)
    pallas_call x10, Pallas kernels, call(): pl.pallas_call(kernel, out_shape=outs, compiler_params=pltpu.CompilerPara...  21.3 us
    ppermute x11, waiting for transfers between devices, send(): return lax.ppermute(value, 'seq', pairs)  14.7 us
    ppermute x11, starting transfers between devices, send(): return lax.ppermute(value, 'seq', pairs)  10.4 us
    all_to_all x1, blocking collectives, local(): gain_total = jnp.sum(lax.all_to_all(copies, 'seq', 0, 0), axis=(0, 1))  9.44 us
    unnamed x16, local copies, waits for them, and re-layouts  3.47 us
    ppermute x1, starting transfers between devices, local(): got = lax.ppermute(dgain, 'dp', [(i, i ^ step) for i in range(rows)])  2.64 us
    ppermute x1, starting transfers between devices, local(): got = lax.ppermute(dgain, 'dp', [(i, i ^ 1) for i in range(rows)])  2.48 us
  transfers between devices with their start and end apart: 13, of which 2 were waited for; matrix products, arithmetic and copies ran while one was open for 0% of the time, Pallas kernels for 20%

profile of v8, /device:TPU:0, one launch (start us, length us, event | category | flops | bytes accessed | tf_op | source)
XLA Modules:
  0.0 66.0 jit_solution(9926862632272262194)
XLA Ops:
  1.3 1.0 %copy-done.4 = bf16[1,256,1024]{2,1,0:T(8,128)(2,1)S(1)} copy-done((bf16[1,256,1024]{2,1,0:T(8,128)(2,1)S(1)}, bf16[1,256,1024]{2,1,0:T(8,128)(2,1)}, u32[]{:S(2)}) %copy-start.4) | copy-done | bytes 524312
  2.4 1.0 %copy-done.5 = bf16[1,256,1024]{2,1,0:T(8,128)(2,1)S(1)} copy-done((bf16[1,256,1024]{2,1,0:T(8,128)(2,1)S(1)}, bf16[1,256,1024]{2,1,0:T(8,128)(2,1)}, u32[]{:S(2)}) %copy-start.5) | copy-done | bytes 524312
  3.4 0.7 %copy-done.6 = f32[1,256,8]{1,2,0:T(8,128)S(1)} copy-done((f32[1,256,8]{1,2,0:T(8,128)S(1)}, f32[1,256,8]{1,2,0:T(8,128)}, u32[]{:S(2)}) %copy-start.6) | copy-done | bytes 8216
  4.1 5.0 %span_state.1 = (f32[2056,128]{1,0:T(8,128)S(1)}, f32[1032,128]{1,0:T(8,128)S(1)}, bf16[8,256,256]{2,1,0:T(8,128)(2,1)S(1)}, bf16[8,256,256]{2,1,0:T(8,128)(2,1)S(1)}, f32[8,128,256]{2,1,0:T(8,128)S(1)}) custom-call(s32[1,256]{1,0:T(1,128)S(1)} %copy-done.2, bf16[256,1024]{1,0:T(8,128)(2,1)S(1)} %bitcast.23, bf16[256,1024]{1,0:T(8,128)(2,1)S(1)} %bitcast.27, ...), custom_call_target="tpu_custom_call" | custom-call | flops 5368709120 | bytes 4000000 | tf_op jit(solution)/shard_map/span_state/pallas_call | solution.py:467
  9.1 0.7 %collective-permute-start.2 = (f32[2056,128]{1,0:T(8,128)S(1)}, f32[2056,128]{1,0:T(8,128)S(1)}, u32[]{:S(2)}, u32[]{:S(2)}) collective-permute-start(f32[2056,128]{1,0:T(8,128)S(1)} %get-tuple-element.50.ab_ref), channel_id=1, source_target_pairs={{8,12},{9,13},{10,14},{11,15}} | collective-permute-start | bytes 3158024 | tf_op jit(solution)/shard_map/ppermute | solution.py:482
  9.9 2.4 %collective-permute-start = (f32[1032,128]{1,0:T(8,128)S(1)}, f32[1032,128]{1,0:T(8,128)S(1)}, u32[]{:S(2)}, u32[]{:S(2)}) collective-permute-start(f32[1032,128]{1,0:T(8,128)S(1)} %get-tuple-element.51), channel_id=1, source_target_pairs={{0,4},{1,5},{2,6},{3,7}} | collective-permute-start | bytes 1585160 | tf_op jit(solution)/shard_map/ppermute | solution.py:482
  12.3 1.5 %collective-permute-done.prev_ref.m1_ref = f32[1032,128]{1,0:T(8,128)S(1)} collective-permute-done((f32[1032,128]{1,0:T(8,128)S(1)}, f32[1032,128]{1,0:T(8,128)S(1)}, u32[]{:S(2)}, u32[]{:S(2)}) %collective-permute-start) | collective-permute-done | bytes 528416 | tf_op jit(solution)/shard_map/ppermute | solution.py:482
  14.1 0.8 %collective-permute-start.1 = (f32[1032,128]{1,0:T(8,128)S(1)}, f32[1032,128]{1,0:T(8,128)S(1)}, u32[]{:S(2)}, u32[]{:S(2)}) collective-permute-start(f32[1032,128]{1,0:T(8,128)S(1)} %step.1), channel_id=1, source_target_pairs={{4,12},{5,13},{6,14},{7,15}} | collective-permute-start | bytes 1585160 | tf_op jit(solution)/shard_map/ppermute | solution.py:482
  15.5 0.7 %collective-permute-start.3 = (f32[1024,128]{1,0:T(8,128)S(1)}, f32[1024,128]{1,0:T(8,128)S(1)}, u32[]{:S(2)}, u32[]{:S(2)}) collective-permute-start(f32[1024,128]{1,0:T(8,128)S(1)} %get-tuple-element.53), channel_id=1, source_target_pairs={{12,4},{13,5},{14,6},{15,7}} | collective-permute-start | bytes 1572872 | tf_op jit(solution)/shard_map/ppermute | solution.py:482
  16.3 3.0 %span_out.1 = (f32[256,1024]{1,0:T(8,128)S(1)}, f32[256,1024]{1,0:T(8,128)S(1)}, f32[8,256,256]{2,1,0:T(8,128)S(1)}, bf16[8,256,256]{2,1,0:T(8,128)(2,1)S(1)}, b...) custom-call(s32[1,256]{1,0:T(1,128)S(1)} %copy-done.2, ...), custom_call_target="tpu_custom_call" | custom-call | flops 2952790016 | bytes 4000000 | tf_op jit(solution)/shard_map/span_out/pallas_call | solution.py:467
  19.3 0.8 %collective-permute-start.4 = (f32[1032,128]{1,0:T(8,128)S(1)}, f32[1032,128]{1,0:T(8,128)S(1)}, u32[]{:S(2)}, u32[]{:S(2)}) collective-permute-start(f32[1032,128]{1,0:T(8,128)S(1)} %step.1), channel_id=1, source_target_pairs={{4,8},{16,20},{20,24},{24,28},{5,9},{17,21},{21,25},{25,29},{6,10}... | collective-permute-start | bytes 1585160 | tf_op jit(solution)/shard_map/ppermute | solution.py:482
  20.7 0.7 %collective-permute-start.5 = (f32[1032,128]{1,0:T(8,128)S(1)}, f32[1032,128]{1,0:T(8,128)S(1)}, u32[]{:S(2)}, u32[]{:S(2)}) collective-permute-start(f32[1032,128]{1,0:T(8,128)S(1)} %apply.1), channel_id=1, source_target_pairs={{12,16},{13,17},{14,18},{15,19}} | collective-permute-start | bytes 1585160 | tf_op jit(solution)/shard_map/ppermute | solution.py:482
  21.4 2.5 %span_norm.1 = (bf16[256,1024]{1,0:T(8,128)(2,1)}, f32[256,1024]{1,0:T(8,128)S(1)}, f32[1032,128]{1,0:T(8,128)S(1)}, f32[8,128,128]{2,1,0:T(8,128)S(1)}, f32[1,128]{1,0:T(1,128)S(1)}) custom-call(s32[1,256]{1,0:T(1,128)S(1)} %copy-done.2, bf16[256,1024]{1,0:T(8,128)(2,1)S(1)} %bitcast.20, f32[256,1024]{1,0:T(8,128)S(1)} %get-tuple-element.62.o_ref, ...), custom_call_target="tpu_custom_call" | custom-call | flops 1073741824 | bytes 4000000 | tf_op jit(solution)/shard_map/span_norm/pallas_call | solution.py:467
  23.9 0.9 %collective-permute-start.9 = (f32[1032,128]{1,0:T(8,128)S(1)}, f32[1032,128]{1,0:T(8,128)S(1)}, u32[]{:S(2)}, u32[]{:S(2)}) collective-permute-start(f32[1032,128]{1,0:T(8,128)S(1)} %get-tuple-element.76.c_ref), channel_id=1, source_target_pairs={{12,8},{13,9},{14,10},{15,11}} | collective-permute-start | bytes 1585160 | tf_op jit(solution)/shard_map/ppermute | solution.py:482
  24.8 0.7 %collective-permute-start.6 = (f32[1032,128]{1,0:T(8,128)S(1)}, f32[1032,128]{1,0:T(8,128)S(1)}, u32[]{:S(2)}, u32[]{:S(2)}) collective-permute-start(f32[1032,128]{1,0:T(8,128)S(1)} %get-tuple-element.76.c_ref), channel_id=1, source_target_pairs={{16,4},{17,5},{18,6},{19,7}} | collective-permute-start | bytes 1585160 | tf_op jit(solution)/shard_map/ppermute | solution.py:482
  25.5 0.7 %collective-permute-start.7 = (f32[1032,128]{1,0:T(8,128)S(1)}, f32[1032,128]{1,0:T(8,128)S(1)}, u32[]{:S(2)}, u32[]{:S(2)}) collective-permute-start(f32[1032,128]{1,0:T(8,128)S(1)} %get-tuple-element.76.c_ref), channel_id=1, source_target_pairs={{16,12},{17,13},{18,14},{19,15}} | collective-permute-start | bytes 1585160 | tf_op jit(solution)/shard_map/ppermute | solution.py:482
  26.6 0.7 %collective-permute-start.10 = (f32[1032,128]{1,0:T(8,128)S(1)}, f32[1032,128]{1,0:T(8,128)S(1)}, u32[]{:S(2)}, u32[]{:S(2)}) collective-permute-start(f32[1032,128]{1,0:T(8,128)S(1)} %back.1), channel_id=1, source_target_pairs={{8,4},{9,5},{10,6},{11,7}} | collective-permute-start | bytes 1585160 | tf_op jit(solution)/shard_map/ppermute | solution.py:482
  27.3 2.5 %collective-permute-start.8 = (f32[1,128]{1,0:T(1,128)S(1)}, f32[1,128]{1,0:T(1,128)S(1)}, u32[]{:S(2)}, u32[]{:S(2)}) collective-permute-start(f32[1,128]{1,0:T(1,128)S(1)} %get-tuple-element.77), channel_id=1, source_target_pairs={{0,1},{1,0},{2,3},{3,2},{4,5},{5,4},{6,7},{7,6},{8,9},{9,8},{10,11... | collective-permute-start | bytes 1544 | tf_op jit(solution)/shard_map/ppermute | solution.py:582
  29.8 4.0 %span_query_grad.1 = (bf16[256,1024]{1,0:T(8,128)(2,1)}, f32[256,1024]{1,0:T(8,128)S(1)}, f32[256,1024]{1,0:T(8,128)S(1)}, f32[256,1024]{1,0:T(8,128)S(1)}) custom-call(s32[1,256]{1,0:T(1,128)S(1)} %copy-done.2, bf16[256,1024]{1,0:T(8,128)(2,1)S(1)} %bitcast.21, bf16[256,1024]{1,0:T(8,128)(2,1)S(1)} %bitcast.25, ...), custom_call_target="tpu_custom_call" | custom-call | flops 3221225472 | bytes 4000000 | tf_op jit(solution)/shard_map/span_query_grad/pallas_call | solution.py:467
  34.5 1.3 %collective-permute-start.11 = (f32[1024,128]{1,0:T(8,128)S(1)}, f32[1024,128]{1,0:T(8,128)S(1)}, u32[]{:S(2)}, u32[]{:S(2)}) collective-permute-start(f32[1024,128]{1,0:T(8,128)S(1)} %get-tuple-element.87), channel_id=1, source_target_pairs={{4,0},{12,8},{20,16},{24,20},{28,24},{5,1},{13,9},{21,17},{25,21},... | collective-permute-start | bytes 1572872 | tf_op jit(solution)/shard_map/ppermute | solution.py:482
  35.8 2.6 %collective-permute-start.12 = (f32[1,128]{1,0:T(1,128)S(1)}, f32[1,128]{1,0:T(1,128)S(1)}, u32[]{:S(2)}, u32[]{:S(2)}) collective-permute-start(f32[1,128]{1,0:T(1,128)S(1)} %add.8), channel_id=1, source_target_pairs={{0,2},{1,3},{2,0},{3,1},{4,6},{5,7},{6,4},{7,5},{8,10},{9,11},{10,... | collective-permute-start | bytes 1544 | tf_op jit(solution)/shard_map/ppermute | solution.py:593
  38.4 13.2 %collective-permute-done.11.h_ref = f32[1024,128]{1,0:T(8,128)S(1)} collective-permute-done((f32[1024,128]{1,0:T(8,128)S(1)}, f32[1024,128]{1,0:T(8,128)S(1)}, u32[]{:S(2)}, u32[]{:S(2)}) %collective-permute-start.11) | collective-permute-done | bytes 524320 | tf_op jit(solution)/shard_map/ppermute | solution.py:482
  51.7 4.3 %span_key_grad.1 = (bf16[256,1024]{1,0:T(8,128)(2,1)}, bf16[256,1024]{1,0:T(8,128)(2,1)}, f32[8,256]{1,0:T(8,128)}) custom-call(s32[1,256]{1,0:T(1,128)S(1)} %copy-done.2, bf16[256,1024]{1,0:T(8,128)(2,1)S(1)} %bitcast.26, bf16[256,1024]{1,0:T(8,128)(2,1)S(1)} %bitcast.29, f32[8,256]{1,0:T(8,128)S(1)} %bitcast.32, ...), custom_call_target="tpu_custom_call" | custom-call | flops 3221225472 | bytes 4000000 | tf_op jit(solution)/shard_map/span_key_grad/pallas_call | solution.py:467
  56.0 9.4 %all_to_all.5 = f32[8,1,128]{2,1,0:T(1,128)S(1)} all-to-all(f32[8,1,128]{2,1,0:T(1,128)S(1)} %broadcast_in_dim_broadcast_in_dim.2), channel_id=1, replica_groups=mesh['seq'=8,'dp'=4] {'seq'}, dimensions={0} | all-to-all | bytes 8192 | tf_op jit(solution)/shard_map/all_to_all | solution.py:611
  (33 shorter events, 3.8 us)
Async XLA Ops:
  0.6 0.7 %copy-start.2 = (s32[1,256]{1,0:T(1,128)S(1)}, s32[1,256]{1,0:T(1,128)}, u32[]{:S(2)}) copy-start(s32[1,256]{1,0:T(1,128)} %ids_ref.13) | copy-start | bytes 3076
  1.3 1.0 %copy-start.4 = (bf16[1,256,1024]{2,1,0:T(8,128)(2,1)S(1)}, bf16[1,256,1024]{2,1,0:T(8,128)(2,1)}, u32[]{:S(2)}) copy-start(bf16[1,256,1024]{2,1,0:T(8,128)(2,1)} %param.8) | copy-start | bytes 1572868
  2.4 1.0 %copy-start.5 = (bf16[1,256,1024]{2,1,0:T(8,128)(2,1)S(1)}, bf16[1,256,1024]{2,1,0:T(8,128)(2,1)}, u32[]{:S(2)}) copy-start(bf16[1,256,1024]{2,1,0:T(8,128)(2,1)} %param.9) | copy-start | bytes 1572868
  3.4 0.7 %copy-start.6 = (f32[1,256,8]{1,2,0:T(8,128)S(1)}, f32[1,256,8]{1,2,0:T(8,128)}, u32[]{:S(2)}) copy-start(f32[1,256,8]{1,2,0:T(8,128)} %param.10) | copy-start | bytes 24580
  9.1 5.8 %collective-permute-start.2 = (f32[2056,128]{1,0:T(8,128)S(1)}, f32[2056,128]{1,0:T(8,128)S(1)}, u32[]{:S(2)}, u32[]{:S(2)}) collective-permute-start(f32[2056,128]{1,0:T(8,128)S(1)} %get-tuple-element.50.ab_ref), channel_id=1, source_target_pairs={{8,12},{9,13},{10,14},{11,15}} | collective-permute-start | bytes 3158024 | tf_op jit(solution)/shard_map/ppermute | solution.py:482
  9.9 3.9 %collective-permute-start = (f32[1032,128]{1,0:T(8,128)S(1)}, f32[1032,128]{1,0:T(8,128)S(1)}, u32[]{:S(2)}, u32[]{:S(2)}) collective-permute-start(f32[1032,128]{1,0:T(8,128)S(1)} %get-tuple-element.51), channel_id=1, source_target_pairs={{0,4},{1,5},{2,6},{3,7}} | collective-permute-start | bytes 1585160 | tf_op jit(solution)/shard_map/ppermute | solution.py:482
  14.1 2.2 %copy-start.1 = (bf16[1,256,1024]{2,1,0:T(8,128)(2,1)S(1)}, bf16[1,256,1024]{2,1,0:T(8,128)(2,1)}, u32[]{:S(2)}) copy-start(bf16[1,256,1024]{2,1,0:T(8,128)(2,1)} %param.7) | copy-start | bytes 1572868
  14.1 6.1 %collective-permute-start.1 = (f32[1032,128]{1,0:T(8,128)S(1)}, f32[1032,128]{1,0:T(8,128)S(1)}, u32[]{:S(2)}, u32[]{:S(2)}) collective-permute-start(f32[1032,128]{1,0:T(8,128)S(1)} %step.1), channel_id=1, source_target_pairs={{4,12},{5,13},{6,14},{7,15}} | collective-permute-start | bytes 1585160 | tf_op jit(solution)/shard_map/ppermute | solution.py:482
  15.5 4.6 %collective-permute-start.3 = (f32[1024,128]{1,0:T(8,128)S(1)}, f32[1024,128]{1,0:T(8,128)S(1)}, u32[]{:S(2)}, u32[]{:S(2)}) collective-permute-start(f32[1024,128]{1,0:T(8,128)S(1)} %get-tuple-element.53), channel_id=1, source_target_pairs={{12,4},{13,5},{14,6},{15,7}} | collective-permute-start | bytes 1572872 | tf_op jit(solution)/shard_map/ppermute | solution.py:482
  19.3 2.1 %copy-start = (bf16[1,256,1024]{2,1,0:T(8,128)(2,1)S(1)}, bf16[1,256,1024]{2,1,0:T(8,128)(2,1)}, u32[]{:S(2)}) copy-start(bf16[1,256,1024]{2,1,0:T(8,128)(2,1)} %param.12) | copy-start | bytes 1572868
  19.3 2.1 %copy-start.3 = (f32[128]{0:T(128)S(1)}, f32[128]{0:T(128)}, u32[]{:S(2)}) copy-start(f32[128]{0:T(128)} %param.13) | copy-start | bytes 1540
  19.3 2.1 %collective-permute-start.4 = (f32[1032,128]{1,0:T(8,128)S(1)}, f32[1032,128]{1,0:T(8,128)S(1)}, u32[]{:S(2)}, u32[]{:S(2)}) collective-permute-start(f32[1032,128]{1,0:T(8,128)S(1)} %step.1), channel_id=1, source_target_pairs={{4,8},{16,20},{20,24},{24,28},{5,9},{17,21},{21,25},{25,29},{6,10}... | collective-permute-start | bytes 1585160 | tf_op jit(solution)/shard_map/ppermute | solution.py:482
  20.7 0.7 %collective-permute-start.5 = (f32[1032,128]{1,0:T(8,128)S(1)}, f32[1032,128]{1,0:T(8,128)S(1)}, u32[]{:S(2)}, u32[]{:S(2)}) collective-permute-start(f32[1032,128]{1,0:T(8,128)S(1)} %apply.1), channel_id=1, source_target_pairs={{12,16},{13,17},{14,18},{15,19}} | collective-permute-start | bytes 1585160 | tf_op jit(solution)/shard_map/ppermute | solution.py:482
  23.9 2.3 %collective-permute-start.9 = (f32[1032,128]{1,0:T(8,128)S(1)}, f32[1032,128]{1,0:T(8,128)S(1)}, u32[]{:S(2)}, u32[]{:S(2)}) collective-permute-start(f32[1032,128]{1,0:T(8,128)S(1)} %get-tuple-element.76.c_ref), channel_id=1, source_target_pairs={{12,8},{13,9},{14,10},{15,11}} | collective-permute-start | bytes 1585160 | tf_op jit(solution)/shard_map/ppermute | solution.py:482
  24.8 9.0 %collective-permute-start.6 = (f32[1032,128]{1,0:T(8,128)S(1)}, f32[1032,128]{1,0:T(8,128)S(1)}, u32[]{:S(2)}, u32[]{:S(2)}) collective-permute-start(f32[1032,128]{1,0:T(8,128)S(1)} %get-tuple-element.76.c_ref), channel_id=1, source_target_pairs={{16,4},{17,5},{18,6},{19,7}} | collective-permute-start | bytes 1585160 | tf_op jit(solution)/shard_map/ppermute | solution.py:482
  25.5 8.3 %collective-permute-start.7 = (f32[1032,128]{1,0:T(8,128)S(1)}, f32[1032,128]{1,0:T(8,128)S(1)}, u32[]{:S(2)}, u32[]{:S(2)}) collective-permute-start(f32[1032,128]{1,0:T(8,128)S(1)} %get-tuple-element.76.c_ref), channel_id=1, source_target_pairs={{16,12},{17,13},{18,14},{19,15}} | collective-permute-start | bytes 1585160 | tf_op jit(solution)/shard_map/ppermute | solution.py:482
  26.6 7.2 %collective-permute-start.10 = (f32[1032,128]{1,0:T(8,128)S(1)}, f32[1032,128]{1,0:T(8,128)S(1)}, u32[]{:S(2)}, u32[]{:S(2)}) collective-permute-start(f32[1032,128]{1,0:T(8,128)S(1)} %back.1), channel_id=1, source_target_pairs={{8,4},{9,5},{10,6},{11,7}} | collective-permute-start | bytes 1585160 | tf_op jit(solution)/shard_map/ppermute | solution.py:482
  27.3 6.5 %collective-permute-start.8 = (f32[1,128]{1,0:T(1,128)S(1)}, f32[1,128]{1,0:T(1,128)S(1)}, u32[]{:S(2)}, u32[]{:S(2)}) collective-permute-start(f32[1,128]{1,0:T(1,128)S(1)} %get-tuple-element.77), channel_id=1, source_target_pairs={{0,1},{1,0},{2,3},{3,2},{4,5},{5,4},{6,7},{7,6},{8,9},{9,8},{10,11... | collective-permute-start | bytes 1544 | tf_op jit(solution)/shard_map/ppermute | solution.py:582
  33.8 17.9 %copy-start.7 = (f32[1,256,8]{1,2,0:T(8,128)S(1)}, f32[1,256,8]{1,2,0:T(8,128)}, u32[]{:S(2)}) copy-start(f32[1,256,8]{1,2,0:T(8,128)} %param.10) | copy-start | bytes 24580
  34.5 17.2 %collective-permute-start.11 = (f32[1024,128]{1,0:T(8,128)S(1)}, f32[1024,128]{1,0:T(8,128)S(1)}, u32[]{:S(2)}, u32[]{:S(2)}) collective-permute-start(f32[1024,128]{1,0:T(8,128)S(1)} %get-tuple-element.87), channel_id=1, source_target_pairs={{4,0},{12,8},{20,16},{24,20},{28,24},{5,1},{13,9},{21,17},{25,21},... | collective-permute-start | bytes 1572872 | tf_op jit(solution)/shard_map/ppermute | solution.py:482
  35.8 20.2 %collective-permute-start.12 = (f32[1,128]{1,0:T(1,128)S(1)}, f32[1,128]{1,0:T(1,128)S(1)}, u32[]{:S(2)}, u32[]{:S(2)}) collective-permute-start(f32[1,128]{1,0:T(1,128)S(1)} %add.8), channel_id=1, source_target_pairs={{0,2},{1,3},{2,0},{3,1},{4,6},{5,7},{6,4},{7,5},{8,10},{9,11},{10,... | collective-permute-start | bytes 1544 | tf_op jit(solution)/shard_map/ppermute | solution.py:593

commit v9 on v8

--- a/solution.py
+++ b/solution.py
@@ -164,6 +164,13 @@
 
     ts = base_inverses(blocks)
     s = BASE
+    inside = (ii // (4 * s) == jj // (4 * s)) & (ii // s != jj // s)
+    tss = [split(t) for t in ts]
+    steps = [split(pack3(t, split(jnp.where(inside, b, 0.0)))) for t, b in zip(tss, blocks)]
+    squares = [split(pack3(m, m)) for m in steps]
+    ts = [t - pack3(m, p) for t, m, p in zip(ts, steps, tss)]
+    ts = [t + pack3(q, split(t)) for t, q in zip(ts, squares)]
+    s *= 4
     while s < n:
         offs = [split(off(b, s)) for b in blocks]
         tss = [split(t) for t in ts]

time: 66.4 us -> 66 us (level)
  no operation moved by 1% of the time
where the time goes in v9:
time: 66 us; the launch traced here: 65.5 us
  Pallas kernels  21.1 us (32%)
  starting transfers between devices  15.5 us (23%)
  waiting for transfers between devices  14.7 us (22%)
  blocking collectives  9.29 us (14%)
  local copies, waits for them, and re-layouts  3.48 us (5%)
  between operations  0.9 us (1%)
    pallas_call x10, Pallas kernels, call(): pl.pallas_call(kernel, out_shape=outs, compiler_params=pltpu.CompilerPara...  21.1 us
    ppermute x11, waiting for transfers between devices, send(): return lax.ppermute(value, 'seq', pairs)  14.7 us
    ppermute x11, starting transfers between devices, send(): return lax.ppermute(value, 'seq', pairs)  10.4 us
    all_to_all x1, blocking collectives, local(): gain_total = jnp.sum(lax.all_to_all(copies, 'seq', 0, 0), axis=(0, 1))  9.29 us
    unnamed x16, local copies, waits for them, and re-layouts  3.47 us
    ppermute x1, starting transfers between devices, local(): got = lax.ppermute(dgain, 'dp', [(i, i ^ step) for i in range(rows)])  2.66 us
    ppermute x1, starting transfers between devices, local(): got = lax.ppermute(dgain, 'dp', [(i, i ^ 1) for i in range(rows)])  2.48 us
  transfers between devices with their start and end apart: 13, of which 2 were waited for; matrix products, arithmetic and copies ran while one was open for 0% of the time, Pallas kernels for 20%

profile of v9, /device:TPU:0, one launch (start us, length us, event | category | flops | bytes accessed | tf_op | source)
XLA Modules:
  0.0 65.5 jit_solution(2487747690331686066)
XLA Ops:
  1.3 1.0 %copy-done.4 = bf16[1,256,1024]{2,1,0:T(8,128)(2,1)S(1)} copy-done((bf16[1,256,1024]{2,1,0:T(8,128)(2,1)S(1)}, bf16[1,256,1024]{2,1,0:T(8,128)(2,1)}, u32[]{:S(2)}) %copy-start.4) | copy-done | bytes 524312
  2.4 1.0 %copy-done.5 = bf16[1,256,1024]{2,1,0:T(8,128)(2,1)S(1)} copy-done((bf16[1,256,1024]{2,1,0:T(8,128)(2,1)S(1)}, bf16[1,256,1024]{2,1,0:T(8,128)(2,1)}, u32[]{:S(2)}) %copy-start.5) | copy-done | bytes 524312
  3.4 0.7 %copy-done.6 = f32[1,256,8]{1,2,0:T(8,128)S(1)} copy-done((f32[1,256,8]{1,2,0:T(8,128)S(1)}, f32[1,256,8]{1,2,0:T(8,128)}, u32[]{:S(2)}) %copy-start.6) | copy-done | bytes 8216
  4.1 4.8 %span_state.1 = (f32[2056,128]{1,0:T(8,128)S(1)}, f32[1032,128]{1,0:T(8,128)S(1)}, bf16[8,256,256]{2,1,0:T(8,128)(2,1)S(1)}, bf16[8,256,256]{2,1,0:T(8,128)(2,1)S(1)}, f32[8,128,256]{2,1,0:T(8,128)S(1)}) custom-call(s32[1,256]{1,0:T(1,128)S(1)} %copy-done.2, bf16[256,1024]{1,0:T(8,128)(2,1)S(1)} %bitcast.23, bf16[256,1024]{1,0:T(8,128)(2,1)S(1)} %bitcast.27, ...), custom_call_target="tpu_custom_call" | custom-call | flops 5368709120 | bytes 4000000 | tf_op jit(solution)/shard_map/span_state/pallas_call | solution.py:474
  8.9 0.7 %collective-permute-start.2 = (f32[2056,128]{1,0:T(8,128)S(1)}, f32[2056,128]{1,0:T(8,128)S(1)}, u32[]{:S(2)}, u32[]{:S(2)}) collective-permute-start(f32[2056,128]{1,0:T(8,128)S(1)} %get-tuple-element.50.ab_ref), channel_id=1, source_target_pairs={{8,12},{9,13},{10,14},{11,15}} | collective-permute-start | bytes 3158024 | tf_op jit(solution)/shard_map/ppermute | solution.py:489
  9.6 2.4 %collective-permute-start = (f32[1032,128]{1,0:T(8,128)S(1)}, f32[1032,128]{1,0:T(8,128)S(1)}, u32[]{:S(2)}, u32[]{:S(2)}) collective-permute-start(f32[1032,128]{1,0:T(8,128)S(1)} %get-tuple-element.51), channel_id=1, source_target_pairs={{0,4},{1,5},{2,6},{3,7}} | collective-permute-start | bytes 1585160 | tf_op jit(solution)/shard_map/ppermute | solution.py:489
  12.0 1.5 %collective-permute-done.prev_ref.m1_ref = f32[1032,128]{1,0:T(8,128)S(1)} collective-permute-done((f32[1032,128]{1,0:T(8,128)S(1)}, f32[1032,128]{1,0:T(8,128)S(1)}, u32[]{:S(2)}, u32[]{:S(2)}) %collective-permute-start) | collective-permute-done | bytes 528416 | tf_op jit(solution)/shard_map/ppermute | solution.py:489
  13.8 0.8 %collective-permute-start.1 = (f32[1032,128]{1,0:T(8,128)S(1)}, f32[1032,128]{1,0:T(8,128)S(1)}, u32[]{:S(2)}, u32[]{:S(2)}) collective-permute-start(f32[1032,128]{1,0:T(8,128)S(1)} %step.1), channel_id=1, source_target_pairs={{4,12},{5,13},{6,14},{7,15}} | collective-permute-start | bytes 1585160 | tf_op jit(solution)/shard_map/ppermute | solution.py:489
  15.3 0.7 %collective-permute-start.3 = (f32[1024,128]{1,0:T(8,128)S(1)}, f32[1024,128]{1,0:T(8,128)S(1)}, u32[]{:S(2)}, u32[]{:S(2)}) collective-permute-start(f32[1024,128]{1,0:T(8,128)S(1)} %get-tuple-element.53), channel_id=1, source_target_pairs={{12,4},{13,5},{14,6},{15,7}} | collective-permute-start | bytes 1572872 | tf_op jit(solution)/shard_map/ppermute | solution.py:489
  16.0 3.0 %span_out.1 = (f32[256,1024]{1,0:T(8,128)S(1)}, f32[256,1024]{1,0:T(8,128)S(1)}, f32[8,256,256]{2,1,0:T(8,128)S(1)}, bf16[8,256,256]{2,1,0:T(8,128)(2,1)S(1)}, b...) custom-call(s32[1,256]{1,0:T(1,128)S(1)} %copy-done.2, ...), custom_call_target="tpu_custom_call" | custom-call | flops 2952790016 | bytes 4000000 | tf_op jit(solution)/shard_map/span_out/pallas_call | solution.py:474
  19.0 0.8 %collective-permute-start.4 = (f32[1032,128]{1,0:T(8,128)S(1)}, f32[1032,128]{1,0:T(8,128)S(1)}, u32[]{:S(2)}, u32[]{:S(2)}) collective-permute-start(f32[1032,128]{1,0:T(8,128)S(1)} %step.1), channel_id=1, source_target_pairs={{4,8},{16,20},{20,24},{24,28},{5,9},{17,21},{21,25},{25,29},{6,10}... | collective-permute-start | bytes 1585160 | tf_op jit(solution)/shard_map/ppermute | solution.py:489
  20.4 0.7 %collective-permute-start.5 = (f32[1032,128]{1,0:T(8,128)S(1)}, f32[1032,128]{1,0:T(8,128)S(1)}, u32[]{:S(2)}, u32[]{:S(2)}) collective-permute-start(f32[1032,128]{1,0:T(8,128)S(1)} %apply.1), channel_id=1, source_target_pairs={{12,16},{13,17},{14,18},{15,19}} | collective-permute-start | bytes 1585160 | tf_op jit(solution)/shard_map/ppermute | solution.py:489
  21.1 2.5 %span_norm.1 = (bf16[256,1024]{1,0:T(8,128)(2,1)}, f32[256,1024]{1,0:T(8,128)S(1)}, f32[1032,128]{1,0:T(8,128)S(1)}, f32[8,128,128]{2,1,0:T(8,128)S(1)}, f32[1,128]{1,0:T(1,128)S(1)}) custom-call(s32[1,256]{1,0:T(1,128)S(1)} %copy-done.2, bf16[256,1024]{1,0:T(8,128)(2,1)S(1)} %bitcast.20, f32[256,1024]{1,0:T(8,128)S(1)} %get-tuple-element.62.o_ref, ...), custom_call_target="tpu_custom_call" | custom-call | flops 1073741824 | bytes 4000000 | tf_op jit(solution)/shard_map/span_norm/pallas_call | solution.py:474
  23.7 0.7 %collective-permute-start.9 = (f32[1032,128]{1,0:T(8,128)S(1)}, f32[1032,128]{1,0:T(8,128)S(1)}, u32[]{:S(2)}, u32[]{:S(2)}) collective-permute-start(f32[1032,128]{1,0:T(8,128)S(1)} %get-tuple-element.76.c_ref), channel_id=1, source_target_pairs={{12,8},{13,9},{14,10},{15,11}} | collective-permute-start | bytes 1585160 | tf_op jit(solution)/shard_map/ppermute | solution.py:489
  24.4 0.7 %collective-permute-start.6 = (f32[1032,128]{1,0:T(8,128)S(1)}, f32[1032,128]{1,0:T(8,128)S(1)}, u32[]{:S(2)}, u32[]{:S(2)}) collective-permute-start(f32[1032,128]{1,0:T(8,128)S(1)} %get-tuple-element.76.c_ref), channel_id=1, source_target_pairs={{16,4},{17,5},{18,6},{19,7}} | collective-permute-start | bytes 1585160 | tf_op jit(solution)/shard_map/ppermute | solution.py:489
  25.1 0.9 %collective-permute-start.7 = (f32[1032,128]{1,0:T(8,128)S(1)}, f32[1032,128]{1,0:T(8,128)S(1)}, u32[]{:S(2)}, u32[]{:S(2)}) collective-permute-start(f32[1032,128]{1,0:T(8,128)S(1)} %get-tuple-element.76.c_ref), channel_id=1, source_target_pairs={{16,12},{17,13},{18,14},{19,15}} | collective-permute-start | bytes 1585160 | tf_op jit(solution)/shard_map/ppermute | solution.py:489
  26.4 0.7 %collective-permute-start.10 = (f32[1032,128]{1,0:T(8,128)S(1)}, f32[1032,128]{1,0:T(8,128)S(1)}, u32[]{:S(2)}, u32[]{:S(2)}) collective-permute-start(f32[1032,128]{1,0:T(8,128)S(1)} %back.1), channel_id=1, source_target_pairs={{8,4},{9,5},{10,6},{11,7}} | collective-permute-start | bytes 1585160 | tf_op jit(solution)/shard_map/ppermute | solution.py:489
  27.1 2.5 %collective-permute-start.8 = (f32[1,128]{1,0:T(1,128)S(1)}, f32[1,128]{1,0:T(1,128)S(1)}, u32[]{:S(2)}, u32[]{:S(2)}) collective-permute-start(f32[1,128]{1,0:T(1,128)S(1)} %get-tuple-element.77), channel_id=1, source_target_pairs={{0,1},{1,0},{2,3},{3,2},{4,5},{5,4},{6,7},{7,6},{8,9},{9,8},{10,11... | collective-permute-start | bytes 1544 | tf_op jit(solution)/shard_map/ppermute | solution.py:589
  29.5 4.0 %span_query_grad.1 = (bf16[256,1024]{1,0:T(8,128)(2,1)}, f32[256,1024]{1,0:T(8,128)S(1)}, f32[256,1024]{1,0:T(8,128)S(1)}, f32[256,1024]{1,0:T(8,128)S(1)}) custom-call(s32[1,256]{1,0:T(1,128)S(1)} %copy-done.2, bf16[256,1024]{1,0:T(8,128)(2,1)S(1)} %bitcast.21, bf16[256,1024]{1,0:T(8,128)(2,1)S(1)} %bitcast.25, ...), custom_call_target="tpu_custom_call" | custom-call | flops 3221225472 | bytes 4000000 | tf_op jit(solution)/shard_map/span_query_grad/pallas_call | solution.py:474
  34.2 1.3 %collective-permute-start.11 = (f32[1024,128]{1,0:T(8,128)S(1)}, f32[1024,128]{1,0:T(8,128)S(1)}, u32[]{:S(2)}, u32[]{:S(2)}) collective-permute-start(f32[1024,128]{1,0:T(8,128)S(1)} %get-tuple-element.87), channel_id=1, source_target_pairs={{4,0},{12,8},{20,16},{24,20},{28,24},{5,1},{13,9},{21,17},{25,21},... | collective-permute-start | bytes 1572872 | tf_op jit(solution)/shard_map/ppermute | solution.py:489
  35.5 2.7 %collective-permute-start.12 = (f32[1,128]{1,0:T(1,128)S(1)}, f32[1,128]{1,0:T(1,128)S(1)}, u32[]{:S(2)}, u32[]{:S(2)}) collective-permute-start(f32[1,128]{1,0:T(1,128)S(1)} %add.8), channel_id=1, source_target_pairs={{0,2},{1,3},{2,0},{3,1},{4,6},{5,7},{6,4},{7,5},{8,10},{9,11},{10,... | collective-permute-start | bytes 1544 | tf_op jit(solution)/shard_map/ppermute | solution.py:600
  38.2 13.2 %collective-permute-done.11.h_ref = f32[1024,128]{1,0:T(8,128)S(1)} collective-permute-done((f32[1024,128]{1,0:T(8,128)S(1)}, f32[1024,128]{1,0:T(8,128)S(1)}, u32[]{:S(2)}, u32[]{:S(2)}) %collective-permute-start.11) | collective-permute-done | bytes 524320 | tf_op jit(solution)/shard_map/ppermute | solution.py:489
  51.4 4.3 %span_key_grad.1 = (bf16[256,1024]{1,0:T(8,128)(2,1)}, bf16[256,1024]{1,0:T(8,128)(2,1)}, f32[8,256]{1,0:T(8,128)}) custom-call(s32[1,256]{1,0:T(1,128)S(1)} %copy-done.2, bf16[256,1024]{1,0:T(8,128)(2,1)S(1)} %bitcast.26, bf16[256,1024]{1,0:T(8,128)(2,1)S(1)} %bitcast.29, f32[8,256]{1,0:T(8,128)S(1)} %bitcast.32, ...), custom_call_target="tpu_custom_call" | custom-call | flops 3221225472 | bytes 4000000 | tf_op jit(solution)/shard_map/span_key_grad/pallas_call | solution.py:474
  55.7 9.3 %all_to_all.5 = f32[8,1,128]{2,1,0:T(1,128)S(1)} all-to-all(f32[8,1,128]{2,1,0:T(1,128)S(1)} %broadcast_in_dim_broadcast_in_dim.2), channel_id=1, replica_groups=mesh['seq'=8,'dp'=4] {'seq'}, dimensions={0} | all-to-all | bytes 8192 | tf_op jit(solution)/shard_map/all_to_all | solution.py:618
  (33 shorter events, 3.8 us)
Async XLA Ops:
  0.6 0.7 %copy-start.2 = (s32[1,256]{1,0:T(1,128)S(1)}, s32[1,256]{1,0:T(1,128)}, u32[]{:S(2)}) copy-start(s32[1,256]{1,0:T(1,128)} %ids_ref.13) | copy-start | bytes 3076
  1.3 1.0 %copy-start.4 = (bf16[1,256,1024]{2,1,0:T(8,128)(2,1)S(1)}, bf16[1,256,1024]{2,1,0:T(8,128)(2,1)}, u32[]{:S(2)}) copy-start(bf16[1,256,1024]{2,1,0:T(8,128)(2,1)} %param.8) | copy-start | bytes 1572868
  2.4 1.0 %copy-start.5 = (bf16[1,256,1024]{2,1,0:T(8,128)(2,1)S(1)}, bf16[1,256,1024]{2,1,0:T(8,128)(2,1)}, u32[]{:S(2)}) copy-start(bf16[1,256,1024]{2,1,0:T(8,128)(2,1)} %param.9) | copy-start | bytes 1572868
  3.4 0.7 %copy-start.6 = (f32[1,256,8]{1,2,0:T(8,128)S(1)}, f32[1,256,8]{1,2,0:T(8,128)}, u32[]{:S(2)}) copy-start(f32[1,256,8]{1,2,0:T(8,128)} %param.10) | copy-start | bytes 24580
  8.9 5.8 %collective-permute-start.2 = (f32[2056,128]{1,0:T(8,128)S(1)}, f32[2056,128]{1,0:T(8,128)S(1)}, u32[]{:S(2)}, u32[]{:S(2)}) collective-permute-start(f32[2056,128]{1,0:T(8,128)S(1)} %get-tuple-element.50.ab_ref), channel_id=1, source_target_pairs={{8,12},{9,13},{10,14},{11,15}} | collective-permute-start | bytes 3158024 | tf_op jit(solution)/shard_map/ppermute | solution.py:489
  9.6 3.9 %collective-permute-start = (f32[1032,128]{1,0:T(8,128)S(1)}, f32[1032,128]{1,0:T(8,128)S(1)}, u32[]{:S(2)}, u32[]{:S(2)}) collective-permute-start(f32[1032,128]{1,0:T(8,128)S(1)} %get-tuple-element.51), channel_id=1, source_target_pairs={{0,4},{1,5},{2,6},{3,7}} | collective-permute-start | bytes 1585160 | tf_op jit(solution)/shard_map/ppermute | solution.py:489
  13.8 2.2 %copy-start.1 = (bf16[1,256,1024]{2,1,0:T(8,128)(2,1)S(1)}, bf16[1,256,1024]{2,1,0:T(8,128)(2,1)}, u32[]{:S(2)}) copy-start(bf16[1,256,1024]{2,1,0:T(8,128)(2,1)} %param.7) | copy-start | bytes 1572868
  13.8 6.1 %collective-permute-start.1 = (f32[1032,128]{1,0:T(8,128)S(1)}, f32[1032,128]{1,0:T(8,128)S(1)}, u32[]{:S(2)}, u32[]{:S(2)}) collective-permute-start(f32[1032,128]{1,0:T(8,128)S(1)} %step.1), channel_id=1, source_target_pairs={{4,12},{5,13},{6,14},{7,15}} | collective-permute-start | bytes 1585160 | tf_op jit(solution)/shard_map/ppermute | solution.py:489
  15.3 4.6 %collective-permute-start.3 = (f32[1024,128]{1,0:T(8,128)S(1)}, f32[1024,128]{1,0:T(8,128)S(1)}, u32[]{:S(2)}, u32[]{:S(2)}) collective-permute-start(f32[1024,128]{1,0:T(8,128)S(1)} %get-tuple-element.53), channel_id=1, source_target_pairs={{12,4},{13,5},{14,6},{15,7}} | collective-permute-start | bytes 1572872 | tf_op jit(solution)/shard_map/ppermute | solution.py:489
  19.0 2.1 %copy-start = (bf16[1,256,1024]{2,1,0:T(8,128)(2,1)S(1)}, bf16[1,256,1024]{2,1,0:T(8,128)(2,1)}, u32[]{:S(2)}) copy-start(bf16[1,256,1024]{2,1,0:T(8,128)(2,1)} %param.12) | copy-start | bytes 1572868
  19.0 2.1 %copy-start.3 = (f32[128]{0:T(128)S(1)}, f32[128]{0:T(128)}, u32[]{:S(2)}) copy-start(f32[128]{0:T(128)} %param.13) | copy-start | bytes 1540
  19.0 2.1 %collective-permute-start.4 = (f32[1032,128]{1,0:T(8,128)S(1)}, f32[1032,128]{1,0:T(8,128)S(1)}, u32[]{:S(2)}, u32[]{:S(2)}) collective-permute-start(f32[1032,128]{1,0:T(8,128)S(1)} %step.1), channel_id=1, source_target_pairs={{4,8},{16,20},{20,24},{24,28},{5,9},{17,21},{21,25},{25,29},{6,10}... | collective-permute-start | bytes 1585160 | tf_op jit(solution)/shard_map/ppermute | solution.py:489
  20.4 0.7 %collective-permute-start.5 = (f32[1032,128]{1,0:T(8,128)S(1)}, f32[1032,128]{1,0:T(8,128)S(1)}, u32[]{:S(2)}, u32[]{:S(2)}) collective-permute-start(f32[1032,128]{1,0:T(8,128)S(1)} %apply.1), channel_id=1, source_target_pairs={{12,16},{13,17},{14,18},{15,19}} | collective-permute-start | bytes 1585160 | tf_op jit(solution)/shard_map/ppermute | solution.py:489
  23.7 2.3 %collective-permute-start.9 = (f32[1032,128]{1,0:T(8,128)S(1)}, f32[1032,128]{1,0:T(8,128)S(1)}, u32[]{:S(2)}, u32[]{:S(2)}) collective-permute-start(f32[1032,128]{1,0:T(8,128)S(1)} %get-tuple-element.76.c_ref), channel_id=1, source_target_pairs={{12,8},{13,9},{14,10},{15,11}} | collective-permute-start | bytes 1585160 | tf_op jit(solution)/shard_map/ppermute | solution.py:489
  24.4 9.2 %collective-permute-start.6 = (f32[1032,128]{1,0:T(8,128)S(1)}, f32[1032,128]{1,0:T(8,128)S(1)}, u32[]{:S(2)}, u32[]{:S(2)}) collective-permute-start(f32[1032,128]{1,0:T(8,128)S(1)} %get-tuple-element.76.c_ref), channel_id=1, source_target_pairs={{16,4},{17,5},{18,6},{19,7}} | collective-permute-start | bytes 1585160 | tf_op jit(solution)/shard_map/ppermute | solution.py:489
  25.1 8.5 %collective-permute-start.7 = (f32[1032,128]{1,0:T(8,128)S(1)}, f32[1032,128]{1,0:T(8,128)S(1)}, u32[]{:S(2)}, u32[]{:S(2)}) collective-permute-start(f32[1032,128]{1,0:T(8,128)S(1)} %get-tuple-element.76.c_ref), channel_id=1, source_target_pairs={{16,12},{17,13},{18,14},{19,15}} | collective-permute-start | bytes 1585160 | tf_op jit(solution)/shard_map/ppermute | solution.py:489
  26.4 7.2 %collective-permute-start.10 = (f32[1032,128]{1,0:T(8,128)S(1)}, f32[1032,128]{1,0:T(8,128)S(1)}, u32[]{:S(2)}, u32[]{:S(2)}) collective-permute-start(f32[1032,128]{1,0:T(8,128)S(1)} %back.1), channel_id=1, source_target_pairs={{8,4},{9,5},{10,6},{11,7}} | collective-permute-start | bytes 1585160 | tf_op jit(solution)/shard_map/ppermute | solution.py:489
  27.1 6.4 %collective-permute-start.8 = (f32[1,128]{1,0:T(1,128)S(1)}, f32[1,128]{1,0:T(1,128)S(1)}, u32[]{:S(2)}, u32[]{:S(2)}) collective-permute-start(f32[1,128]{1,0:T(1,128)S(1)} %get-tuple-element.77), channel_id=1, source_target_pairs={{0,1},{1,0},{2,3},{3,2},{4,5},{5,4},{6,7},{7,6},{8,9},{9,8},{10,11... | collective-permute-start | bytes 1544 | tf_op jit(solution)/shard_map/ppermute | solution.py:589
  33.5 17.9 %copy-start.7 = (f32[1,256,8]{1,2,0:T(8,128)S(1)}, f32[1,256,8]{1,2,0:T(8,128)}, u32[]{:S(2)}) copy-start(f32[1,256,8]{1,2,0:T(8,128)} %param.10) | copy-start | bytes 24580
  34.2 17.2 %collective-permute-start.11 = (f32[1024,128]{1,0:T(8,128)S(1)}, f32[1024,128]{1,0:T(8,128)S(1)}, u32[]{:S(2)}, u32[]{:S(2)}) collective-permute-start(f32[1024,128]{1,0:T(8,128)S(1)} %get-tuple-element.87), channel_id=1, source_target_pairs={{4,0},{12,8},{20,16},{24,20},{28,24},{5,1},{13,9},{21,17},{25,21},... | collective-permute-start | bytes 1572872 | tf_op jit(solution)/shard_map/ppermute | solution.py:489
  35.5 20.2 %collective-permute-start.12 = (f32[1,128]{1,0:T(1,128)S(1)}, f32[1,128]{1,0:T(1,128)S(1)}, u32[]{:S(2)}, u32[]{:S(2)}) collective-permute-start(f32[1,128]{1,0:T(1,128)S(1)} %add.8), channel_id=1, source_target_pairs={{0,2},{1,3},{2,0},{3,1},{4,6},{5,7},{6,4},{7,5},{8,10},{9,11},{10,... | collective-permute-start | bytes 1544 | tf_op jit(solution)/shard_map/ppermute | solution.py:600
